TPU v7x, 256 devices: a whole 4x4x8 slice. The times are simulated.
256 devices in a mesh: req: 64 (over z, x, core), tp: 4 (over y).
Axes of the slice: x: 4, y: 4, z: 8, core: 2. Of those that a mesh axis runs over, the one named last changes fastest.
Arguments:
- conv_input: bfloat16 [32768, 16384], P('req', 'tp'), may hold values from -6 to 6
- gate_input: bfloat16 [32768, 16384], P('req', 'tp'), may hold values from -6 to 6
- conv_weight: float32 [4, 16384], P(None, 'tp'), may hold values from -3 to 3
- conv_bias: float32 [16384], P('tp'), may hold values from -3 to 3
- select_weight: bfloat16 [16384, 288], P('tp'), may hold values from -0.046875 to 0.046875
- step_weight: bfloat16 [256, 16384], P(None, 'tp'), may hold values from -0.375 to 0.375
- step_bias: float32 [16384], P('tp'), may hold values from -7 to -2
- decay_log: float32 [16, 16384], P(None, 'tp'), may hold values from 0 to 2.8
- skip_gain: float32 [16384], P('tp'), may hold values from 0.5 to 1.5
- store_state: float32 [128, 64, 16, 256], P(None, 'req', None, 'tp'), may hold values from -4 to 4
- store_edge: bfloat16 [128, 64, 3, 256], P(None, 'req', None, 'tp'), may hold values from -6 to 6
- read_slot: int32 [64], replicated, may hold values from 0 to 127
- save_slot: int32 [64], replicated, may hold values from 0 to 127, as said below
- cache_hit: int32 [64], P('req'), may hold values 0 or 1
- suffix_length: int32 [64], P('req'), may hold values from 128 to 512, as said below
Outputs:
- gated: bfloat16 [32768, 16384], P('req', 'tp')
- new_state: float32 [128, 64, 16, 256], P(None, 'req', None, 'tp')
- new_edge_store: bfloat16 [128, 64, 3, 256], P(None, 'req', None, 'tp')
Inputs may be any that keep to these rules, and one draw needn't show every extreme that they name: `save_slot`: the 64 entries are distinct. `suffix_length`: some request has exactly 512 live rows.
All inputs are finite; a program needn't handle non-finite values. No bound on the sum of `cache_hit` on one device may be relied on, other than what follows from the above.
Results may differ from a plain program's by a relative error of at most 0.007.
Values may be sent and summed in bfloat16 or wider, within the bound.
No kernel may reach another device: no remote copies, remote signals or barrier semaphores. Data moves between devices by JAX's collectives and lax.ppermute only.
A program may use at most 128 MiB of HBM per device.

v0:
```python
import jax
import jax.numpy as jnp
from jax import lax
from jax.sharding import PartitionSpec as P

STATE = 16
CONV = 4
RANK = 256


def run_blocks(start_state, decay_rate, step_size, drive, b_rows, c_rows):
    total_rows, channels = step_size.shape

    def step_block(carry, pieces):
        state, block = carry
        size_block, drive_block = pieces
        b_block = lax.dynamic_slice_in_dim(b_rows, block * 16, 16, 1)
        c_block = lax.dynamic_slice_in_dim(c_rows, block * 16, 16, 1)
        results = []
        for position in range(16):
            state = (
                jnp.exp(size_block[position][None, :] * decay_rate) * state
                + b_block[:, position][:, None] * drive_block[position][None, :]
            )
            results.append(jnp.sum(c_block[:, position][:, None] * state, axis=0))
        return ((state, block + 1), jnp.stack(results))

    (end_state, _), scanned = lax.scan(
        step_block,
        (start_state, jnp.int32(0)),
        (step_size.reshape(-1, 16, channels), drive.reshape(-1, 16, channels)),
    )
    return (end_state, scanned.reshape(total_rows, channels))


def normalize(low_part):
    return (
        low_part / jnp.sqrt(jnp.mean(low_part * low_part, axis=-1, keepdims=True) + 1e-06)
    ).astype(jnp.bfloat16)


def local(
    conv_input,
    gate_input,
    conv_weight,
    conv_bias,
    select_weight,
    step_weight,
    step_bias,
    decay_log,
    skip_gain,
    store_state,
    store_edge,
    read_slot,
    save_slot,
    cache_hit,
    suffix_length,
):
    local_rows, channels = conv_input.shape
    decay_rate = -jnp.exp(decay_log)
    held_state = store_state[read_slot, 0]
    held_edge = store_edge[read_slot, 0]
    is_hit = cache_hit[0] > 0
    length = suffix_length[0]
    got_state, got_edge = (
        lax.all_to_all(
            held_state.astype(jnp.bfloat16), "req", split_axis=0, concat_axis=2, tiled=True
        ).astype(held_state.dtype),
        lax.all_to_all(
            held_edge.astype(jnp.float32).astype(jnp.bfloat16),
            "req",
            split_axis=0,
            concat_axis=2,
            tiled=True,
        ).astype(jnp.float32),
    )
    start_state = jnp.where(is_hit, got_state[0], 0.0)
    edge_rows = jnp.where(is_hit, got_edge[0], 0.0).astype(jnp.bfloat16)
    padded = jnp.concatenate([edge_rows, conv_input], 0)
    conv_sum = conv_bias + jnp.zeros((local_rows, channels), jnp.float32)
    for tap in range(CONV):
        conv_sum = conv_sum + conv_weight[tap] * padded[tap : tap + local_rows].astype(jnp.float32)
    mixed = jax.nn.silu(conv_sum)
    partial_proj = jnp.dot(
        mixed.astype(jnp.bfloat16), select_weight, preferred_element_type=jnp.float32
    )
    projected = lax.psum(partial_proj, "tp")
    normed = normalize(projected[:, :RANK])
    selectors = projected[:, RANK:]
    selector_rows = selectors.T
    b_rows = selector_rows[:STATE]
    c_rows = selector_rows[STATE:]
    live = (jnp.arange(local_rows) < length)[:, None]
    step_size = jax.nn.softplus(
        jnp.dot(normed, step_weight, preferred_element_type=jnp.float32) + step_bias
    )
    step_size = jnp.where(live, step_size, 0.0)
    drive = step_size * mixed
    end_state, scanned = run_blocks(start_state, decay_rate, step_size, drive, b_rows, c_rows)
    output = (scanned + skip_gain * mixed) * jax.nn.silu(gate_input.astype(jnp.float32))
    output = jnp.where(live, output, 0.0).astype(jnp.bfloat16)
    edge_next = lax.dynamic_slice_in_dim(padded, length, CONV - 1, 0)
    back_state, back_edge = (
        lax.all_to_all(
            end_state[None].astype(jnp.bfloat16), "req", split_axis=2, concat_axis=0, tiled=True
        ).astype(jnp.float32),
        lax.all_to_all(
            edge_next.astype(jnp.float32)[None].astype(jnp.bfloat16),
            "req",
            split_axis=2,
            concat_axis=0,
            tiled=True,
        ).astype(jnp.float32),
    )
    new_state = store_state.at[save_slot, 0].set(back_state)
    new_edge_store = store_edge.at[save_slot, 0].set(back_edge.astype(jnp.bfloat16))
    return (output, new_state, new_edge_store)


def solution(mesh):
    placed = (
        P("req", "tp"),
        P("req", "tp"),
        P(None, "tp"),
        P("tp"),
        P("tp", None),
        P(None, "tp"),
        P("tp"),
        P(None, "tp"),
        P("tp"),
        P(None, "req", None, "tp"),
        P(None, "req", None, "tp"),
        P(),
        P(),
        P("req"),
        P("req"),
    )
    return jax.shard_map(
        local,
        mesh=mesh,
        in_specs=placed,
        out_specs=(P("req", "tp"), P(None, "req", None, "tp"), P(None, "req", None, "tp")),
        check_vma=False,
    )
```

profile of v0, /device:TPU:1, one launch (start us, length us, event | category | flops | bytes accessed | tf_op | source)
XLA Modules:
  0.0 521.9 jit_solution(15995057156849733562)
XLA Ops:
  10.3 13.0 %all-to-all-start.1 = ((bf16[64,3,64]{2,1,0:T(4,128)(2,1)}), bf16[64,3,64]{2,1,0:T(4,128)(2,1)S(1)}, u32[]{:S(2)}, u32[]{:S(2)}) async-start(bf16[64,3,64]{2,1,0:T(4,128)(2,1)} %gather_fusion.1), calls=%async_computation.1 | async-start | bytes 131072 | tf_op jit(solution)/shard_map/all_to_all | solution.py:69
  28.6 4.7 all-to-all-done.1
  34.5 3.9 copy.87
  38.4 5.8 %all-to-all-start.3 = ((bf16[1,3,4096]{1,0,2:T(2,128)(2,1)}), bf16[1,3,4096]{1,0,2:T(2,128)(2,1)}, u32[]{:S(2)}, u32[]{:S(2)}) async-start(bf16[1,3,4096]{1,0,2:T(2,128)(2,1)} %copy.87), calls=%async_computation.3 | async-start | bytes 4194304 | tf_op jit(solution)/shard_map/all_to_all | solution.py:107
  44.2 10.6 %divide_multiply_fusion = f32[512,4096]{1,0:T(8,128)S(1)} fusion(bf16[512,4096]{1,0:T(8,128)(2,1)} %param.17, bf16[3,4096]{1,0:T(4,128)(2,1)S(1)} %convert_element_type.83, f32[4096]{0:T(1024)S(1)} %bitcast.402, f32[4096]{0:T(1024)S(1)} %bitcast.403, f32[4096]{0:T(1024)S(1)} %bitcast.401, f32[4096]{0:T(1024)S(1)} %bitcast.400, f32[4096]{0:T(1024)S(1)} %copy-done.5), kind=kLoop, calls=%fused_computation.115 | loop fusion | flops 52428800 | bytes 12689408 | tf_op jit(solution)/shard_map/jit(silu)/mul | solution.py:83
  54.9 3.2 copy-done.2
  60.4 33.4 %all-to-all-done.3 = bf16[1,3,4096]{1,0,2:T(2,128)(2,1)} async-done(((bf16[1,3,4096]{1,0,2:T(2,128)(2,1)}), bf16[1,3,4096]{1,0,2:T(2,128)(2,1)}, u32[]{:S(2)}, u32[]{:S(2)}) %all-to-all-start.3) | async-done | bytes 24608 | tf_op jit(solution)/shard_map/all_to_all | solution.py:107
  93.8 7.0 %all-to-all-start = ((bf16[64,2,512]{2,1,0:T(2,128)(2,1)}), bf16[64,2,512]{2,1,0:T(2,128)(2,1)S(1)}, u32[]{:S(2)}, u32[]{:S(2)}) async-start(bf16[64,2,512]{2,1,0:T(2,128)(2,1)} %reshape.175), calls=%async_computation | async-start | bytes 262144 | tf_op jit(solution)/shard_map/all_to_all | solution.py:66
  102.6 4.6 copy.88
  114.5 15.6 %fusion.20 = (f32[512,4096]{1,0:T(8,128)}, f32[512,4096]{1,0:T(8,128)}) fusion(f32[512,4096]{1,0:T(8,128)} %copy-done.2, f32[4096]{0:T(1024)S(1)} %copy-done.9, bf16[256,4096]{1,0:T(8,128)(2,1)} %param.22, f32[512,288]{0,1:T(8,128)} %all-reduce.4.cloned.1.call-done, f32[512]{0:T(512)S(1)} %add_sqrt_fusion, pred[512]{0:T(512)(128)(4,1)S(1)} %iota_compare_fusion), kind=kOutput, calls=%fused_computation.143 | convolution fusion | flops 1092878336 | bytes 27806208 | tf_op jit(solution)/shard_map/dot_general | solution.py:95
  130.2 317.1 %while.15 = (s32[]{:T(128)}, f32[16,4096]{1,0:T(8,128)S(1)}, f32[32,16,4096]{2,1,0:T(8,128)}, f32[32,16,4096]{2,1,0:T(8,128)}, f32[16,4096]{1,0:T(8,128)S(1)}, /...) while((s32[]{:T(128)}, f32[16,4096]{1,0:T(8,128)S(1)}, ...), condition=%wide.region_19.20_spmd, body=%wide.region_2.19_spmd.sunk | while | flops 9371684 | bytes 6959107 | solution.py:28
  130.8 3.1 constant_dynamic-slice_fusion.67
  140.5 3.7 constant_dynamic-slice_fusion.67
  150.7 3.5 constant_dynamic-slice_fusion.67
  160.7 3.5 constant_dynamic-slice_fusion.67
  170.7 3.5 constant_dynamic-slice_fusion.67
  180.7 3.3 constant_dynamic-slice_fusion.67
  190.5 3.1 constant_dynamic-slice_fusion.67
  200.1 3.2 constant_dynamic-slice_fusion.67
  219.5 3.7 constant_dynamic-slice_fusion.67
  229.7 3.3 constant_dynamic-slice_fusion.67
  239.5 3.4 constant_dynamic-slice_fusion.67
  249.4 3.6 constant_dynamic-slice_fusion.67
  259.5 3.2 constant_dynamic-slice_fusion.67
  269.2 3.6 constant_dynamic-slice_fusion.67
  279.3 3.5 constant_dynamic-slice_fusion.67
  289.3 3.2 constant_dynamic-slice_fusion.67
  299.1 3.2 constant_dynamic-slice_fusion.67
  308.9 3.4 constant_dynamic-slice_fusion.67
  318.8 3.4 constant_dynamic-slice_fusion.67
  328.7 3.6 constant_dynamic-slice_fusion.67
  338.8 3.5 constant_dynamic-slice_fusion.67
  348.8 3.5 constant_dynamic-slice_fusion.67
  358.8 3.3 constant_dynamic-slice_fusion.67
  368.6 3.2 constant_dynamic-slice_fusion.67
  378.3 3.5 constant_dynamic-slice_fusion.67
  388.3 3.5 constant_dynamic-slice_fusion.67
  398.3 3.4 constant_dynamic-slice_fusion.67
  408.3 3.5 constant_dynamic-slice_fusion.67
  418.3 3.4 constant_dynamic-slice_fusion.67
  428.2 3.5 constant_dynamic-slice_fusion.67
  438.2 3.2 constant_dynamic-slice_fusion.67
  450.6 23.4 %reduce = bf16[4096,16]{1,0:T(8,128)(2,1)} reduce(bf16[4096,1,16]{2,1,0:T(2,128)(2,1)S(1)} %bitcast.294, bf16[]{:T(256)} %broadcast.127), dimensions={1}, to_apply=%bitcast.124.reduce_sub_computation | reduce | bytes 262146
  477.1 8.9 %all-to-all-start.2 = ((bf16[64,2,512]{2,1,0:T(2,128)(2,1)}), bf16[64,2,512]{2,1,0:T(2,128)(2,1)S(1)}, u32[]{:S(2)}, u32[]{:S(2)}) async-start(bf16[64,2,512]{2,1,0:T(2,128)(2,1)} %reshape.177), calls=%async_computation.2 | async-start | bytes 262144 | tf_op jit(solution)/shard_map/all_to_all | solution.py:104
  486.0 10.8 %fusion.6 = bf16[512,4096]{1,0:T(8,128)(2,1)} fusion(bf16[512,4096]{1,0:T(8,128)(2,1)} %param.18, f32[512,4096]{1,0:T(8,128)} %copy-done.2, f32[32,16,4096]{2,1,0:T(8,128)} %get-tuple-element.143, f32[4096]{0:T(1024)S(1)} %copy-done.6, pred[512]{0:T(512)(128)(4,1)} %copy-done.8), kind=kLoop, calls=%fused_computation.116 | loop fusion | flops 20971520 | bytes 25182720 | tf_op jit(solution)/shard_map/convert_element_type | solution.py:101
  497.1 3.9 reshape.178
  501.0 4.4 copy.84
  508.6 5.2 %scatter_fusion = f32[128,16,64]{2,1,0:T(8,128)S(1)} fusion(f32[128,16,64]{2,1,0:T(8,128)S(1)} %bitcast.296, s32[64]{0:T(128)} %copy-done.7, f32[64,16,64]{2,1,0:T(8,128)} %copy.85), kind=kCustom, calls=%fused_computation.2 | custom fusion | bytes 786688 | tf_op jit(solution)/shard_map/scatter | solution.py:115
  (1341 shorter events, 240.3 us)
Async XLA Ops:
  7.2 50.9 %copy-start = (bf16[4096,288]{0,1:T(8,128)(2,1)S(1)}, bf16[4096,288]{0,1:T(8,128)(2,1)}, u32[]{:S(2)}) copy-start(bf16[4096,288]{0,1:T(8,128)(2,1)} %param.21) | copy-start | bytes 7077892
  7.2 37.0 %copy-start.5 = (f32[4096]{0:T(1024)S(1)}, f32[4096]{0:T(1024)}, u32[]{:S(2)}) copy-start(f32[4096]{0:T(1024)} %param.20) | copy-start | bytes 49156
  9.0 98.3 %copy-start.7 = (s32[64]{0:T(128)}, s32[64]{0:T(128)S(1)}, u32[]{:S(2)}) copy-start(s32[64]{0:T(128)S(1)} %get-tuple-element.348) | copy-start | bytes 772
  10.3 23.1 %all-to-all-start.1 = ((bf16[64,3,64]{2,1,0:T(4,128)(2,1)}), bf16[64,3,64]{2,1,0:T(4,128)(2,1)S(1)}, u32[]{:S(2)}, u32[]{:S(2)}) async-start(bf16[64,3,64]{2,1,0:T(4,128)(2,1)} %gather_fusion.1), calls=%async_computation.1 | async-start | bytes 131072 | tf_op jit(solution)/shard_map/all_to_all | solution.py:69
  38.4 55.4 %all-to-all-start.3 = ((bf16[1,3,4096]{1,0,2:T(2,128)(2,1)}), bf16[1,3,4096]{1,0,2:T(2,128)(2,1)}, u32[]{:S(2)}, u32[]{:S(2)}) async-start(bf16[1,3,4096]{1,0,2:T(2,128)(2,1)} %copy.87), calls=%async_computation.3 | async-start | bytes 4194304 | tf_op jit(solution)/shard_map/all_to_all | solution.py:107
  44.2 68.4 %all-reduce.4.cloned.1.call-start = ((), (), s32[]{:S(2)}) async-start(), calls=%async_computation.4 | async-start | bytes 1179648 | tf_op jit(solution)/shard_map/psum | solution.py:87
  54.8 3.2 copy-start.2
  58.1 42.7 %copy-start.3 = (f32[16,4096]{1,0:T(8,128)S(1)}, f32[16,4096]{1,0:T(8,128)}, u32[]{:S(2)}) copy-start(f32[16,4096]{1,0:T(8,128)} %param.24) | copy-start | bytes 786436
  58.1 44.3 %copy-start.4 = (bf16[128,1,3,64]{0,3,2,1:T(8,128)(2,1)S(1)}, bf16[128,1,3,64]{0,3,2,1:T(8,128)(2,1)}, u32[]{:S(2)}) copy-start(bf16[128,1,3,64]{0,3,2,1:T(8,128)(2,1)} %param.27) | copy-start | bytes 147460
  58.1 56.5 %copy-start.9 = (f32[4096]{0:T(1024)S(1)}, f32[4096]{0:T(1024)}, u32[]{:S(2)}) copy-start(f32[4096]{0:T(1024)} %param.23) | copy-start | bytes 49156
  93.8 18.1 %all-to-all-start = ((bf16[64,2,512]{2,1,0:T(2,128)(2,1)}), bf16[64,2,512]{2,1,0:T(2,128)(2,1)S(1)}, u32[]{:S(2)}, u32[]{:S(2)}) async-start(bf16[64,2,512]{2,1,0:T(2,128)(2,1)} %reshape.175), calls=%async_computation | async-start | bytes 262144 | tf_op jit(solution)/shard_map/all_to_all | solution.py:66
  102.6 27.6 %copy-start.8 = (pred[512]{0:T(512)(128)(4,1)}, pred[512]{0:T(512)(128)(4,1)S(1)}, u32[]{:S(2)}) copy-start(pred[512]{0:T(512)(128)(4,1)S(1)} %iota_compare_fusion) | copy-start | bytes 1540
  130.2 355.8 %copy-start.6 = (f32[4096]{0:T(1024)S(1)}, f32[4096]{0:T(1024)}, u32[]{:S(2)}) copy-start(f32[4096]{0:T(1024)} %param.25) | copy-start | bytes 49156
  477.1 20.0 %all-to-all-start.2 = ((bf16[64,2,512]{2,1,0:T(2,128)(2,1)}), bf16[64,2,512]{2,1,0:T(2,128)(2,1)S(1)}, u32[]{:S(2)}, u32[]{:S(2)}) async-start(bf16[64,2,512]{2,1,0:T(2,128)(2,1)} %reshape.177), calls=%async_computation.2 | async-start | bytes 262144 | tf_op jit(solution)/shard_map/all_to_all | solution.py:104
  486.0 29.1 %copy-start.1 = (bf16[4096,288]{0,1:T(8,128)(2,1)S(1)}, bf16[4096,288]{0,1:T(8,128)(2,1)}, u32[]{:S(2)}) copy-start(bf16[4096,288]{0,1:T(8,128)(2,1)} %param.21) | copy-start | bytes 7077892
Sparse Core Ops, SparseCore 0:
  60.5 47.7 all-reduce.3
where the time goes:
time: 523 us; the launch traced here: 522 us
  local copies, waits for them, and re-layouts  280 us (54%)
  other arithmetic  132 us (25%)
  waiting for transfers between devices  39.9 us (8%)
  starting transfers between devices  34.7 us (7%)
  matrix products  17.9 us (3%)
  between operations  15.6 us (3%)
    slice x32, local copies, waits for them, and re-layouts, step_block(): drive_block[position][None, :]  108 us
    reduce_sum x160, other arithmetic, step_block(): results.append(jnp.sum(c_block[:, position][:, None] * state, axis=0))  83.9 us
    while x1024, local copies, waits for them, and re-layouts  81 us
    all_to_all x1, waiting for transfers between devices, local(): lax.all_to_all(edge_next.astype(jnp.float32)[None].astype(jnp.bfloat16),...  33.4 us
    unnamed x1, other arithmetic  23.4 us
    dynamic_update_slice x32, local copies, waits for them, and re-layouts, run_blocks(): lax.scan(step_block, (start_state, jnp.int32(0)), (step_size.reshape(-1,...  23.4 us
    unnamed x31, local copies, waits for them, and re-layouts  18.1 us
    dot_general x1, matrix products, local(): jnp.dot(normed, step_weight, preferred_element_type=jnp.float32) + step_bias  15.6 us
  transfers between devices with their start and end apart: 5, of which 4 were waited for; matrix products, arithmetic and copies ran while one was open for 7% of the time, Pallas kernels for 0%

commit v1 on v0

v1 whole, which is shorter than its diff:
```python
import functools

import jax
import jax.numpy as jnp
from jax import lax
from jax.experimental import pallas as pl
from jax.experimental.pallas import tpu as pltpu
from jax.sharding import PartitionSpec as P

STATE = 16
CONV = 4
RANK = 256
HALO = 16
WIDE = 1024
LANES = 128
SUBLANES = 8
LOG2E = 1.4426950408889634
F32 = jnp.float32
BF16 = jnp.bfloat16
VMEM_LIMIT = 48 * 1024 * 1024


def conv_kernel(prev_ref, x_ref, weight_ref, bias_ref, select_ref, mixed_ref, part_ref, send_ref, rows_scr, low_scr):
    rows = x_ref.shape[0]
    groups = x_ref.shape[1] // LANES
    for group in range(groups):
        at = slice(group * LANES, (group + 1) * LANES)
        scr = rows_scr.at[group]
        scr[0:HALO, :] = prev_ref[:, at].astype(F32)
        scr[HALO : HALO + rows, :] = x_ref[:, at].astype(F32)
        total = bias_ref[:, at] + weight_ref[CONV - 1 : CONV, at] * scr[HALO : HALO + rows, :]
        for tap in range(CONV - 1):
            first = HALO - (CONV - 1) + tap
            total = total + weight_ref[tap : tap + 1, at] * scr[first : first + rows, :]
        mixed = total / (1.0 + jnp.exp(-total))
        mixed_ref[:, at] = mixed
        low_scr[:, at] = mixed.astype(BF16)
    part = lax.dot_general(
        select_ref[...], low_scr[...], (((1,), (1,)), ((), ())), preferred_element_type=F32
    ).T
    part_ref[...] = part
    send_ref[...] = part.astype(BF16)


def conv_rows(prev, x, weight, bias, select_t, first_row, n_rows, block):
    channels = x.shape[1]
    wide = select_t.shape[0]
    first = first_row // block
    if prev is None:
        prev = x
        prev_spec = pl.BlockSpec((HALO, channels), lambda i: ((first + i) * (block // HALO) - 1, 0))
    else:
        prev_spec = pl.BlockSpec((HALO, channels), lambda i: (0, 0))
    return pl.pallas_call(
        conv_kernel,
        grid=(n_rows // block,),
        in_specs=[
            prev_spec,
            pl.BlockSpec((block, channels), lambda i: (first + i, 0)),
            pl.BlockSpec((CONV, channels), lambda i: (0, 0)),
            pl.BlockSpec((1, channels), lambda i: (0, 0)),
            pl.BlockSpec((wide, channels), lambda i: (0, 0)),
        ],
        out_specs=[
            pl.BlockSpec((block, channels), lambda i: (i, 0)),
            pl.BlockSpec((block, wide), lambda i: (i, 0)),
            pl.BlockSpec((block, wide), lambda i: (i, 0)),
        ],
        out_shape=[
            jax.ShapeDtypeStruct((n_rows, channels), F32),
            jax.ShapeDtypeStruct((n_rows, wide), F32),
            jax.ShapeDtypeStruct((n_rows, wide), BF16),
        ],
        scratch_shapes=[
            pltpu.VMEM((channels // LANES, HALO + block, LANES), F32),
            pltpu.VMEM((block, channels), BF16),
        ],
        compiler_params=pltpu.CompilerParams(vmem_limit_bytes=VMEM_LIMIT),
        cost_estimate=pl.CostEstimate(
            flops=2 * n_rows * channels * wide,
            bytes_accessed=n_rows * channels * 24,
            transcendentals=2 * n_rows * channels,
        ),
        name="conv_rows",
    )(prev, x, weight, bias, select_t)


def scan_kernel(
    length_ref, own_ref, got1_ref, got2_ref, got3_ref, step_ref, bias_ref, decay_ref, skip_ref, mixed_ref, gate_ref,
    start_ref, *rest, first_row, aliased
):
    if aliased:
        rest = rest[1:]
    out_ref, end_ref, norm_scr, wide_scr, size_scr, drive_scr, scan_scr, state_scr, rate_scr = rest
    channel_block, row_block = pl.program_id(0), pl.program_id(1)
    rows = mixed_ref.shape[0]
    at_rows = pl.ds(pl.multiple_of(row_block * rows, rows), rows)

    @pl.when(channel_block == 0)
    def _():
        projected = (own_ref[...] + got1_ref[...].astype(F32)) + (
            got2_ref[...].astype(F32) + got3_ref[...].astype(F32)
        )
        low = projected[:, :RANK]
        scale = lax.rsqrt(jnp.mean(low * low, axis=-1, keepdims=True) + 1e-06)
        norm_scr[at_rows, :] = (low * scale).astype(BF16)
        picks = projected[:, RANK:]
        high = picks.astype(BF16)
        both = jnp.concatenate([high, (picks - high.astype(F32)).astype(BF16)], axis=1)
        shape = (4 * STATE, 2 * STATE * LANES)
        source = lax.broadcasted_iota(jnp.int32, shape, 0) % (2 * STATE)
        spread = (source == lax.broadcasted_iota(jnp.int32, shape, 1) // LANES).astype(BF16)
        wide_scr[at_rows, :] = jnp.dot(both, spread, preferred_element_type=F32)

    @pl.when(row_block == 0)
    def _():
        state_scr[...] = start_ref[0]
        rate = -jnp.exp(decay_ref[...]) * LOG2E
        for sub in range(SUBLANES):
            rate_scr[pl.ds(sub, STATE, stride=SUBLANES), :] = rate[:, sub * LANES : (sub + 1) * LANES]

    value = jnp.dot(norm_scr[at_rows, :], step_ref[...], preferred_element_type=F32) + bias_ref[...]
    row = first_row + row_block * rows + lax.broadcasted_iota(jnp.int32, (rows, 1), 0)
    live = row < length_ref[0]
    size = jnp.maximum(value, 0.0) + jnp.log1p(jnp.exp(-jnp.abs(value)))
    size = jnp.where(live, size, 0.0)
    drive = size * mixed_ref[...]
    for sub in range(SUBLANES):
        at = slice(sub * LANES, (sub + 1) * LANES)
        size_scr[pl.ds(sub, rows, stride=SUBLANES), :] = size[:, at]
        drive_scr[pl.ds(sub, rows, stride=SUBLANES), :] = drive[:, at]

    rates = [rate_scr[n * SUBLANES : (n + 1) * SUBLANES, :] for n in range(STATE)]

    def eight_rows(step, state):
        state = list(state)
        first = pl.multiple_of(row_block * rows + step * SUBLANES, SUBLANES)
        picks = wide_scr.at[pl.ds(first, SUBLANES), :]
        for position in range(SUBLANES):
            here = pl.ds(pl.multiple_of((step * SUBLANES + position) * SUBLANES, SUBLANES), SUBLANES)
            size_row, drive_row = size_scr[here, :], drive_scr[here, :]
            sums = [None, None]
            for n in range(STATE):
                b = jnp.broadcast_to(picks[position : position + 1, n * LANES : (n + 1) * LANES], (SUBLANES, LANES))
                m = STATE + n
                c = jnp.broadcast_to(picks[position : position + 1, m * LANES : (m + 1) * LANES], (SUBLANES, LANES))
                state[n] = jnp.exp2(size_row * rates[n]) * state[n] + b * drive_row
                term = c * state[n]
                sums[n % 2] = term if sums[n % 2] is None else sums[n % 2] + term
            scan_scr[here, :] = sums[0] + sums[1]
        return tuple(state)

    state = lax.fori_loop(0, rows // SUBLANES, eight_rows, tuple(state_scr[n] for n in range(STATE)))
    for n in range(STATE):
        state_scr[n] = state[n]

    gate = gate_ref[...].astype(F32)
    gate = gate / (1.0 + jnp.exp(-gate))
    direct = skip_ref[...] * mixed_ref[...]
    for sub in range(SUBLANES):
        at = slice(sub * LANES, (sub + 1) * LANES)
        scanned = scan_scr[pl.ds(sub, rows, stride=SUBLANES), :]
        out_ref[:, at] = jnp.where(live, (scanned + direct[:, at]) * gate[:, at], 0.0).astype(BF16)

    @pl.when(row_block == pl.num_programs(1) - 1)
    def _():
        end_ref[0] = state_scr[...]


def scan_rows(length, parts, step_weight, step_bias, decay_log, skip_gain, mixed, gate, start, out, first_row, block):
    n_rows, channels = mixed.shape
    blocks = channels // WIDE
    first = first_row // block
    wide = parts[0].shape[1]
    by_channel = lambda c, i, *_: (0, c)
    part_spec = pl.BlockSpec((block, wide), lambda c, i, *_: (jnp.where(c == 0, i, 0), 0))
    state_spec = pl.BlockSpec((1, STATE, SUBLANES, LANES), lambda c, i, *_: (c, 0, 0, 0))
    operands = [length, *parts, step_weight, step_bias, decay_log, skip_gain, mixed, gate, start]
    in_specs = [part_spec] * 4 + [
        pl.BlockSpec((RANK, WIDE), by_channel),
        pl.BlockSpec((1, WIDE), by_channel),
        pl.BlockSpec((STATE, WIDE), by_channel),
        pl.BlockSpec((1, WIDE), by_channel),
        pl.BlockSpec((block, WIDE), lambda c, i, *_: (i, c)),
        pl.BlockSpec((block, WIDE), lambda c, i, *_: (first + i, c)),
        state_spec,
    ]
    aliases = {}
    if out is not None:
        aliases = {len(operands): 0}
        operands.append(out)
        in_specs.append(pl.BlockSpec(memory_space=pl.ANY))
    return pl.pallas_call(
        functools.partial(scan_kernel, first_row=first_row, aliased=out is not None),
        grid_spec=pltpu.PrefetchScalarGridSpec(
            num_scalar_prefetch=1,
            grid=(blocks, n_rows // block),
            in_specs=in_specs,
            out_specs=[pl.BlockSpec((block, WIDE), lambda c, i, *_: (first + i, c)), state_spec],
            scratch_shapes=[
                pltpu.VMEM((n_rows, RANK), BF16),
                pltpu.VMEM((n_rows, 2 * STATE * LANES), F32),
                pltpu.VMEM((block * SUBLANES, LANES), F32),
                pltpu.VMEM((block * SUBLANES, LANES), F32),
                pltpu.VMEM((block * SUBLANES, LANES), F32),
                pltpu.VMEM((STATE, SUBLANES, LANES), F32),
                pltpu.VMEM((STATE * SUBLANES, LANES), F32),
            ],
        ),
        out_shape=[
            jax.ShapeDtypeStruct(gate.shape, BF16),
            jax.ShapeDtypeStruct((blocks, STATE, SUBLANES, LANES), F32),
        ],
        input_output_aliases=aliases,
        compiler_params=pltpu.CompilerParams(vmem_limit_bytes=VMEM_LIMIT),
        cost_estimate=pl.CostEstimate(
            flops=2 * n_rows * channels * RANK + 100 * n_rows * channels * STATE,
            bytes_accessed=n_rows * channels * 8,
            transcendentals=n_rows * channels * STATE,
        ),
        name="scan_rows",
    )(*operands)


def from_others(sent, n_tp):
    return [lax.ppermute(sent, "tp", [(d, (d + s) % n_tp) for d in range(n_tp)]) for s in range(1, n_tp)]


def local(
    n_req,
    n_tp,
    conv_input,
    gate_input,
    conv_weight,
    conv_bias,
    select_weight,
    step_weight,
    step_bias,
    decay_log,
    skip_gain,
    store_state,
    store_edge,
    read_slot,
    save_slot,
    cache_hit,
    suffix_length,
):
    local_rows, channels = conv_input.shape
    slots, _, _, stripe = store_state.shape
    edge_rows = CONV - 1
    n_state, n_edge = STATE * stripe, edge_rows * stripe
    is_hit = cache_hit[0] > 0
    length = suffix_length[0]
    store = store_state.transpose(1, 2, 3, 0).reshape(n_state, slots)
    edges = store_edge.transpose(1, 2, 3, 0).reshape(n_edge, slots)

    slot_ids = jnp.arange(slots, dtype=jnp.int32)
    reads = (read_slot[:, None] == slot_ids[None, :]).astype(BF16)
    contract_slots = (((1,), (1,)), ((), ()))
    held_state = lax.dot_general(reads, store.astype(BF16), contract_slots, preferred_element_type=F32)
    held_edge = lax.dot_general(reads, edges, contract_slots, preferred_element_type=F32)
    edge_next = lax.dynamic_slice_in_dim(conv_input, length - edge_rows, edge_rows, 0)
    edge_next = edge_next.reshape(edge_rows, n_req, stripe).transpose(1, 0, 2).reshape(n_req, n_edge)
    outgoing = jnp.concatenate([held_state.astype(BF16), held_edge.astype(BF16), edge_next], axis=1)
    arrived = lax.all_to_all(outgoing, "req", split_axis=0, concat_axis=0, tiled=True)

    select_t = select_weight.T
    conv_bias = conv_bias.reshape(1, channels)
    step_bias = step_bias.reshape(1, channels)
    skip_gain = skip_gain.reshape(1, channels)
    block = min(128, local_rows // 2)
    conv = functools.partial(conv_rows, block=block)
    late_mixed, late_part, late_send = conv(
        None, conv_input, conv_weight, conv_bias, select_t, block, local_rows - block
    )
    late_parts = [late_part] + from_others(late_send, n_tp)

    got = jnp.where(is_hit, arrived[:, : n_state + n_edge], 0)
    start = got[:, :n_state].astype(F32).reshape(n_req, STATE, stripe).transpose(1, 0, 2)
    start = start.reshape(STATE, channels // WIDE, SUBLANES, LANES).transpose(1, 0, 2, 3)
    edge = got[:, n_state:].reshape(n_req, edge_rows, stripe).transpose(1, 0, 2).reshape(edge_rows, channels)
    edge = jnp.pad(edge, ((HALO - edge_rows, 0), (0, 0)))
    early_mixed, early_part, early_send = conv(edge, conv_input, conv_weight, conv_bias, select_t, 0, block)
    early_parts = [early_part] + from_others(early_send, n_tp)

    scan = functools.partial(scan_rows, block=block)
    shared = (step_weight, step_bias, decay_log, skip_gain)
    out, state = scan(suffix_length, early_parts, *shared, early_mixed, gate_input, start, None, 0)
    out, state = scan(suffix_length, late_parts, *shared, late_mixed, gate_input, state, out, block)

    back = state.astype(BF16).reshape(channels // WIDE, STATE, SUBLANES, LANES // stripe, stripe)
    back = back.transpose(0, 2, 3, 1, 4).reshape(n_req, n_state)
    back = lax.all_to_all(back, "req", split_axis=0, concat_axis=0, tiled=True)
    saves = (save_slot[:, None] == slot_ids[None, :]).astype(BF16)
    saved = jnp.any(save_slot[:, None] == slot_ids[None, :], axis=0)[None, :]
    contract_requests = (((0,), (0,)), ((), ()))
    new_store = lax.dot_general(back, saves, contract_requests, preferred_element_type=F32)
    new_store = jnp.where(saved, new_store, store)
    new_edges = lax.dot_general(
        arrived[:, n_state + n_edge :], saves, contract_requests, preferred_element_type=F32
    ).astype(BF16)
    new_edges = jnp.where(saved, new_edges, edges)
    new_state = new_store.reshape(1, STATE, stripe, slots).transpose(3, 0, 1, 2)
    new_edge_store = new_edges.reshape(1, edge_rows, stripe, slots).transpose(3, 0, 1, 2)
    return (out, new_state, new_edge_store)


def solution(mesh):
    placed = (
        P("req", "tp"),
        P("req", "tp"),
        P(None, "tp"),
        P("tp"),
        P("tp", None),
        P(None, "tp"),
        P("tp"),
        P(None, "tp"),
        P("tp"),
        P(None, "req", None, "tp"),
        P(None, "req", None, "tp"),
        P(),
        P(),
        P("req"),
        P("req"),
    )
    return jax.shard_map(
        functools.partial(local, mesh.shape["req"], mesh.shape["tp"]),
        mesh=mesh,
        in_specs=placed,
        out_specs=(P("req", "tp"), P(None, "req", None, "tp"), P(None, "req", None, "tp")),
        check_vma=False,
    )
```

time: 523 us -> 149 us (0.28)
  local copies, waits for them, and re-layouts: 280 us -> 11.8 us
  other arithmetic: 132 us -> 3.29 us
  Pallas kernels: 0 us -> 64.2 us
  matrix products: 17.9 us -> 4.62 us
  between operations: 15.6 us -> 2.39 us
  starting transfers between devices: 34.7 us -> 25.4 us
    slice x66 -> x2, local copies, waits for them, and re-layouts: 115 us -> 0.02 us  [the longest x1 0.02 us: local(): got[:, :n_state].astype(F32).reshape(n_req, STATE, stripe)]
    reduce_sum x161 -> x0, other arithmetic: 85 us -> none  [the longest x160 83.9 us: step_block(): results.append(jnp.sum(c_block[:, position][:, None] * state, axis=0))]
    while x1024 -> x0, local copies, waits for them, and re-layouts: 81 us -> none
    pallas_call x0 -> x4, Pallas kernels: none -> 64.2 us  [the longest x2 52 us: scan_rows(): pl.pallas_call(functools.partial(scan_kernel, first_row=first_row, aliase...]
    unnamed x1 -> x0, other arithmetic: 23.4 us -> none
    dynamic_update_slice x32 -> x0, local copies, waits for them, and re-layouts: 23.4 us -> none  [run_blocks(): lax.scan(step_block, (start_state, jnp.int32(0)), (step_size.reshape(-1,...]
    all_to_all x4 -> x2, waiting for transfers between devices: 39.8 us -> 21 us  [the longest x1 11.4 us: local(): lax.all_to_all(outgoing, 'req', split_axis=0, concat_axis=0, tiled=True)]
    all_to_all x4 -> x2, starting transfers between devices: 34.7 us -> 17.5 us  [the longest x1 13 us: local(): lax.all_to_all(outgoing, 'req', split_axis=0, concat_axis=0, tiled=True)]
  transfers between devices with their start and end apart: 5 -> 8, of which waited for: 4 -> 4; matrix products, arithmetic and copies ran while one was open for 7% -> 1% of each run, Pallas kernels for 0% -> 15%
where the time goes in v1:
time: 149 us; the launch traced here: 148 us
  Pallas kernels  64.2 us (43%)
  waiting for transfers between devices  36.7 us (25%)
  starting transfers between devices  25.4 us (17%)
  local copies, waits for them, and re-layouts  11.8 us (8%)
  matrix products  4.62 us (3%)
  other arithmetic  3.29 us (2%)
  between operations  2.39 us (2%)
    pallas_call x2, Pallas kernels, scan_rows(): pl.pallas_call(functools.partial(scan_kernel, first_row=first_row, aliase...  52 us
    ppermute x6, waiting for transfers between devices, from_others(): lax.ppermute(sent, 'tp', [(d, (d + s) % n_tp) for d in range(n_tp)])  15.7 us
    all_to_all x1, starting transfers between devices, local(): lax.all_to_all(outgoing, 'req', split_axis=0, concat_axis=0, tiled=True)  13 us
    pallas_call x2, Pallas kernels, conv_rows(): pl.pallas_call(conv_kernel, grid=(n_rows // block,), in_specs=[prev_spec,...  12.1 us
    all_to_all x1, waiting for transfers between devices, local(): lax.all_to_all(outgoing, 'req', split_axis=0, concat_axis=0, tiled=True)  11.4 us
    all_to_all x1, waiting for transfers between devices, local(): back = lax.all_to_all(back, 'req', split_axis=0, concat_axis=0, tiled=True)  9.61 us
    unnamed x40, local copies, waits for them, and re-layouts  8.33 us
    ppermute x6, starting transfers between devices, from_others(): lax.ppermute(sent, 'tp', [(d, (d + s) % n_tp) for d in range(n_tp)])  7.86 us
  transfers between devices with their start and end apart: 8, of which 4 were waited for; matrix products, arithmetic and copies ran while one was open for 1% of the time, Pallas kernels for 15%

profile of v1, /device:TPU:1, one launch (start us, length us, event | category | flops | bytes accessed | tf_op | source)
XLA Modules:
  0.0 148.4 jit_solution(6787605399710848783)
XLA Ops:
  1.5 0.9 constant_dynamic-slice_fusion
  2.4 0.1 reshape.70
  2.5 0.1 copy.36
  2.6 0.1 copy.37
  2.7 1.1 bitcast_convert_fusion
  3.8 1.0 convolution_convert_fusion.2
  4.8 0.9 convolution_convert_fusion
  5.7 0.1 concatenate.3
  5.8 0.5 broadcast.5
  6.3 0.7 reduce
  7.0 0.9 reshape.81
  7.9 13.0 %all-to-all-start = ((bf16[64,2,704]{2,1,0:T(2,128)(2,1)}), bf16[64,2,704]{2,1,0:T(2,128)(2,1)S(1)}, u32[]{:S(2)}, u32[]{:S(2)}) async-start(bf16[64,2,704]{2,1,0:T(2,128)(2,1)} %reshape.81), calls=%async_computation | async-start | bytes 393216 | tf_op jit(solution)/shard_map/all_to_all | solution.py:265
  21.5 11.4 %all-to-all-done = bf16[64,2,704]{2,1,0:T(2,128)(2,1)S(1)} async-done(((bf16[64,2,704]{2,1,0:T(2,128)(2,1)}), bf16[64,2,704]{2,1,0:T(2,128)(2,1)S(1)}, u32[]{:S(2)}, u32[]{:S(2)}) %all-to-all-start) | async-done | bytes 180256 | tf_op jit(solution)/shard_map/all_to_all | solution.py:265
  32.9 0.2 reshape.82
  33.2 0.8 copy.39
  34.0 0.1 copy.40
  34.1 0.7 copy-done.14
  34.8 0.1 reshape.73
  34.9 3.8 %conv_rows.3 = (f32[128,4096]{1,0:T(8,128)S(1)}, f32[128,288]{1,0:T(8,128)S(1)}, bf16[128,288]{1,0:T(8,128)(2,1)}) custom-call(bf16[16,4096]{1,0:T(8,128)(2,1)S(1)} %pad.4.prev_ref, bf16[512,4096]{1,0:T(8,128)(2,1)} %x_ref.3, f32[4,4096]{1,0:T(4,128)S(1)} %copy-done.1, f32[1,4096]{1,0:T(1,128)S(1)} %bitcast.48, bf16[288,4096]{1,0:T(8,128)(2,1)S(1)} %bitcast.45), custom_call_target="tpu_custom_call" | custom-call | flops 301989888 | bytes 12582912 | tf_op jit(solution)/shard_map/conv_rows/pallas_call | solution.py:54
  38.8 0.0 copy-start.11
  38.8 2.8 %collective-permute-start.5 = (bf16[128,288]{1,0:T(8,128)(2,1)}, bf16[128,288]{1,0:T(8,128)(2,1)S(1)}, u32[]{:S(2)}, u32[]{:S(2)}) collective-permute-start(bf16[128,288]{1,0:T(8,128)(2,1)} %get-tuple-element.17), channel_id=1, source_target_pairs={{0,3},{1,0},{2,1},{3,2},{4,7},{5,4},{6,5},{7,6},{8,11},{9,8},{10,9... | collective-permute-start | bytes 221192 | tf_op jit(solution)/shard_map/ppermute | solution.py:226
  41.6 8.3 %conv_rows.2 = (f32[384,4096]{1,0:T(8,128)}, f32[384,288]{1,0:T(8,128)S(1)}, bf16[384,288]{1,0:T(8,128)(2,1)S(1)}) custom-call(bf16[512,4096]{1,0:T(8,128)(2,1)} %x_ref.3, bf16[512,4096]{1,0:T(8,128)(2,1)} %x_ref.3, f32[4,4096]{1,0:T(4,128)S(1)} %copy-done.1, f32[1,4096]{1,0:T(1,128)S(1)} %bitcast.49, bf16[288,4096]{1,0:T(8,128)(2,1)S(1)} %bitcast.46), custom_call_target="tpu_custom_call" | custom-call | flops 905969664 | bytes 37748736 | tf_op jit(solution)/shard_map/conv_rows/pallas_call | solution.py:54
  49.9 0.8 collective-permute-start.2
  50.7 0.4 collective-permute-start.1
  51.0 0.7 collective-permute-start
  51.7 3.2 %collective-permute-start.4 = (bf16[128,288]{1,0:T(8,128)(2,1)}, bf16[128,288]{1,0:T(8,128)(2,1)S(1)}, u32[]{:S(2)}, u32[]{:S(2)}) collective-permute-start(bf16[128,288]{1,0:T(8,128)(2,1)} %get-tuple-element.17), channel_id=1, source_target_pairs={{0,2},{1,3},{2,0},{3,1},{4,6},{5,7},{6,4},{7,5},{8,10},{9,11},{10,... | collective-permute-start | bytes 221192 | tf_op jit(solution)/shard_map/ppermute | solution.py:226
  55.0 0.6 copy-done.8
  55.6 0.1 copy.41
  55.8 0.1 reshape.79
  55.9 12.3 %collective-permute-done.4.got2_ref = bf16[128,288]{1,0:T(8,128)(2,1)S(1)} collective-permute-done((bf16[128,288]{1,0:T(8,128)(2,1)}, bf16[128,288]{1,0:T(8,128)(2,1)S(1)}, u32[]{:S(2)}, u32[]{:S(2)}) %collective-permute-start.4) | collective-permute-done | bytes 73760 | tf_op jit(solution)/shard_map/ppermute | solution.py:226
  68.3 3.4 %collective-permute-done.3.got1_ref = bf16[128,288]{1,0:T(8,128)(2,1)S(1)} collective-permute-done((bf16[128,288]{1,0:T(8,128)(2,1)}, bf16[128,288]{1,0:T(8,128)(2,1)S(1)}, u32[]{:S(2)}, u32[]{:S(2)}) %collective-permute-start.3) | collective-permute-done | bytes 73760 | tf_op jit(solution)/shard_map/ppermute | solution.py:226
  71.6 1.6 %copy-done.3 = bf16[256,4096]{1,0:T(8,128)(2,1)S(1)} copy-done((bf16[256,4096]{1,0:T(8,128)(2,1)S(1)}, bf16[256,4096]{1,0:T(8,128)(2,1)}, u32[]{:S(2)}) %copy-start.3) | copy-done | bytes 2097176
  73.2 1.6 %copy-done.6 = f32[128,4096]{1,0:T(8,128)S(1)} copy-done((f32[128,4096]{1,0:T(8,128)S(1)}, f32[128,4096]{1,0:T(8,128)}, u32[]{:S(2)}) %copy-start.6) | copy-done | bytes 2097176
  74.8 0.9 copy-done.7
  75.8 0.9 copy-done.9
  76.7 14.3 %scan_rows.2 = (bf16[512,4096]{1,0:T(8,128)(2,1)}, f32[4,16,8,128]{3,2,1,0:T(8,128)S(1)}) custom-call(s32[1]{0:T(128)S(6)} %copy.57.length_ref, f32[128,288]{1,0:T(8,128)S(1)} %get-tuple-element.16.own_ref, bf16[128,288]{1,0:T(8,128)(2,1)S(1)} %collective-permute-done.3.got1_ref, bf16[128,288]{1,0:T(8,128)(2,1)S(1)} %collective-permute-done.4.got2_ref, ...), custom_call_target="tpu_custom_call" | custom-call | flops 1107296256 | bytes 4194304 | tf_op jit(solution)/shard_map/scan_rows/pallas_call | solution.py:193
  91.0 37.7 %scan_rows.3 = (bf16[512,4096]{1,0:T(8,128)(2,1)}, f32[4,16,8,128]{3,2,1,0:T(8,128)S(1)}) custom-call(s32[1]{0:T(128)S(6)} %copy.57.length_ref, f32[384,288]{1,0:T(8,128)S(1)} %get-tuple-element.13.own_ref, bf16[384,288]{1,0:T(8,128)(2,1)S(1)} %collective-permute-done.got1_ref, ...), custom_call_target="tpu_custom_call", output_to_operand_aliasing={{0}: (12, {})} | custom-call | flops 3321888768 | bytes 12582912 | tf_op jit(solution)/shard_map/scan_rows/pallas_call | solution.py:193
  128.8 0.1 reshape.76
  128.9 0.1 copy.52
  129.0 0.2 all_to_all.22
  129.2 1.4 reduce.1
  130.6 0.7 reshape.83
  131.3 4.5 %all-to-all-start.1 = ((bf16[64,2,512]{2,1,0:T(2,128)(2,1)}), bf16[64,2,512]{2,1,0:T(2,128)(2,1)S(1)}, u32[]{:S(2)}, u32[]{:S(2)}) async-start(bf16[64,2,512]{2,1,0:T(2,128)(2,1)} %reshape.83), calls=%async_computation.1 | async-start | bytes 262144 | tf_op jit(solution)/shard_map/all_to_all | solution.py:293
  135.8 0.1 fusion.4
  135.9 1.6 %fusion = bf16[192,128]{1,0:T(8,128)(2,1)} fusion(bf16[192,128]{1,0:T(8,128)(2,1)S(1)} %bitcast.66, bf16[64,1408]{0,1:T(8,128)(2,1)} %bitcast.57, pred[128]{0:T(512)(128)(4,1)S(1)} %fusion.4, s32[64]{0:T(128)S(1)} %copy-done.17), kind=kOutput, calls=%fused_computation.3 | convolution fusion | flops 3203072 | bytes 147840 | tf_op jit(solution)/shard_map/dot_general | solution.py:299
  137.6 9.6 %all-to-all-done.1 = bf16[64,2,512]{2,1,0:T(2,128)(2,1)S(1)} async-done(((bf16[64,2,512]{2,1,0:T(2,128)(2,1)}), bf16[64,2,512]{2,1,0:T(2,128)(2,1)S(1)}, u32[]{:S(2)}, u32[]{:S(2)}) %all-to-all-start.1) | async-done | bytes 131104 | tf_op jit(solution)/shard_map/all_to_all | solution.py:293
  147.2 0.1 reshape.84
  147.3 1.1 convolution_select_fusion
  (40 shorter events, 0.2 us)
Async XLA Ops:
  0.6 34.3 %copy-start.1 = (f32[4,4096]{1,0:T(4,128)S(1)}, f32[4,4096]{1,0:T(4,128)}, u32[]{:S(2)}) copy-start(f32[4,4096]{1,0:T(4,128)} %weight_ref.3) | copy-start | bytes 196612
  0.6 34.3 %copy-start = (bf16[4096,288]{0,1:T(8,128)(2,1)S(1)}, bf16[4096,288]{0,1:T(8,128)(2,1)}, u32[]{:S(2)}) copy-start(bf16[4096,288]{0,1:T(8,128)(2,1)} %param.19) | copy-start | bytes 7077892
  0.7 34.3 %copy-start.2 = (f32[4096]{0:T(1024)S(1)}, f32[4096]{0:T(1024)}, u32[]{:S(2)}) copy-start(f32[4096]{0:T(1024)} %param.18) | copy-start | bytes 49156
  7.9 25.0 %all-to-all-start = ((bf16[64,2,704]{2,1,0:T(2,128)(2,1)}), bf16[64,2,704]{2,1,0:T(2,128)(2,1)S(1)}, u32[]{:S(2)}, u32[]{:S(2)}) async-start(bf16[64,2,704]{2,1,0:T(2,128)(2,1)} %reshape.81), calls=%async_computation | async-start | bytes 393216 | tf_op jit(solution)/shard_map/all_to_all | solution.py:265
  33.9 4.8 %copy-start.13 = (bf16[64,1,1408]{0,2,1:T(8,128)(2,1)}, bf16[64,1,1408]{0,2,1:T(8,128)(2,1)S(1)}, u32[]{:S(2)}) copy-start(bf16[64,1,1408]{0,2,1:T(8,128)(2,1)S(1)} %copy.39) | copy-start | bytes 540676
  34.0 0.8 copy-start.14
  38.8 11.1 %copy-start.5 = (f32[128,4096]{1,0:T(8,128)}, f32[128,4096]{1,0:T(8,128)S(1)}, u32[]{:S(2)}) copy-start(f32[128,4096]{1,0:T(8,128)S(1)} %get-tuple-element.18.mixed_ref) | copy-start | bytes 6291460
  38.8 16.8 %copy-start.15 = (bf16[64,1216]{0,1:T(8,128)(2,1)S(1)}, bf16[64,1216]{0,1:T(8,128)(2,1)}, u32[]{:S(2)}) copy-start(bf16[64,1216]{0,1:T(8,128)(2,1)} %copy-done.14) | copy-start | bytes 466948
  38.8 32.9 %copy-start.10 = (f32[4096]{0:T(1024)S(1)}, f32[4096]{0:T(1024)}, u32[]{:S(2)}) copy-start(f32[4096]{0:T(1024)} %param.21) | copy-start | bytes 49156
  38.8 32.9 %copy-start.11 = (f32[4096]{0:T(1024)S(1)}, f32[4096]{0:T(1024)}, u32[]{:S(2)}) copy-start(f32[4096]{0:T(1024)} %param.23) | copy-start | bytes 49156
  38.8 16.2 %collective-permute-start.5 = (bf16[128,288]{1,0:T(8,128)(2,1)}, bf16[128,288]{1,0:T(8,128)(2,1)S(1)}, u32[]{:S(2)}, u32[]{:S(2)}) collective-permute-start(bf16[128,288]{1,0:T(8,128)(2,1)} %get-tuple-element.17), channel_id=1, source_target_pairs={{0,3},{1,0},{2,1},{3,2},{4,7},{5,4},{6,5},{7,6},{8,11},{9,8},{10,9... | collective-permute-start | bytes 221192 | tf_op jit(solution)/shard_map/ppermute | solution.py:226
  49.9 41.1 %collective-permute-start.2 = (bf16[384,288]{1,0:T(8,128)(2,1)S(1)}, bf16[384,288]{1,0:T(8,128)(2,1)S(1)}, u32[]{:S(2)}, u32[]{:S(2)}) collective-permute-start(bf16[384,288]{1,0:T(8,128)(2,1)S(1)} %get-tuple-element.14), channel_id=1, source_target_pairs={{0,3},{1,0},{2,1},{3,2},{4,7},{5,4},{6,5},{7,6},{8,11},{9,8},{10,9... | collective-permute-start | bytes 663560 | tf_op jit(solution)/shard_map/ppermute | solution.py:226
  50.7 40.3 %collective-permute-start.1 = (bf16[384,288]{1,0:T(8,128)(2,1)S(1)}, bf16[384,288]{1,0:T(8,128)(2,1)S(1)}, u32[]{:S(2)}, u32[]{:S(2)}) collective-permute-start(bf16[384,288]{1,0:T(8,128)(2,1)S(1)} %get-tuple-element.14), channel_id=1, source_target_pairs={{0,2},{1,3},{2,0},{3,1},{4,6},{5,7},{6,4},{7,5},{8,10},{9,11},{10,... | collective-permute-start | bytes 663560 | tf_op jit(solution)/shard_map/ppermute | solution.py:226
  51.0 39.9 %collective-permute-start = (bf16[384,288]{1,0:T(8,128)(2,1)S(1)}, bf16[384,288]{1,0:T(8,128)(2,1)S(1)}, u32[]{:S(2)}, u32[]{:S(2)}) collective-permute-start(bf16[384,288]{1,0:T(8,128)(2,1)S(1)} %get-tuple-element.14), channel_id=1, source_target_pairs={{0,1},{1,2},{2,3},{3,0},{4,5},{5,6},{6,7},{7,4},{8,9},{9,10},{10,1... | collective-permute-start | bytes 663560 | tf_op jit(solution)/shard_map/ppermute | solution.py:226
  51.7 16.5 %collective-permute-start.4 = (bf16[128,288]{1,0:T(8,128)(2,1)}, bf16[128,288]{1,0:T(8,128)(2,1)S(1)}, u32[]{:S(2)}, u32[]{:S(2)}) collective-permute-start(bf16[128,288]{1,0:T(8,128)(2,1)} %get-tuple-element.17), channel_id=1, source_target_pairs={{0,2},{1,3},{2,0},{3,1},{4,6},{5,7},{6,4},{7,5},{8,10},{9,11},{10,... | collective-permute-start | bytes 221192 | tf_op jit(solution)/shard_map/ppermute | solution.py:226
  55.0 0.6 copy-start.8
  55.6 16.0 %collective-permute-start.3 = (bf16[128,288]{1,0:T(8,128)(2,1)}, bf16[128,288]{1,0:T(8,128)(2,1)S(1)}, u32[]{:S(2)}, u32[]{:S(2)}) collective-permute-start(bf16[128,288]{1,0:T(8,128)(2,1)} %get-tuple-element.17), channel_id=1, source_target_pairs={{0,1},{1,2},{2,3},{3,0},{4,5},{5,6},{6,7},{7,4},{8,9},{9,10},{10,1... | collective-permute-start | bytes 221192 | tf_op jit(solution)/shard_map/ppermute | solution.py:226
  71.6 1.6 %copy-start.3 = (bf16[256,4096]{1,0:T(8,128)(2,1)S(1)}, bf16[256,4096]{1,0:T(8,128)(2,1)}, u32[]{:S(2)}) copy-start(bf16[256,4096]{1,0:T(8,128)(2,1)} %step_ref.3) | copy-start | bytes 6291460
  73.2 1.6 %copy-start.6 = (f32[128,4096]{1,0:T(8,128)S(1)}, f32[128,4096]{1,0:T(8,128)}, u32[]{:S(2)}) copy-start(f32[128,4096]{1,0:T(8,128)} %copy-done.5) | copy-start | bytes 6291460
  74.8 0.9 copy-start.7
  75.8 0.9 copy-start.9
  76.7 14.3 %copy-start.4 = (bf16[256,4096]{1,0:T(8,128)(2,1)S(1)}, bf16[256,4096]{1,0:T(8,128)(2,1)}, u32[]{:S(2)}) copy-start(bf16[256,4096]{1,0:T(8,128)(2,1)} %step_ref.3) | copy-start | bytes 6291460
  91.0 44.8 %copy-start.17 = (s32[64]{0:T(128)S(1)}, s32[64]{0:T(128)}, u32[]{:S(2)}) copy-start(s32[64]{0:T(128)} %param.27) | copy-start | bytes 772
  91.0 44.9 %copy-start.16 = (bf16[128,1,3,64]{0,3,2,1:T(8,128)(2,1)S(1)}, bf16[128,1,3,64]{0,3,2,1:T(8,128)(2,1)}, u32[]{:S(2)}) copy-start(bf16[128,1,3,64]{0,3,2,1:T(8,128)(2,1)} %param.25) | copy-start | bytes 147460
  91.0 56.3 %copy-start.12 = (f32[128,1,16,64]{0,3,2,1:T(8,128)S(1)}, f32[128,1,16,64]{0,3,2,1:T(8,128)}, u32[]{:S(2)}) copy-start(f32[128,1,16,64]{0,3,2,1:T(8,128)} %param.24) | copy-start | bytes 1572868
  131.3 15.9 %all-to-all-start.1 = ((bf16[64,2,512]{2,1,0:T(2,128)(2,1)}), bf16[64,2,512]{2,1,0:T(2,128)(2,1)S(1)}, u32[]{:S(2)}, u32[]{:S(2)}) async-start(bf16[64,2,512]{2,1,0:T(2,128)(2,1)} %reshape.83), calls=%async_computation.1 | async-start | bytes 262144 | tf_op jit(solution)/shard_map/all_to_all | solution.py:293

commit v2 on v1

v2 whole, which is shorter than its diff:
```python
import functools

import jax
import jax.numpy as jnp
from jax import lax
from jax.experimental import pallas as pl
from jax.experimental.pallas import tpu as pltpu
from jax.sharding import PartitionSpec as P

STATE = 16
CONV = 4
RANK = 256
HALO = 16
WIDE = 1024
LANES = 128
SUBLANES = 8
LOG2E = 1.4426950408889634
F32 = jnp.float32
BF16 = jnp.bfloat16
HALF = 64
EDGE_AT = 8
NEXT_AT = 11
CHUNK = 16
FETCHES = 6
GROUPS_AT_ONCE = 4
VMEM_LIMIT = 60 * 1024 * 1024
SMALL_LIMIT = 24 * 1024 * 1024


def low_half():
    return lax.broadcasted_iota(jnp.int32, (1, LANES), 1) < HALF


def silu(v):
    half = 0.5 * v
    return half + half * jnp.tanh(half)


def pack_kernel(length_ref, read_ref, store_ref, edge_ref, x_ref, out_ref, tiles_scr, low_scr, rows_scr, sem):
    n_req = read_ref.shape[1]
    slots = store_ref.shape[1]
    edge_rows = CONV - 1
    last = length_ref[0] - edge_rows
    first = pl.multiple_of(jnp.minimum(last // HALO * HALO, x_ref.shape[0] - 2 * HALO), HALO)
    copy = pltpu.make_async_copy(x_ref.at[pl.ds(first, 2 * HALO), :], low_scr, sem)
    copy.start()
    reads = (lax.broadcasted_iota(jnp.int32, (slots, n_req), 0) == read_ref[...]).astype(BF16)
    for row in range(STATE // 2):
        held = lax.dot_general(
            reads, store_ref[row * LANES : (row + 1) * LANES, :].astype(BF16), (((0,), (1,)), ((), ())),
            preferred_element_type=F32,
        )
        tiles_scr[pl.ds(row, n_req, stride=CHUNK), :] = held
    for row in range(edge_rows):
        edge = edge_ref[row * HALF : (row + 1) * HALF, :]
        held = lax.dot_general(
            reads, jnp.concatenate([edge, edge], axis=0), (((0,), (1,)), ((), ())), preferred_element_type=F32
        )
        tiles_scr[pl.ds(EDGE_AT + row, n_req, stride=CHUNK), :] = held
    for row in range(NEXT_AT + edge_rows, CHUNK):
        tiles_scr[pl.ds(row, n_req, stride=CHUNK), :] = jnp.zeros((n_req, LANES), F32)
    copy.wait()
    rows_scr[...] = low_scr[...].astype(F32)
    for row in range(edge_rows):
        line = rows_scr[pl.ds(last - first + row, 1), :]
        for req in range(n_req):
            at = req // 2 * LANES
            tiles_scr[req * CHUNK + NEXT_AT + row : req * CHUNK + NEXT_AT + row + 1, :] = line[:, at : at + LANES]
    out_ref[...] = tiles_scr[...].astype(BF16).reshape(out_ref.shape)


def pack(length, read_slot, store, edges, x):
    n_req = read_slot.shape[0]
    channels = x.shape[1]
    whole = lambda *_: (0, 0)
    return pl.pallas_call(
        pack_kernel,
        grid_spec=pltpu.PrefetchScalarGridSpec(
            num_scalar_prefetch=1,
            grid=(1,),
            in_specs=[
                pl.BlockSpec((1, n_req), whole),
                pl.BlockSpec(store.shape, whole),
                pl.BlockSpec(edges.shape, whole),
                pl.BlockSpec(memory_space=pl.ANY),
            ],
            out_specs=pl.BlockSpec((n_req, CHUNK, LANES), lambda *_: (0, 0, 0)),
            scratch_shapes=[
                pltpu.VMEM((n_req * CHUNK, LANES), F32),
                pltpu.VMEM((2 * HALO, channels), BF16),
                pltpu.VMEM((2 * HALO, channels), F32),
                pltpu.SemaphoreType.DMA,
            ],
        ),
        out_shape=jax.ShapeDtypeStruct((n_req, CHUNK, LANES), BF16),
        compiler_params=pltpu.CompilerParams(vmem_limit_bytes=VMEM_LIMIT),
        name="pack",
    )(length, read_slot.reshape(1, n_req), store, edges, x)


def conv_block(prev, x_ref, weight_ref, bias_ref, select_hbm, mixed_ref, part_ref, send_ref, rows_scr, select_ref, sems):
    rows = x_ref.shape[0]
    groups = x_ref.shape[1] // LANES
    is_first = pl.program_id(0) == 0
    height = select_ref.shape[0] // FETCHES
    copies = [
        pltpu.make_async_copy(
            select_hbm.at[k * height : (k + 1) * height, :], select_ref.at[k * height : (k + 1) * height, :], sems.at[k]
        )
        for k in range(FETCHES)
    ]

    @pl.when(is_first)
    def _():
        for copy in copies:
            copy.start()

    def some_groups(step, _):
        for k in range(GROUPS_AT_ONCE):
            group = step * GROUPS_AT_ONCE + k
            at = pl.ds(pl.multiple_of(group * LANES, LANES), LANES)
            scr = rows_scr.at[k]
            scr[0:HALO, :] = prev(group)
            scr[HALO : HALO + rows, :] = x_ref[:, at].astype(F32)
            total = bias_ref[:, at] + weight_ref[CONV - 1 : CONV, at] * scr[HALO : HALO + rows, :]
            for tap in range(CONV - 1):
                first = HALO - (CONV - 1) + tap
                total = total + weight_ref[tap : tap + 1, at] * scr[first : first + rows, :]
            mixed_ref[:, at] = silu(total).astype(BF16)
        return 0

    lax.fori_loop(0, groups // GROUPS_AT_ONCE, some_groups, 0)

    @pl.when(is_first)
    def _():
        for copy in copies:
            copy.wait()

    part = lax.dot_general(
        select_ref[...], mixed_ref[...], (((1,), (1,)), ((), ())), preferred_element_type=F32
    ).T
    part_ref[...] = part
    send_ref[...] = part.astype(BF16)


def late_kernel(prev_ref, x_ref, weight_ref, bias_ref, select_ref, mixed_ref, part_ref, send_ref, *scr):
    prev = lambda group: prev_ref[:, pl.ds(pl.multiple_of(group * LANES, LANES), LANES)].astype(F32)
    conv_block(prev, x_ref, weight_ref, bias_ref, select_ref, mixed_ref, part_ref, send_ref, *scr)


def early_kernel(
    hit_ref, arrived_ref, after_ref, x_ref, weight_ref, bias_ref, select_ref, mixed_ref, part_ref, send_ref, start_ref,
    tiles_scr, edge_scr, *scr
):
    del after_ref
    hit = hit_ref[0] > 0
    n_req = arrived_ref.shape[0]
    pairs = n_req // 2
    tiles = arrived_ref[...].astype(F32).reshape(n_req * CHUNK, LANES)
    tiles_scr[...] = jnp.where(hit, tiles, 0.0)
    low = low_half()
    even = lambda row: tiles_scr[pl.ds(row, pairs, stride=2 * CHUNK), :]
    odd = lambda row: tiles_scr[pl.ds(CHUNK + row, pairs, stride=2 * CHUNK), :]
    for row in range(STATE // 2):
        a, b = even(row), odd(row)
        first, second = jnp.where(low, a, pltpu.roll(b, HALF, 1)), jnp.where(low, pltpu.roll(a, HALF, 1), b)
        for block in range(pairs // SUBLANES):
            at = slice(block * SUBLANES, (block + 1) * SUBLANES)
            start_ref[block, 2 * row] = first[at]
            start_ref[block, 2 * row + 1] = second[at]
    edge_scr[...] = jnp.zeros(edge_scr.shape, F32)
    for row in range(CONV - 1):
        edge_scr[pl.ds(HALO - (CONV - 1) + row, pairs, stride=HALO), :] = jnp.where(low, even(EDGE_AT + row), odd(EDGE_AT + row))
    prev = lambda group: edge_scr[pl.ds(pl.multiple_of(group * HALO, HALO), HALO), :]
    conv_block(prev, x_ref, weight_ref, bias_ref, select_ref, mixed_ref, part_ref, send_ref, *scr)


def conv_rows(x, weight, bias, select_t, first_row, n_rows, block, arrived=None, hit=None, after=None):
    channels = x.shape[1]
    wide = select_t.shape[0]
    first = first_row // block
    fixed = lambda *_: (0, 0)
    in_specs = [
        pl.BlockSpec((block, channels), lambda i, *_: (first + i, 0)),
        pl.BlockSpec((CONV, channels), fixed),
        pl.BlockSpec((1, channels), fixed),
        pl.BlockSpec(memory_space=pl.ANY),
    ]
    out_specs = [
        pl.BlockSpec((block, channels), lambda i, *_: (i, 0)),
        pl.BlockSpec((block, wide), lambda i, *_: (i, 0)),
        pl.BlockSpec((block, wide), lambda i, *_: (i, 0)),
    ]
    out_shape = [
        jax.ShapeDtypeStruct((n_rows, channels), BF16),
        jax.ShapeDtypeStruct((n_rows, wide), F32),
        jax.ShapeDtypeStruct((n_rows, wide), BF16),
    ]
    scratch = [
        pltpu.VMEM((GROUPS_AT_ONCE, HALO + block, LANES), F32),
        pltpu.VMEM(select_t.shape, BF16),
        pltpu.SemaphoreType.DMA((FETCHES,)),
    ]
    operands = [x, weight, bias, select_t]
    if arrived is None:
        kernel, name, scalars = late_kernel, "conv_late", []
        in_specs = [
            pl.BlockSpec((HALO, channels), lambda i, *_: ((first + i) * (block // HALO) - 1, 0))
        ] + in_specs
        operands = [x] + operands
    else:
        kernel, name, scalars = early_kernel, "conv_early", [hit]
        n_req = arrived.shape[0]
        in_specs = [
            pl.BlockSpec(arrived.shape, lambda *_: (0, 0, 0)),
            pl.BlockSpec(memory_space=pl.ANY),
        ] + in_specs
        operands = [arrived, after] + operands
        start_shape = (channels // WIDE, STATE, SUBLANES, LANES)
        out_specs.append(pl.BlockSpec(start_shape, lambda *_: (0, 0, 0, 0)))
        out_shape.append(jax.ShapeDtypeStruct(start_shape, F32))
        scratch = [
            pltpu.VMEM((n_req * CHUNK, LANES), F32),
            pltpu.VMEM((channels // LANES * HALO, LANES), F32),
        ] + scratch
    return pl.pallas_call(
        kernel,
        grid_spec=pltpu.PrefetchScalarGridSpec(
            num_scalar_prefetch=len(scalars),
            grid=(n_rows // block,),
            in_specs=in_specs,
            out_specs=out_specs,
            scratch_shapes=scratch,
        ),
        out_shape=out_shape,
        compiler_params=pltpu.CompilerParams(vmem_limit_bytes=VMEM_LIMIT),
        cost_estimate=pl.CostEstimate(
            flops=2 * n_rows * channels * wide,
            bytes_accessed=n_rows * channels * 24,
            transcendentals=2 * n_rows * channels,
        ),
        name=name,
    )(*scalars, *operands)


def scan_kernel(
    length_ref, *refs, n_parts, first_row, aliased, packed
):
    part_refs, refs = refs[:n_parts], refs[n_parts:]
    step_ref, bias_ref, decay_ref, skip_ref, mixed_ref, gate_ref, start_ref, *refs = refs
    if aliased:
        refs = refs[1:]
    out_ref, end_ref, norm_scr, wide_scr, value_scr, state_scr, rate_scr, back_scr, *lines = refs
    sizes, drives, scans = lines[0:2], lines[2:4], lines[4:6]
    channel_block, row_block = pl.program_id(0), pl.program_id(1)
    rows = mixed_ref.shape[0]
    pairs = rows // HALO
    at_rows = pl.ds(pl.multiple_of(row_block * rows, rows), rows)

    @pl.when(channel_block == 0)
    def _():
        projected = part_refs[0][...].astype(F32)
        for part_ref in part_refs[1:]:
            projected = projected + part_ref[...].astype(F32)
        low = projected[:, :RANK]
        scale = lax.rsqrt(jnp.mean(low * low, axis=-1, keepdims=True) + 1e-06)
        norm_scr[at_rows, :] = (low * scale).astype(BF16)
        picks = projected[:, RANK:]
        high = picks.astype(BF16)
        both = jnp.concatenate([high, (picks - high.astype(F32)).astype(BF16)], axis=1)
        shape = (4 * STATE, 2 * STATE * LANES)
        source = lax.broadcasted_iota(jnp.int32, shape, 0) % (2 * STATE)
        spread = (source == lax.broadcasted_iota(jnp.int32, shape, 1) // LANES).astype(BF16)
        wide_scr[at_rows, :] = jnp.dot(both, spread, preferred_element_type=F32)

    @pl.when(row_block == 0)
    def _():
        state_scr[...] = start_ref[0]
        rate = -jnp.exp(decay_ref[...]) * LOG2E
        for sub in range(SUBLANES):
            rate_scr[pl.ds(sub, STATE, stride=SUBLANES), :] = rate[:, sub * LANES : (sub + 1) * LANES]

    value_scr[...] = jnp.dot(norm_scr[at_rows, :], step_ref[...], preferred_element_type=F32)
    rates = [rate_scr[n * SUBLANES : (n + 1) * SUBLANES, :] for n in range(STATE)]
    row_in_tile = lax.broadcasted_iota(jnp.int32, (SUBLANES, LANES), 0)
    left = length_ref[0] - first_row - row_block * rows

    def steps_of(pair, tile):
        first = pl.multiple_of(pair * HALO, HALO)
        live = row_in_tile < left - first - tile * SUBLANES
        for sub in range(SUBLANES):
            at = slice(sub * LANES, (sub + 1) * LANES)
            value = value_scr[pl.ds(first + tile * SUBLANES, SUBLANES), at] + bias_ref[:, at]
            small = jnp.exp2(jnp.abs(value) * -LOG2E)
            soft = jnp.where(small < 4e-3, small - 0.5 * small * small, jnp.log(1.0 + small))
            size = jnp.where(live, jnp.maximum(value, 0.0) + soft, 0.0)
            mixed = mixed_ref[pl.ds(first, HALO), at].astype(F32)[tile * SUBLANES : (tile + 1) * SUBLANES]
            sizes[tile][pl.ds(sub, SUBLANES, stride=SUBLANES), :] = size
            drives[tile][pl.ds(sub, SUBLANES, stride=SUBLANES), :] = size * mixed

    def advance(state, pair, tile):
        state = list(state)
        first = pl.multiple_of(row_block * rows + pair * HALO + tile * SUBLANES, SUBLANES)
        picks = wide_scr.at[pl.ds(first, SUBLANES), :]
        for position in range(SUBLANES):
            here = slice(position * SUBLANES, (position + 1) * SUBLANES)
            size_row, drive_row = sizes[tile][here, :], drives[tile][here, :]
            sums = [None, None]
            for n in range(STATE):
                b = jnp.broadcast_to(picks[position : position + 1, n * LANES : (n + 1) * LANES], (SUBLANES, LANES))
                m = STATE + n
                c = jnp.broadcast_to(picks[position : position + 1, m * LANES : (m + 1) * LANES], (SUBLANES, LANES))
                state[n] = jnp.exp2(size_row * rates[n]) * state[n] + b * drive_row
                term = c * state[n]
                sums[n % 2] = term if sums[n % 2] is None else sums[n % 2] + term
            scans[tile][here, :] = sums[0] + sums[1]
        return tuple(state)

    def gate_of(pair):
        first = pl.multiple_of(pair * HALO, HALO)
        here = pl.ds(first, HALO)
        for sub in range(SUBLANES):
            at = slice(sub * LANES, (sub + 1) * LANES)
            scanned = jnp.concatenate(
                [scans[tile][pl.ds(sub, SUBLANES, stride=SUBLANES), :] for tile in range(2)], axis=0
            )
            value = scanned + skip_ref[:, at] * mixed_ref[here, at].astype(F32)
            value = value * silu(gate_ref[here, at].astype(F32))
            live = jnp.concatenate([row_in_tile, row_in_tile + SUBLANES], axis=0) < left - first
            out_ref[here, at] = jnp.where(live, value, 0.0).astype(BF16)

    def one_pair(pair, state):
        gate_of(jnp.maximum(pair - 1, 0))
        steps_of(pair, 1)
        state = advance(state, pair, 0)
        steps_of(jnp.minimum(pair + 1, pairs - 1), 0)
        return advance(state, pair, 1)

    steps_of(0, 0)
    state = lax.fori_loop(0, pairs, one_pair, tuple(state_scr[n] for n in range(STATE)))
    gate_of(pairs - 1)
    for n in range(STATE):
        state_scr[n] = state[n]

    @pl.when(row_block == pl.num_programs(1) - 1)
    def _():
        if packed:
            low = low_half()
            for row in range(STATE // 2):
                a, b = state_scr[2 * row], state_scr[2 * row + 1]
                even = jnp.where(low, a, pltpu.roll(b, HALF, 1))
                odd = jnp.where(low, pltpu.roll(a, HALF, 1), b)
                back_scr[pl.ds(row, SUBLANES, stride=2 * SUBLANES), :] = even
                back_scr[pl.ds(SUBLANES + row, SUBLANES, stride=2 * SUBLANES), :] = odd
            end_ref[...] = back_scr[...].astype(BF16).reshape(end_ref.shape)
        else:
            end_ref[0] = state_scr[...]


def scan_rows(length, parts, step_weight, step_bias, decay_log, skip_gain, mixed, gate, start, out, first_row, block):
    n_rows, channels = mixed.shape
    blocks = channels // WIDE
    first = first_row // block
    wide = parts[0].shape[1]
    packed = first_row > 0
    by_channel = lambda c, i, *_: (0, c)
    part_spec = pl.BlockSpec((block, wide), lambda c, i, *_: (jnp.where(c == 0, i, 0), 0))
    state_shape = (1, STATE, SUBLANES, LANES)
    state_spec = pl.BlockSpec(state_shape, lambda c, i, *_: (c, 0, 0, 0))
    operands = [length, *parts, step_weight, step_bias, decay_log, skip_gain, mixed, gate, start]
    in_specs = [part_spec] * len(parts) + [
        pl.BlockSpec((RANK, WIDE), by_channel),
        pl.BlockSpec((1, WIDE), by_channel),
        pl.BlockSpec((STATE, WIDE), by_channel),
        pl.BlockSpec((1, WIDE), by_channel),
        pl.BlockSpec((block, WIDE), lambda c, i, *_: (i, c)),
        pl.BlockSpec((block, WIDE), lambda c, i, *_: (first + i, c)),
        state_spec,
    ]
    aliases = {}
    if out is not None:
        aliases = {len(operands): 0}
        operands.append(out)
        in_specs.append(pl.BlockSpec(memory_space=pl.ANY))
    if packed:
        per_block = WIDE // HALF
        end_spec = pl.BlockSpec((per_block, SUBLANES, LANES), lambda c, i, *_: (c, 0, 0))
        end_shape = jax.ShapeDtypeStruct((blocks * per_block, SUBLANES, LANES), BF16)
    else:
        end_spec = state_spec
        end_shape = jax.ShapeDtypeStruct((blocks, *state_shape[1:]), F32)
    return pl.pallas_call(
        functools.partial(
            scan_kernel, n_parts=len(parts), first_row=first_row, aliased=out is not None, packed=packed
        ),
        grid_spec=pltpu.PrefetchScalarGridSpec(
            num_scalar_prefetch=1,
            grid=(blocks, n_rows // block),
            in_specs=in_specs,
            out_specs=[pl.BlockSpec((block, WIDE), lambda c, i, *_: (first + i, c)), end_spec],
            scratch_shapes=[
                pltpu.VMEM((n_rows, RANK), BF16),
                pltpu.VMEM((n_rows, 2 * STATE * LANES), F32),
                pltpu.VMEM((block, WIDE), F32),
                pltpu.VMEM((STATE, SUBLANES, LANES), F32),
                pltpu.VMEM((STATE * SUBLANES, LANES), F32),
                pltpu.VMEM((WIDE // HALF * SUBLANES, LANES), F32),
            ]
            + [pltpu.VMEM((SUBLANES * SUBLANES, LANES), F32)] * 6,
        ),
        out_shape=[jax.ShapeDtypeStruct(gate.shape, BF16), end_shape],
        input_output_aliases=aliases,
        compiler_params=pltpu.CompilerParams(vmem_limit_bytes=VMEM_LIMIT),
        cost_estimate=pl.CostEstimate(
            flops=2 * n_rows * channels * RANK + 100 * n_rows * channels * STATE,
            bytes_accessed=n_rows * channels * 8,
            transcendentals=n_rows * channels * STATE,
        ),
        name="scan_rows",
    )(*operands)


def save_kernel(slot_ref, half_ref, tiles_ref, store_ref, out_ref, tiles_scr, *, n_rows, first_row, halves):
    n_req, chunk, _ = tiles_ref.shape
    slots = store_ref.shape[1]
    saves = slot_ref[...] == lax.broadcasted_iota(jnp.int32, (n_req, slots), 1)
    saved = jnp.max(saves.astype(F32), axis=0, keepdims=True) > 0.0
    saves = saves.astype(BF16)
    tiles = tiles_ref[...].astype(F32).reshape(n_req * chunk, LANES)
    if halves:
        tiles = jnp.where(half_ref[0] > 0, pltpu.roll(tiles, HALF, 1), tiles)
    tiles_scr[...] = tiles
    height = HALF if halves else LANES
    for row in range(n_rows):
        new = tiles_scr[pl.ds(first_row + row, n_req, stride=chunk), :].astype(BF16)
        new = lax.dot_general(new, saves, (((0,), (0,)), ((), ())), preferred_element_type=F32)[:height]
        at = slice(row * height, (row + 1) * height)
        out_ref[at, :] = jnp.where(saved, new, store_ref[at, :].astype(F32)).astype(out_ref.dtype)


def save(save_slot, half, tiles, store, n_rows, first_row, halves):
    n_req, chunk, _ = tiles.shape
    whole = lambda *_: (0, 0)
    return pl.pallas_call(
        functools.partial(save_kernel, n_rows=n_rows, first_row=first_row, halves=halves),
        grid=(1,),
        in_specs=[
            pl.BlockSpec((n_req, 1), whole),
            pl.BlockSpec(memory_space=pltpu.SMEM),
            pl.BlockSpec(tiles.shape, lambda *_: (0, 0, 0)),
            pl.BlockSpec(store.shape, whole),
        ],
        out_specs=pl.BlockSpec(store.shape, whole),
        out_shape=jax.ShapeDtypeStruct(store.shape, store.dtype),
        scratch_shapes=[pltpu.VMEM((n_req * chunk, LANES), F32)],
        compiler_params=pltpu.CompilerParams(vmem_limit_bytes=SMALL_LIMIT),
        name="save",
    )(save_slot.reshape(n_req, 1), half, tiles, store)


def from_others(part, sent, n_tp):
    return [part] + [
        lax.ppermute(sent, "tp", [(d, (d + s) % n_tp) for d in range(n_tp)]) for s in range(1, n_tp)
    ]


def local(
    n_tp,
    conv_input,
    gate_input,
    conv_weight,
    conv_bias,
    select_weight,
    step_weight,
    step_bias,
    decay_log,
    skip_gain,
    store_state,
    store_edge,
    read_slot,
    save_slot,
    cache_hit,
    suffix_length,
):
    local_rows, channels = conv_input.shape
    slots, _, _, stripe = store_state.shape
    edge_rows = CONV - 1
    store = store_state.transpose(1, 2, 3, 0).reshape(STATE * stripe, slots)
    edges = store_edge.transpose(1, 2, 3, 0).reshape(edge_rows * stripe, slots)
    outgoing = pack(suffix_length, read_slot, store, edges, conv_input)
    arrived = lax.all_to_all(outgoing, "req", split_axis=0, concat_axis=0, tiled=True)

    select_t = select_weight.T
    conv_bias = conv_bias.reshape(1, channels)
    step_bias = step_bias.reshape(1, channels)
    skip_gain = skip_gain.reshape(1, channels)
    block = 128
    late_mixed, late_part, late_sent = conv_rows(
        conv_input, conv_weight, conv_bias, select_t, block, local_rows - block, block
    )
    late_parts = from_others(late_part, late_sent, n_tp)
    early_mixed, early_part, early_sent, start = conv_rows(
        conv_input, conv_weight, conv_bias, select_t, 0, block, block, arrived, cache_hit, late_part
    )
    early_parts = from_others(early_part, early_sent, n_tp)

    scan = functools.partial(scan_rows, block=block)
    shared = (step_weight, step_bias, decay_log, skip_gain)
    out, state = scan(suffix_length, early_parts, *shared, early_mixed, gate_input, start, None, 0)
    out, back = scan(suffix_length, late_parts, *shared, late_mixed, gate_input, state, out, block)

    half = (lax.axis_index("req") % 2).astype(jnp.int32).reshape(1)
    arrived, back = lax.optimization_barrier((arrived, back))
    new_edges = save(save_slot, half, arrived, edges, edge_rows, NEXT_AT, True)
    new_edges, back = lax.optimization_barrier((new_edges, back))
    back = lax.all_to_all(back, "req", split_axis=0, concat_axis=0, tiled=True)
    new_store = save(save_slot, half, back, store, STATE // 2, 0, False)
    new_state = new_store.reshape(1, STATE, stripe, slots).transpose(3, 0, 1, 2)
    new_edge_store = new_edges.reshape(1, edge_rows, stripe, slots).transpose(3, 0, 1, 2)
    return (out, new_state, new_edge_store)


def solution(mesh):
    placed = (
        P("req", "tp"),
        P("req", "tp"),
        P(None, "tp"),
        P("tp"),
        P("tp", None),
        P(None, "tp"),
        P("tp"),
        P(None, "tp"),
        P("tp"),
        P(None, "req", None, "tp"),
        P(None, "req", None, "tp"),
        P(),
        P(),
        P("req"),
        P("req"),
    )
    return jax.shard_map(
        functools.partial(local, mesh.shape["tp"]),
        mesh=mesh,
        in_specs=placed,
        out_specs=(P("req", "tp"), P(None, "req", None, "tp"), P(None, "req", None, "tp")),
        check_vma=False,
    )
```

time: 149 us -> 133 us (0.89)
  waiting for transfers between devices: 36.7 us -> 17.3 us
  blocking collectives: 0 us -> 18.9 us
  local copies, waits for them, and re-layouts: 11.8 us -> 2.35 us
  Pallas kernels: 64.2 us -> 71 us
  matrix products: 4.62 us -> 0 us
  starting transfers between devices: 25.4 us -> 20.9 us
  other arithmetic: 3.29 us -> 0 us
    all_to_all x0 -> x1, blocking collectives: none -> 18.9 us  [local(): back = lax.all_to_all(back, 'req', split_axis=0, concat_axis=0, tiled=True)]
    all_to_all x1 -> x0, waiting for transfers between devices: 9.61 us -> none  [local(): back = lax.all_to_all(back, 'req', split_axis=0, concat_axis=0, tiled=True)]
    all_to_all x1, waiting for transfers between devices: 11.4 us -> 3.69 us  [local(): lax.all_to_all(outgoing, 'req', split_axis=0, concat_axis=0, tiled=True)]
    pallas_call x4 -> x7, Pallas kernels: 64.2 us -> 71 us  [the longest x2 52.8 us: scan_rows(): pl.pallas_call(functools.partial(scan_kernel, n_parts=len(parts), first_r...]
    unnamed x40 -> x24, local copies, waits for them, and re-layouts: 8.33 us -> 2.25 us
    dot_general x4 -> x0, matrix products: 4.62 us -> none  [the longest x1 1.63 us: local(): lax.dot_general(arrived[:, n_state + n_edge:], saves, contract_requests,...]
    all_to_all x1 -> x0, starting transfers between devices: 4.52 us -> none  [local(): back = lax.all_to_all(back, 'req', split_axis=0, concat_axis=0, tiled=True)]
    ppermute x6, waiting for transfers between devices: 15.7 us -> 13.6 us  [from_others(): lax.ppermute(sent, 'tp', [(d, (d + s) % n_tp) for d in range(n_tp)])]
  transfers between devices with their start and end apart: 8 -> 7, of which waited for: 4 -> 2; matrix products, arithmetic and copies ran while one was open for 1% -> 0% of each run, Pallas kernels for 15% -> 17%
where the time goes in v2:
time: 133 us; the launch traced here: 132 us
  Pallas kernels  71 us (53%)
  starting transfers between devices  20.9 us (16%)
  blocking collectives  18.9 us (14%)
  waiting for transfers between devices  17.3 us (13%)
  local copies, waits for them, and re-layouts  2.35 us (2%)
  between operations  2.06 us (2%)
    pallas_call x2, Pallas kernels, scan_rows(): pl.pallas_call(functools.partial(scan_kernel, n_parts=len(parts), first_r...  52.8 us
    all_to_all x1, blocking collectives, local(): back = lax.all_to_all(back, 'req', split_axis=0, concat_axis=0, tiled=True)  18.9 us
    ppermute x6, waiting for transfers between devices, from_others(): lax.ppermute(sent, 'tp', [(d, (d + s) % n_tp) for d in range(n_tp)])  13.6 us
    pallas_call x2, Pallas kernels, conv_rows(): pl.pallas_call(kernel, grid_spec=pltpu.PrefetchScalarGridSpec(num_scalar_...  13.3 us
    all_to_all x1, starting transfers between devices, local(): lax.all_to_all(outgoing, 'req', split_axis=0, concat_axis=0, tiled=True)  13 us
    ppermute x6, starting transfers between devices, from_others(): lax.ppermute(sent, 'tp', [(d, (d + s) % n_tp) for d in range(n_tp)])  7.95 us
    all_to_all x1, waiting for transfers between devices, local(): lax.all_to_all(outgoing, 'req', split_axis=0, concat_axis=0, tiled=True)  3.69 us
    pallas_call x1, Pallas kernels, pack(): pl.pallas_call(pack_kernel, grid_spec=pltpu.PrefetchScalarGridSpec(num_sc...  2.86 us
  transfers between devices with their start and end apart: 7, of which 2 were waited for; matrix products, arithmetic and copies ran while one was open for 0% of the time, Pallas kernels for 17%

profile of v2, /device:TPU:1, one launch (start us, length us, event | category | flops | bytes accessed | tf_op | source)
XLA Modules:
  0.0 132.5 jit_solution(13541634369301692293)
XLA Ops:
  1.3 2.9 %pack.1 = bf16[64,16,128]{2,1,0:T(8,128)(2,1)} custom-call(s32[1]{0:T(128)S(6)} %copy.23.length_ref, s32[1,64]{1,0:T(1,128)} %bitcast.29, f32[1024,128]{1,0:T(8,128)} %bitcast.19, bf16[192,128]{1,0:T(8,128)(2,1)} %bitcast.21, bf16[512,4096]{1,0:T(8,128)(2,1)} %x_ref.5), custom_call_target="tpu_custom_call" | custom-call | tf_op jit(solution)/shard_map/pack/pallas_call | solution.py:76
  4.1 13.0 %all-to-all-start = ((bf16[64,16,128]{2,1,0:T(8,128)(2,1)}), bf16[64,16,128]{2,1,0:T(8,128)(2,1)S(1)}, u32[]{:S(2)}, u32[]{:S(2)}) async-start(bf16[64,16,128]{2,1,0:T(8,128)(2,1)} %pack.1), calls=%async_computation | async-start | bytes 524288 | tf_op jit(solution)/shard_map/all_to_all | solution.py:491
  17.8 8.8 %conv_late.1 = (bf16[384,4096]{1,0:T(8,128)(2,1)}, f32[384,288]{1,0:T(8,128)}, bf16[384,288]{1,0:T(8,128)(2,1)}) custom-call(bf16[512,4096]{1,0:T(8,128)(2,1)} %x_ref.5, bf16[512,4096]{1,0:T(8,128)(2,1)} %x_ref.5, f32[4,4096]{1,0:T(4,128)} %weight_ref.3, f32[1,4096]{1,0:T(1,128)} %bitcast.26, bf16[288,4096]{1,0:T(8,128)(2,1)} %bitcast.23), custom_call_target="tpu_custom_call" | custom-call | flops 905969664 | bytes 37748736 | tf_op jit(solution)/shard_map/conv_late/pallas_call | solution.py:226
  26.6 0.0 copy-start.5
  26.6 0.0 copy-start.4
  26.6 3.7 %all-to-all-done.arrived_ref.tiles_ref = bf16[64,16,128]{2,1,0:T(8,128)(2,1)S(1)} async-done(((bf16[64,16,128]{2,1,0:T(8,128)(2,1)}), bf16[64,16,128]{2,1,0:T(8,128)(2,1)S(1)}, u32[]{:S(2)}, u32[]{:S(2)}) %all-to-all-start) | async-done | bytes 262176 | tf_op jit(solution)/shard_map/all_to_all | solution.py:491
  30.3 0.0 copy-start
  30.3 0.7 copy-done
  31.0 4.5 %conv_early.1 = (bf16[128,4096]{1,0:T(8,128)(2,1)}, f32[128,288]{1,0:T(8,128)}, bf16[128,288]{1,0:T(8,128)(2,1)}, f32[4,16,8,128]{3,2,1,0:T(8,128)}) custom-call(s32[1]{0:T(128)S(6)} %copy.22.hit_ref, bf16[64,16,128]{2,1,0:T(8,128)(2,1)} %copy-done, f32[384,288]{1,0:T(8,128)} %get-tuple-element.18.after_ref.refs_0_, bf16[512,4096]{1,0:T(8,128)(2,1)} %x_ref.5, ...), custom_call_target="tpu_custom_call" | custom-call | flops 301989888 | bytes 12582912 | tf_op jit(solution)/shard_map/conv_early/pallas_call | solution.py:226
  35.5 1.4 %collective-permute-start.3 = (bf16[128,288]{1,0:T(8,128)(2,1)}, bf16[128,288]{1,0:T(8,128)(2,1)S(1)}, u32[]{:S(2)}, u32[]{:S(2)}) collective-permute-start(bf16[128,288]{1,0:T(8,128)(2,1)} %get-tuple-element.22), channel_id=1, source_target_pairs={{0,1},{1,2},{2,3},{3,0},{4,5},{5,6},{6,7},{7,4},{8,9},{9,10},{10,1... | collective-permute-start | bytes 221192 | tf_op jit(solution)/shard_map/ppermute | solution.py:463
  36.9 0.0 copy-done.5
  36.9 1.3 collective-permute-start
  38.2 1.4 %collective-permute-start.1 = (bf16[384,288]{1,0:T(8,128)(2,1)S(1)}, bf16[384,288]{1,0:T(8,128)(2,1)S(1)}, u32[]{:S(2)}, u32[]{:S(2)}) collective-permute-start(bf16[384,288]{1,0:T(8,128)(2,1)S(1)} %copy-done.5), channel_id=1, source_target_pairs={{0,2},{1,3},{2,0},{3,1},{4,6},{5,7},{6,4},{7,5},{8,10},{9,11},{10,... | collective-permute-start | bytes 663560 | tf_op jit(solution)/shard_map/ppermute | solution.py:463
  39.6 2.0 %collective-permute-start.2 = (bf16[384,288]{1,0:T(8,128)(2,1)S(1)}, bf16[384,288]{1,0:T(8,128)(2,1)S(1)}, u32[]{:S(2)}, u32[]{:S(2)}) collective-permute-start(bf16[384,288]{1,0:T(8,128)(2,1)S(1)} %copy-done.5), channel_id=1, source_target_pairs={{0,3},{1,0},{2,1},{3,2},{4,7},{5,4},{6,5},{7,6},{8,11},{9,8},{10,9... | collective-permute-start | bytes 663560 | tf_op jit(solution)/shard_map/ppermute | solution.py:463
  41.6 0.3 collective-permute-start.4
  41.9 0.0 collective-permute-done.3.refs_1_
  41.9 0.0 copy-start.9
  41.9 1.5 %collective-permute-start.5 = (bf16[128,288]{1,0:T(8,128)(2,1)}, bf16[128,288]{1,0:T(8,128)(2,1)S(1)}, u32[]{:S(2)}, u32[]{:S(2)}) collective-permute-start(bf16[128,288]{1,0:T(8,128)(2,1)} %get-tuple-element.22), channel_id=1, source_target_pairs={{0,3},{1,0},{2,1},{3,2},{4,7},{5,4},{6,5},{7,6},{8,11},{9,8},{10,9... | collective-permute-start | bytes 221192 | tf_op jit(solution)/shard_map/ppermute | solution.py:463
  43.5 0.0 copy-done.4
  43.5 0.1 copy.20.slot_ref
  43.6 13.5 %collective-permute-done.4.refs_2_ = bf16[128,288]{1,0:T(8,128)(2,1)S(1)} collective-permute-done((bf16[128,288]{1,0:T(8,128)(2,1)}, bf16[128,288]{1,0:T(8,128)(2,1)S(1)}, u32[]{:S(2)}, u32[]{:S(2)}) %collective-permute-start.4) | collective-permute-done | bytes 73760 | tf_op jit(solution)/shard_map/ppermute | solution.py:463
  57.1 0.0 copy-start.10
  57.1 0.0 collective-permute-done.5.refs_3_
  57.1 0.0 copy-start.11
  57.1 0.0 copy-done.9
  57.1 0.6 copy-done.10
  57.8 0.0 copy-done.11
  57.8 14.0 %scan_rows.2 = (bf16[512,4096]{1,0:T(8,128)(2,1)}, f32[4,16,8,128]{3,2,1,0:T(8,128)}) custom-call(s32[1]{0:T(128)S(6)} %copy.23.length_ref, f32[128,288]{1,0:T(8,128)} %get-tuple-element.21.refs_0_, bf16[128,288]{1,0:T(8,128)(2,1)} %copy-done.9, bf16[128,288]{1,0:T(8,128)(2,1)} %copy-done.10, bf16[128,288]{1,0:T(8,128)(2,1)} %copy-done.11, ...), custom_call_target="tpu_custom_call" | custom-call | flops 1107296256 | bytes 4194304 | tf_op jit(solution)/shard_map/scan_rows/pallas_call | solution.py:392
  71.8 0.0 collective-permute-done.refs_1_
  71.8 0.0 copy-start.6
  71.8 0.0 collective-permute-done.1.refs_2_
  71.8 0.0 copy-start.7
  71.8 0.0 collective-permute-done.2.refs_3_
  71.9 0.0 copy-start.8
  71.9 0.7 copy-done.6
  72.5 0.1 copy-done.7
  72.6 0.1 copy-done.8
  72.7 0.0 copy-start.1
  72.7 0.0 copy-start.3
  72.7 0.0 copy-start.2
  72.7 38.8 %scan_rows.3 = (bf16[512,4096]{1,0:T(8,128)(2,1)}, bf16[64,8,128]{2,1,0:T(8,128)(2,1)}) custom-call(s32[1]{0:T(128)S(6)} %copy.23.length_ref, f32[384,288]{1,0:T(8,128)} %get-tuple-element.18.after_ref.refs_0_, bf16[384,288]{1,0:T(8,128)(2,1)} %copy-done.6, bf16[384,288]{1,0:T(8,128)(2,1)} %copy-done.7, ...), custom_call_target="tpu_custom_call", output_to_operand_aliasing={{0}: (12, {})} | custom-call | flops 3321888768 | bytes 12582912 | tf_op jit(solution)/shard_map/scan_rows/pallas_call | solution.py:392
  111.6 0.0 copy-done.1
  111.6 0.0 copy-done.3
  111.6 0.9 save.2
  112.5 18.9 %all_to_all.10.tiles_ref = bf16[64,8,128]{2,1,0:T(8,128)(2,1)S(1)} all-to-all(bf16[64,8,128]{2,1,0:T(8,128)(2,1)} %get-tuple-element.31), channel_id=1, replica_groups=mesh['req'=64,'tp'=4] {'req'}, dimensions={0} | all-to-all | bytes 262144 | tf_op jit(solution)/shard_map/all_to_all | solution.py:516
  131.4 0.0 copy-done.2
  131.4 1.1 save.3
Async XLA Ops:
  4.1 26.2 %all-to-all-start = ((bf16[64,16,128]{2,1,0:T(8,128)(2,1)}), bf16[64,16,128]{2,1,0:T(8,128)(2,1)S(1)}, u32[]{:S(2)}, u32[]{:S(2)}) async-start(bf16[64,16,128]{2,1,0:T(8,128)(2,1)} %pack.1), calls=%async_computation | async-start | bytes 524288 | tf_op jit(solution)/shard_map/all_to_all | solution.py:491
  26.6 10.3 %copy-start.5 = (bf16[384,288]{1,0:T(8,128)(2,1)S(1)}, bf16[384,288]{1,0:T(8,128)(2,1)}, u32[]{:S(2)}) copy-start(bf16[384,288]{1,0:T(8,128)(2,1)} %get-tuple-element.19) | copy-start | bytes 663556
  26.6 16.9 %copy-start.4 = (s32[64]{0:T(128)S(1)}, s32[64]{0:T(128)}, u32[]{:S(2)}) copy-start(s32[64]{0:T(128)} %param.27) | copy-start | bytes 772
  30.3 0.7 copy-start
  35.5 6.4 %collective-permute-start.3 = (bf16[128,288]{1,0:T(8,128)(2,1)}, bf16[128,288]{1,0:T(8,128)(2,1)S(1)}, u32[]{:S(2)}, u32[]{:S(2)}) collective-permute-start(bf16[128,288]{1,0:T(8,128)(2,1)} %get-tuple-element.22), channel_id=1, source_target_pairs={{0,1},{1,2},{2,3},{3,0},{4,5},{5,6},{6,7},{7,4},{8,9},{9,10},{10,1... | collective-permute-start | bytes 221192 | tf_op jit(solution)/shard_map/ppermute | solution.py:463
  36.9 34.9 %collective-permute-start = (bf16[384,288]{1,0:T(8,128)(2,1)S(1)}, bf16[384,288]{1,0:T(8,128)(2,1)S(1)}, u32[]{:S(2)}, u32[]{:S(2)}) collective-permute-start(bf16[384,288]{1,0:T(8,128)(2,1)S(1)} %copy-done.5), channel_id=1, source_target_pairs={{0,1},{1,2},{2,3},{3,0},{4,5},{5,6},{6,7},{7,4},{8,9},{9,10},{10,1... | collective-permute-start | bytes 663560 | tf_op jit(solution)/shard_map/ppermute | solution.py:463
  38.2 33.6 %collective-permute-start.1 = (bf16[384,288]{1,0:T(8,128)(2,1)S(1)}, bf16[384,288]{1,0:T(8,128)(2,1)S(1)}, u32[]{:S(2)}, u32[]{:S(2)}) collective-permute-start(bf16[384,288]{1,0:T(8,128)(2,1)S(1)} %copy-done.5), channel_id=1, source_target_pairs={{0,2},{1,3},{2,0},{3,1},{4,6},{5,7},{6,4},{7,5},{8,10},{9,11},{10,... | collective-permute-start | bytes 663560 | tf_op jit(solution)/shard_map/ppermute | solution.py:463
  39.6 32.2 %collective-permute-start.2 = (bf16[384,288]{1,0:T(8,128)(2,1)S(1)}, bf16[384,288]{1,0:T(8,128)(2,1)S(1)}, u32[]{:S(2)}, u32[]{:S(2)}) collective-permute-start(bf16[384,288]{1,0:T(8,128)(2,1)S(1)} %copy-done.5), channel_id=1, source_target_pairs={{0,3},{1,0},{2,1},{3,2},{4,7},{5,4},{6,5},{7,6},{8,11},{9,8},{10,9... | collective-permute-start | bytes 663560 | tf_op jit(solution)/shard_map/ppermute | solution.py:463
  41.6 15.5 %collective-permute-start.4 = (bf16[128,288]{1,0:T(8,128)(2,1)}, bf16[128,288]{1,0:T(8,128)(2,1)S(1)}, u32[]{:S(2)}, u32[]{:S(2)}) collective-permute-start(bf16[128,288]{1,0:T(8,128)(2,1)} %get-tuple-element.22), channel_id=1, source_target_pairs={{0,2},{1,3},{2,0},{3,1},{4,6},{5,7},{6,4},{7,5},{8,10},{9,11},{10,... | collective-permute-start | bytes 221192 | tf_op jit(solution)/shard_map/ppermute | solution.py:463
  41.9 15.2 %copy-start.9 = (bf16[128,288]{1,0:T(8,128)(2,1)}, bf16[128,288]{1,0:T(8,128)(2,1)S(1)}, u32[]{:S(2)}) copy-start(bf16[128,288]{1,0:T(8,128)(2,1)S(1)} %collective-permute-done.3.refs_1_) | copy-start | bytes 221188
  41.9 15.2 %collective-permute-start.5 = (bf16[128,288]{1,0:T(8,128)(2,1)}, bf16[128,288]{1,0:T(8,128)(2,1)S(1)}, u32[]{:S(2)}, u32[]{:S(2)}) collective-permute-start(bf16[128,288]{1,0:T(8,128)(2,1)} %get-tuple-element.22), channel_id=1, source_target_pairs={{0,3},{1,0},{2,1},{3,2},{4,7},{5,4},{6,5},{7,6},{8,11},{9,8},{10,9... | collective-permute-start | bytes 221192 | tf_op jit(solution)/shard_map/ppermute | solution.py:463
  57.1 0.6 copy-start.10
  57.1 0.7 copy-start.11
  71.8 0.7 copy-start.6
  71.8 0.8 copy-start.7
  71.9 0.9 copy-start.8
  72.7 38.8 %copy-start.1 = (bf16[64,16,128]{2,1,0:T(8,128)(2,1)S(1)}, bf16[64,16,128]{2,1,0:T(8,128)(2,1)}, u32[]{:S(2)}) copy-start(bf16[64,16,128]{2,1,0:T(8,128)(2,1)} %copy-done) | copy-start | bytes 786436
  72.7 38.8 %copy-start.3 = (bf16[128,1,3,64]{0,3,2,1:T(8,128)(2,1)S(1)}, bf16[128,1,3,64]{0,3,2,1:T(8,128)(2,1)}, u32[]{:S(2)}) copy-start(bf16[128,1,3,64]{0,3,2,1:T(8,128)(2,1)} %param.25) | copy-start | bytes 147460
  72.7 58.7 %copy-start.2 = (f32[128,1,16,64]{0,3,2,1:T(8,128)S(1)}, f32[128,1,16,64]{0,3,2,1:T(8,128)}, u32[]{:S(2)}) copy-start(f32[128,1,16,64]{0,3,2,1:T(8,128)} %param.24) | copy-start | bytes 1572868

commit v3 on v2

--- a/solution.py
+++ b/solution.py
@@ -23,6 +23,7 @@
 CHUNK = 16
 FETCHES = 6
 GROUPS_AT_ONCE = 4
+PAIRS = 2
 VMEM_LIMIT = 60 * 1024 * 1024
 SMALL_LIMIT = 24 * 1024 * 1024
 
@@ -98,7 +99,7 @@
     )(length, read_slot.reshape(1, n_req), store, edges, x)
 
 
-def conv_block(prev, x_ref, weight_ref, bias_ref, select_hbm, mixed_ref, part_ref, send_ref, rows_scr, select_ref, sems):
+def conv_block(prev, x_ref, weight_ref, bias_ref, select_hbm, mixed_ref, part_ref, send, rows_scr, select_ref, sems):
     rows = x_ref.shape[0]
     groups = x_ref.shape[1] // LANES
     is_first = pl.program_id(0) == 0
@@ -140,19 +141,32 @@
         select_ref[...], mixed_ref[...], (((1,), (1,)), ((), ())), preferred_element_type=F32
     ).T
     part_ref[...] = part
-    send_ref[...] = part.astype(BF16)
-
-
-def late_kernel(prev_ref, x_ref, weight_ref, bias_ref, select_ref, mixed_ref, part_ref, send_ref, *scr):
+    send(part.astype(BF16))
+
+
+def late_kernel(
+    prev_ref, x_ref, weight_ref, bias_ref, select_ref, mixed_ref, part_ref, upper_ref, lower_ref, *scr, per_half
+):
     prev = lambda group: prev_ref[:, pl.ds(pl.multiple_of(group * LANES, LANES), LANES)].astype(F32)
-    conv_block(prev, x_ref, weight_ref, bias_ref, select_ref, mixed_ref, part_ref, send_ref, *scr)
+    block = 1 + pl.program_id(0)
+
+    def send(part):
+        @pl.when(block < per_half)
+        def _():
+            upper_ref[...] = part
+
+        @pl.when(block >= per_half)
+        def _():
+            lower_ref[...] = part
+
+    conv_block(prev, x_ref, weight_ref, bias_ref, select_ref, mixed_ref, part_ref, send, *scr)
 
 
 def early_kernel(
-    hit_ref, arrived_ref, after_ref, x_ref, weight_ref, bias_ref, select_ref, mixed_ref, part_ref, send_ref, start_ref,
-    tiles_scr, edge_scr, *scr
+    hit_ref, arrived_ref, x_ref, weight_ref, bias_ref, select_ref, late_mixed, late_part, late_upper,
+    mixed_ref, part_ref, upper_ref, start_ref, tiles_scr, edge_scr, *scr
 ):
-    del after_ref
+    del late_mixed, late_part, late_upper
     hit = hit_ref[0] > 0
     n_req = arrived_ref.shape[0]
     pairs = n_req // 2
@@ -172,29 +186,38 @@
     for row in range(CONV - 1):
         edge_scr[pl.ds(HALO - (CONV - 1) + row, pairs, stride=HALO), :] = jnp.where(low, even(EDGE_AT + row), odd(EDGE_AT + row))
     prev = lambda group: edge_scr[pl.ds(pl.multiple_of(group * HALO, HALO), HALO), :]
-    conv_block(prev, x_ref, weight_ref, bias_ref, select_ref, mixed_ref, part_ref, send_ref, *scr)
-
-
-def conv_rows(x, weight, bias, select_t, first_row, n_rows, block, arrived=None, hit=None, after=None):
-    channels = x.shape[1]
+
+    def send(part):
+        upper_ref[...] = part
+
+    conv_block(prev, x_ref, weight_ref, bias_ref, select_ref, mixed_ref, part_ref, send, *scr)
+
+
+def conv_rows(x, weight, bias, select_t, block, arrived=None, hit=None, late=None):
+    rows, channels = x.shape
     wide = select_t.shape[0]
-    first = first_row // block
+    first = 1 if late is None else 0
+    steps = rows // block - 1 if late is None else 1
+    per_half = rows // block // 2
     fixed = lambda *_: (0, 0)
+    at = lambda i, *_: (first + i, 0)
     in_specs = [
-        pl.BlockSpec((block, channels), lambda i, *_: (first + i, 0)),
+        pl.BlockSpec((block, channels), at),
         pl.BlockSpec((CONV, channels), fixed),
         pl.BlockSpec((1, channels), fixed),
         pl.BlockSpec(memory_space=pl.ANY),
     ]
+    upper_at = lambda i, *_: (jnp.minimum(first + i, per_half - 1), 0)
+    lower_at = lambda i, *_: (jnp.maximum(first + i - per_half, 0), 0)
     out_specs = [
-        pl.BlockSpec((block, channels), lambda i, *_: (i, 0)),
-        pl.BlockSpec((block, wide), lambda i, *_: (i, 0)),
-        pl.BlockSpec((block, wide), lambda i, *_: (i, 0)),
+        pl.BlockSpec((block, channels), at),
+        pl.BlockSpec((block, wide), at),
+        pl.BlockSpec((block, wide), upper_at),
     ]
     out_shape = [
-        jax.ShapeDtypeStruct((n_rows, channels), BF16),
-        jax.ShapeDtypeStruct((n_rows, wide), F32),
-        jax.ShapeDtypeStruct((n_rows, wide), BF16),
+        jax.ShapeDtypeStruct((rows, channels), BF16),
+        jax.ShapeDtypeStruct((rows, wide), F32),
+        jax.ShapeDtypeStruct((rows // 2, wide), BF16),
     ]
     scratch = [
         pltpu.VMEM((GROUPS_AT_ONCE, HALO + block, LANES), F32),
@@ -202,20 +225,23 @@
         pltpu.SemaphoreType.DMA((FETCHES,)),
     ]
     operands = [x, weight, bias, select_t]
-    if arrived is None:
-        kernel, name, scalars = late_kernel, "conv_late", []
+    aliases = {}
+    if late is None:
+        kernel, name, scalars = functools.partial(late_kernel, per_half=per_half), "conv_late", []
         in_specs = [
             pl.BlockSpec((HALO, channels), lambda i, *_: ((first + i) * (block // HALO) - 1, 0))
         ] + in_specs
         operands = [x] + operands
+        out_specs.append(pl.BlockSpec((block, wide), lower_at))
+        out_shape.append(jax.ShapeDtypeStruct((rows // 2, wide), BF16))
     else:
         kernel, name, scalars = early_kernel, "conv_early", [hit]
         n_req = arrived.shape[0]
-        in_specs = [
-            pl.BlockSpec(arrived.shape, lambda *_: (0, 0, 0)),
-            pl.BlockSpec(memory_space=pl.ANY),
-        ] + in_specs
-        operands = [arrived, after] + operands
+        in_specs = (
+            [pl.BlockSpec(arrived.shape, lambda *_: (0, 0, 0))] + in_specs + [pl.BlockSpec(memory_space=pl.ANY)] * 3
+        )
+        operands = [arrived] + operands + list(late)
+        aliases = {6: 0, 7: 1, 8: 2}
         start_shape = (channels // WIDE, STATE, SUBLANES, LANES)
         out_specs.append(pl.BlockSpec(start_shape, lambda *_: (0, 0, 0, 0)))
         out_shape.append(jax.ShapeDtypeStruct(start_shape, F32))
@@ -227,63 +253,60 @@
         kernel,
         grid_spec=pltpu.PrefetchScalarGridSpec(
             num_scalar_prefetch=len(scalars),
-            grid=(n_rows // block,),
+            grid=(steps,),
             in_specs=in_specs,
             out_specs=out_specs,
             scratch_shapes=scratch,
         ),
         out_shape=out_shape,
+        input_output_aliases=aliases,
         compiler_params=pltpu.CompilerParams(vmem_limit_bytes=VMEM_LIMIT),
         cost_estimate=pl.CostEstimate(
-            flops=2 * n_rows * channels * wide,
-            bytes_accessed=n_rows * channels * 24,
-            transcendentals=2 * n_rows * channels,
+            flops=2 * steps * block * channels * wide,
+            bytes_accessed=steps * block * channels * 24,
+            transcendentals=2 * steps * block * channels,
         ),
         name=name,
     )(*scalars, *operands)
 
 
-def scan_kernel(
-    length_ref, *refs, n_parts, first_row, aliased, packed
-):
-    part_refs, refs = refs[:n_parts], refs[n_parts:]
+def scan_kernel(length_ref, *refs):
+    part_refs, refs = refs[:4], refs[4:]
     step_ref, bias_ref, decay_ref, skip_ref, mixed_ref, gate_ref, start_ref, *refs = refs
-    if aliased:
-        refs = refs[1:]
     out_ref, end_ref, norm_scr, wide_scr, value_scr, state_scr, rate_scr, back_scr, *lines = refs
     sizes, drives, scans = lines[0:2], lines[2:4], lines[4:6]
-    channel_block, row_block = pl.program_id(0), pl.program_id(1)
     rows = mixed_ref.shape[0]
     pairs = rows // HALO
-    at_rows = pl.ds(pl.multiple_of(row_block * rows, rows), rows)
-
-    @pl.when(channel_block == 0)
+
+    @pl.when(pl.program_id(0) == 0)
     def _():
-        projected = part_refs[0][...].astype(F32)
-        for part_ref in part_refs[1:]:
-            projected = projected + part_ref[...].astype(F32)
-        low = projected[:, :RANK]
-        scale = lax.rsqrt(jnp.mean(low * low, axis=-1, keepdims=True) + 1e-06)
-        norm_scr[at_rows, :] = (low * scale).astype(BF16)
-        picks = projected[:, RANK:]
-        high = picks.astype(BF16)
-        both = jnp.concatenate([high, (picks - high.astype(F32)).astype(BF16)], axis=1)
         shape = (4 * STATE, 2 * STATE * LANES)
         source = lax.broadcasted_iota(jnp.int32, shape, 0) % (2 * STATE)
         spread = (source == lax.broadcasted_iota(jnp.int32, shape, 1) // LANES).astype(BF16)
-        wide_scr[at_rows, :] = jnp.dot(both, spread, preferred_element_type=F32)
-
-    @pl.when(row_block == 0)
-    def _():
-        state_scr[...] = start_ref[0]
-        rate = -jnp.exp(decay_ref[...]) * LOG2E
-        for sub in range(SUBLANES):
-            rate_scr[pl.ds(sub, STATE, stride=SUBLANES), :] = rate[:, sub * LANES : (sub + 1) * LANES]
-
-    value_scr[...] = jnp.dot(norm_scr[at_rows, :], step_ref[...], preferred_element_type=F32)
+        for half in range(2):
+            sum_ref, more_ref = part_refs[2 * half : 2 * half + 2]
+            for first in range(0, rows // 2, LANES):
+                here = slice(first, first + LANES)
+                there = slice(half * rows // 2 + first, half * rows // 2 + first + LANES)
+                projected = sum_ref[here, :] + more_ref[here, :].astype(F32)
+                low = projected[:, :RANK]
+                scale = lax.rsqrt(jnp.mean(low * low, axis=-1, keepdims=True) + 1e-06)
+                norm_scr[there, :] = (low * scale).astype(BF16)
+                picks = projected[:, RANK:]
+                high = picks.astype(BF16)
+                both = jnp.concatenate([high, (picks - high.astype(F32)).astype(BF16)], axis=1)
+                wide_scr[there, :] = jnp.dot(both, spread, preferred_element_type=F32)
+
+    state_scr[...] = start_ref[0]
+    rate = -jnp.exp(decay_ref[...]) * LOG2E
+    for sub in range(SUBLANES):
+        rate_scr[pl.ds(sub, STATE, stride=SUBLANES), :] = rate[:, sub * LANES : (sub + 1) * LANES]
+    for first in range(0, rows, LANES):
+        here = slice(first, first + LANES)
+        value_scr[here, :] = jnp.dot(norm_scr[here, :], step_ref[...], preferred_element_type=F32)
     rates = [rate_scr[n * SUBLANES : (n + 1) * SUBLANES, :] for n in range(STATE)]
     row_in_tile = lax.broadcasted_iota(jnp.int32, (SUBLANES, LANES), 0)
-    left = length_ref[0] - first_row - row_block * rows
+    left = length_ref[0]
 
     def steps_of(pair, tile):
         first = pl.multiple_of(pair * HALO, HALO)
@@ -300,7 +323,7 @@
 
     def advance(state, pair, tile):
         state = list(state)
-        first = pl.multiple_of(row_block * rows + pair * HALO + tile * SUBLANES, SUBLANES)
+        first = pl.multiple_of(pair * HALO + tile * SUBLANES, SUBLANES)
         picks = wide_scr.at[pl.ds(first, SUBLANES), :]
         for position in range(SUBLANES):
             here = slice(position * SUBLANES, (position + 1) * SUBLANES)
@@ -336,88 +359,71 @@
         steps_of(jnp.minimum(pair + 1, pairs - 1), 0)
         return advance(state, pair, 1)
 
+    def some_pairs(step, state):
+        for k in range(PAIRS):
+            state = one_pair(step * PAIRS + k, state)
+        return state
+
     steps_of(0, 0)
-    state = lax.fori_loop(0, pairs, one_pair, tuple(state_scr[n] for n in range(STATE)))
+    state = lax.fori_loop(0, pairs // PAIRS, some_pairs, tuple(state_scr[n] for n in range(STATE)))
     gate_of(pairs - 1)
-    for n in range(STATE):
-        state_scr[n] = state[n]
-
-    @pl.when(row_block == pl.num_programs(1) - 1)
-    def _():
-        if packed:
-            low = low_half()
-            for row in range(STATE // 2):
-                a, b = state_scr[2 * row], state_scr[2 * row + 1]
-                even = jnp.where(low, a, pltpu.roll(b, HALF, 1))
-                odd = jnp.where(low, pltpu.roll(a, HALF, 1), b)
-                back_scr[pl.ds(row, SUBLANES, stride=2 * SUBLANES), :] = even
-                back_scr[pl.ds(SUBLANES + row, SUBLANES, stride=2 * SUBLANES), :] = odd
-            end_ref[...] = back_scr[...].astype(BF16).reshape(end_ref.shape)
-        else:
-            end_ref[0] = state_scr[...]
-
-
-def scan_rows(length, parts, step_weight, step_bias, decay_log, skip_gain, mixed, gate, start, out, first_row, block):
-    n_rows, channels = mixed.shape
+
+    low = low_half()
+    for row in range(STATE // 2):
+        a, b = state[2 * row], state[2 * row + 1]
+        even = jnp.where(low, a, pltpu.roll(b, HALF, 1))
+        odd = jnp.where(low, pltpu.roll(a, HALF, 1), b)
+        back_scr[pl.ds(row, SUBLANES, stride=2 * SUBLANES), :] = even
+        back_scr[pl.ds(SUBLANES + row, SUBLANES, stride=2 * SUBLANES), :] = odd
+    end_ref[...] = back_scr[...].astype(BF16).reshape(end_ref.shape)
+
+
+def scan_rows(length, parts, step_weight, step_bias, decay_log, skip_gain, mixed, gate, start):
+    rows, channels = mixed.shape
     blocks = channels // WIDE
-    first = first_row // block
-    wide = parts[0].shape[1]
-    packed = first_row > 0
-    by_channel = lambda c, i, *_: (0, c)
-    part_spec = pl.BlockSpec((block, wide), lambda c, i, *_: (jnp.where(c == 0, i, 0), 0))
-    state_shape = (1, STATE, SUBLANES, LANES)
-    state_spec = pl.BlockSpec(state_shape, lambda c, i, *_: (c, 0, 0, 0))
-    operands = [length, *parts, step_weight, step_bias, decay_log, skip_gain, mixed, gate, start]
-    in_specs = [part_spec] * len(parts) + [
-        pl.BlockSpec((RANK, WIDE), by_channel),
-        pl.BlockSpec((1, WIDE), by_channel),
-        pl.BlockSpec((STATE, WIDE), by_channel),
-        pl.BlockSpec((1, WIDE), by_channel),
-        pl.BlockSpec((block, WIDE), lambda c, i, *_: (i, c)),
-        pl.BlockSpec((block, WIDE), lambda c, i, *_: (first + i, c)),
-        state_spec,
-    ]
-    aliases = {}
-    if out is not None:
-        aliases = {len(operands): 0}
-        operands.append(out)
-        in_specs.append(pl.BlockSpec(memory_space=pl.ANY))
-    if packed:
-        per_block = WIDE // HALF
-        end_spec = pl.BlockSpec((per_block, SUBLANES, LANES), lambda c, i, *_: (c, 0, 0))
-        end_shape = jax.ShapeDtypeStruct((blocks * per_block, SUBLANES, LANES), BF16)
-    else:
-        end_spec = state_spec
-        end_shape = jax.ShapeDtypeStruct((blocks, *state_shape[1:]), F32)
+    by_channel = lambda c, *_: (0, c)
+    per_block = WIDE // HALF
     return pl.pallas_call(
-        functools.partial(
-            scan_kernel, n_parts=len(parts), first_row=first_row, aliased=out is not None, packed=packed
-        ),
+        scan_kernel,
         grid_spec=pltpu.PrefetchScalarGridSpec(
             num_scalar_prefetch=1,
-            grid=(blocks, n_rows // block),
-            in_specs=in_specs,
-            out_specs=[pl.BlockSpec((block, WIDE), lambda c, i, *_: (first + i, c)), end_spec],
+            grid=(blocks,),
+            in_specs=[pl.BlockSpec(part.shape, lambda c, *_: (0, 0)) for part in parts]
+            + [
+                pl.BlockSpec((RANK, WIDE), by_channel),
+                pl.BlockSpec((1, WIDE), by_channel),
+                pl.BlockSpec((STATE, WIDE), by_channel),
+                pl.BlockSpec((1, WIDE), by_channel),
+                pl.BlockSpec((rows, WIDE), by_channel),
+                pl.BlockSpec((rows, WIDE), by_channel),
+                pl.BlockSpec((1, STATE, SUBLANES, LANES), lambda c, *_: (c, 0, 0, 0)),
+            ],
+            out_specs=[
+                pl.BlockSpec((rows, WIDE), by_channel),
+                pl.BlockSpec((per_block, SUBLANES, LANES), lambda c, *_: (c, 0, 0)),
+            ],
             scratch_shapes=[
-                pltpu.VMEM((n_rows, RANK), BF16),
-                pltpu.VMEM((n_rows, 2 * STATE * LANES), F32),
-                pltpu.VMEM((block, WIDE), F32),
+                pltpu.VMEM((rows, RANK), BF16),
+                pltpu.VMEM((rows, 2 * STATE * LANES), F32),
+                pltpu.VMEM((rows, WIDE), F32),
                 pltpu.VMEM((STATE, SUBLANES, LANES), F32),
                 pltpu.VMEM((STATE * SUBLANES, LANES), F32),
-                pltpu.VMEM((WIDE // HALF * SUBLANES, LANES), F32),
+                pltpu.VMEM((per_block * SUBLANES, LANES), F32),
             ]
             + [pltpu.VMEM((SUBLANES * SUBLANES, LANES), F32)] * 6,
         ),
-        out_shape=[jax.ShapeDtypeStruct(gate.shape, BF16), end_shape],
-        input_output_aliases=aliases,
+        out_shape=[
+            jax.ShapeDtypeStruct(gate.shape, BF16),
+            jax.ShapeDtypeStruct((blocks * per_block, SUBLANES, LANES), BF16),
+        ],
         compiler_params=pltpu.CompilerParams(vmem_limit_bytes=VMEM_LIMIT),
         cost_estimate=pl.CostEstimate(
-            flops=2 * n_rows * channels * RANK + 100 * n_rows * channels * STATE,
-            bytes_accessed=n_rows * channels * 8,
-            transcendentals=n_rows * channels * STATE,
+            flops=2 * rows * channels * RANK + 100 * rows * channels * STATE,
+            bytes_accessed=rows * channels * 8,
+            transcendentals=rows * channels * STATE,
         ),
         name="scan_rows",
-    )(*operands)
+    )(length, *parts, step_weight, step_bias, decay_log, skip_gain, mixed, gate, start)
 
 
 def save_kernel(slot_ref, half_ref, tiles_ref, store_ref, out_ref, tiles_scr, *, n_rows, first_row, halves):
@@ -458,10 +464,15 @@
     )(save_slot.reshape(n_req, 1), half, tiles, store)
 
 
-def from_others(part, sent, n_tp):
-    return [part] + [
-        lax.ppermute(sent, "tp", [(d, (d + s) % n_tp) for d in range(n_tp)]) for s in range(1, n_tp)
-    ]
+def pairwise(part, sent, n_tp):
+    rows = sent[0].shape[0]
+    inner = [(d, d ^ 1) for d in range(n_tp)]
+    outer = [(d, n_tp - 1 - d) for d in range(n_tp)]
+    orders = ((inner, outer), (outer, inner))
+    got = [lax.ppermute(half, "tp", order[0]) for half, order in zip(sent, orders)]
+    sums = [part[k * rows : (k + 1) * rows] + got[k].astype(F32) for k in range(2)]
+    more = [lax.ppermute(total.astype(BF16), "tp", order[1]) for total, order in zip(sums, orders)]
+    return [sums[0], more[0], sums[1], more[1]]
 
 
 def local(
@@ -494,25 +505,17 @@
     conv_bias = conv_bias.reshape(1, channels)
     step_bias = step_bias.reshape(1, channels)
     skip_gain = skip_gain.reshape(1, channels)
-    block = 128
-    late_mixed, late_part, late_sent = conv_rows(
-        conv_input, conv_weight, conv_bias, select_t, block, local_rows - block, block
+    block = local_rows // 4
+    conv = functools.partial(conv_rows, conv_input, conv_weight, conv_bias, select_t, block)
+    *late, lower = conv()
+    mixed, part, upper, start = conv(arrived, cache_hit, late)
+    half = (lax.axis_index("req") % 2).astype(jnp.int32).reshape(1)
+    new_edges = save(save_slot, half, arrived, edges, edge_rows, NEXT_AT, True)
+    parts = pairwise(part, (upper, lower), n_tp)
+    new_edges, *parts = lax.optimization_barrier((new_edges, *parts))
+    out, back = scan_rows(
+        suffix_length, parts, step_weight, step_bias, decay_log, skip_gain, mixed, gate_input, start
     )
-    late_parts = from_others(late_part, late_sent, n_tp)
-    early_mixed, early_part, early_sent, start = conv_rows(
-        conv_input, conv_weight, conv_bias, select_t, 0, block, block, arrived, cache_hit, late_part
-    )
-    early_parts = from_others(early_part, early_sent, n_tp)
-
-    scan = functools.partial(scan_rows, block=block)
-    shared = (step_weight, step_bias, decay_log, skip_gain)
-    out, state = scan(suffix_length, early_parts, *shared, early_mixed, gate_input, start, None, 0)
-    out, back = scan(suffix_length, late_parts, *shared, late_mixed, gate_input, state, out, block)
-
-    half = (lax.axis_index("req") % 2).astype(jnp.int32).reshape(1)
-    arrived, back = lax.optimization_barrier((arrived, back))
-    new_edges = save(save_slot, half, arrived, edges, edge_rows, NEXT_AT, True)
-    new_edges, back = lax.optimization_barrier((new_edges, back))
     back = lax.all_to_all(back, "req", split_axis=0, concat_axis=0, tiled=True)
     new_store = save(save_slot, half, back, store, STATE // 2, 0, False)
     new_state = new_store.reshape(1, STATE, stripe, slots).transpose(3, 0, 1, 2)

time: 133 us -> 122 us (0.917)
  waiting for transfers between devices: 17.3 us -> 7.82 us
  Pallas kernels: 71 us -> 65.5 us
  blocking collectives: 18.9 us -> 21.3 us
  other arithmetic: 0 us -> 2.11 us
    ppermute x6 -> x4, waiting for transfers between devices: 13.6 us -> 7.43 us  [the longest x2 5.05 us: pairwise(): lax.ppermute(half, 'tp', order[0])]
    pallas_call x2 -> x1, Pallas kernels: 52.8 us -> 46.8 us  [scan_rows(): pl.pallas_call(scan_kernel, grid_spec=pltpu.PrefetchScalarGridSpec(num_sc...]
    all_to_all x1, waiting for transfers between devices: 3.69 us -> 0.4 us  [local(): lax.all_to_all(outgoing, 'req', split_axis=0, concat_axis=0, tiled=True)]
    all_to_all x1, blocking collectives: 18.9 us -> 21.3 us  [local(): back = lax.all_to_all(back, 'req', split_axis=0, concat_axis=0, tiled=True)]
    convert_element_type x0 -> x1, other arithmetic: none -> 2.11 us  [pairwise(): total.astype(BF16)]
    ppermute x6 -> x4, starting transfers between devices: 7.95 us -> 7.5 us  [the longest x2 4.2 us: pairwise(): lax.ppermute(half, 'tp', order[0])]
  transfers between devices with their start and end apart: 7 -> 5, of which waited for: 2 -> 3; matrix products, arithmetic and copies ran while one was open for 0% -> 0% of each run, Pallas kernels for 17% -> 12%
where the time goes in v3:
time: 122 us
  Pallas kernels  65.5 us (54%)
  blocking collectives  21.3 us (17%)
  starting transfers between devices  20.5 us (17%)
  waiting for transfers between devices  7.82 us (6%)
  local copies, waits for them, and re-layouts  2.44 us (2%)
  other arithmetic  2.11 us (2%)
  between operations  1.98 us (2%)
    pallas_call x1, Pallas kernels, scan_rows(): pl.pallas_call(scan_kernel, grid_spec=pltpu.PrefetchScalarGridSpec(num_sc...  46.8 us
    all_to_all x1, blocking collectives, local(): back = lax.all_to_all(back, 'req', split_axis=0, concat_axis=0, tiled=True)  21.3 us
    pallas_call x2, Pallas kernels, conv_rows(): pl.pallas_call(kernel, grid_spec=pltpu.PrefetchScalarGridSpec(num_scalar_...  13.8 us
    all_to_all x1, starting transfers between devices, local(): lax.all_to_all(outgoing, 'req', split_axis=0, concat_axis=0, tiled=True)  13 us
    ppermute x2, waiting for transfers between devices, pairwise(): lax.ppermute(half, 'tp', order[0])  5.05 us
    ppermute x2, starting transfers between devices, pairwise(): lax.ppermute(half, 'tp', order[0])  4.2 us
    ppermute x2, starting transfers between devices, pairwise(): lax.ppermute(total.astype(BF16), 'tp', order[1])  3.3 us
    pallas_call x1, Pallas kernels, pack(): pl.pallas_call(pack_kernel, grid_spec=pltpu.PrefetchScalarGridSpec(num_sc...  2.86 us
  transfers between devices with their start and end apart: 5, of which 3 were waited for; matrix products, arithmetic and copies ran while one was open for 0% of the time, Pallas kernels for 12%

profile of v3, /device:TPU:1, one launch (start us, length us, event | category | flops | bytes accessed | tf_op | source)
XLA Modules:
  0.0 121.7 jit_solution(8653402707953523990)
XLA Ops:
  1.3 2.9 %pack.1 = bf16[64,16,128]{2,1,0:T(8,128)(2,1)} custom-call(s32[1]{0:T(128)S(6)} %copy.27.length_ref, s32[1,64]{1,0:T(1,128)} %bitcast.29, f32[1024,128]{1,0:T(8,128)} %bitcast.19, bf16[192,128]{1,0:T(8,128)(2,1)} %bitcast.21, bf16[512,4096]{1,0:T(8,128)(2,1)} %x_ref.5), custom_call_target="tpu_custom_call" | custom-call | tf_op jit(solution)/shard_map/pack/pallas_call | solution.py:77
  4.1 13.0 %all-to-all-start = ((bf16[64,16,128]{2,1,0:T(8,128)(2,1)}), bf16[64,16,128]{2,1,0:T(8,128)(2,1)S(1)}, u32[]{:S(2)}, u32[]{:S(2)}) async-start(bf16[64,16,128]{2,1,0:T(8,128)(2,1)} %pack.1), calls=%async_computation | async-start | bytes 524288 | tf_op jit(solution)/shard_map/all_to_all | solution.py:502
  17.2 9.3 %conv_late.1 = (bf16[512,4096]{1,0:T(8,128)(2,1)}, f32[512,288]{1,0:T(8,128)}, bf16[256,288]{1,0:T(8,128)(2,1)}, bf16[256,288]{1,0:T(8,128)(2,1)}) custom-call(bf16[512,4096]{1,0:T(8,128)(2,1)} %x_ref.5, bf16[512,4096]{1,0:T(8,128)(2,1)} %x_ref.5, f32[4,4096]{1,0:T(4,128)} %weight_ref.3, f32[1,4096]{1,0:T(1,128)} %bitcast.26, bf16[288,4096]{1,0:T(8,128)(2,1)} %bitcast.23), custom_call_target="tpu_custom_call" | custom-call | flops 905969664 | bytes 37748736 | tf_op jit(solution)/shard_map/conv_late/pallas_call | solution.py:252
  26.4 2.8 %collective-permute-start.2 = (bf16[256,288]{1,0:T(8,128)(2,1)}, bf16[256,288]{1,0:T(8,128)(2,1)S(1)}, u32[]{:S(2)}, u32[]{:S(2)}) collective-permute-start(bf16[256,288]{1,0:T(8,128)(2,1)} %get-tuple-element.23), channel_id=1, source_target_pairs={{0,3},{1,2},{2,1},{3,0},{4,7},{5,6},{6,5},{7,4},{8,11},{9,10},{10,... | collective-permute-start | bytes 442376 | tf_op jit(solution)/shard_map/ppermute | solution.py:472
  29.9 0.4 all-to-all-done.tiles_ref.arrived_ref
  30.3 0.0 copy-start
  30.3 0.7 copy-done
  31.0 0.0 copy-start.4
  31.0 0.0 copy-start.3
  31.0 4.5 %conv_early.1 = (bf16[512,4096]{1,0:T(8,128)(2,1)}, f32[512,288]{1,0:T(8,128)}, bf16[256,288]{1,0:T(8,128)(2,1)}, f32[4,16,8,128]{3,2,1,0:T(8,128)}) custom-call(s32[1]{0:T(128)S(6)} %copy.26.hit_ref, bf16[64,16,128]{2,1,0:T(8,128)(2,1)} %copy-done, bf16[512,4096]{1,0:T(8,128)(2,1)} %x_ref.5, ...), custom_call_target="tpu_custom_call", output_to_operand_aliasing={{0}: (6, {}), {1}: (7, {}), {2}: (8, {})} | custom-call | flops 301989888 | bytes 12582912 | tf_op jit(solution)/shard_map/conv_early/pallas_call | solution.py:252
  35.5 1.4 %collective-permute-start = (bf16[256,288]{1,0:T(8,128)(2,1)}, bf16[256,288]{1,0:T(8,128)(2,1)S(1)}, u32[]{:S(2)}, u32[]{:S(2)}) collective-permute-start(bf16[256,288]{1,0:T(8,128)(2,1)} %get-tuple-element.22), channel_id=1, source_target_pairs={{0,1},{1,0},{2,3},{3,2},{4,5},{5,4},{6,7},{7,6},{8,9},{9,8},{10,11... | collective-permute-start | bytes 442376 | tf_op jit(solution)/shard_map/ppermute | solution.py:472
  36.9 0.0 collective-permute-done.2
  36.9 5.0 %collective-permute-done = bf16[256,288]{1,0:T(8,128)(2,1)S(1)} collective-permute-done((bf16[256,288]{1,0:T(8,128)(2,1)}, bf16[256,288]{1,0:T(8,128)(2,1)S(1)}, u32[]{:S(2)}, u32[]{:S(2)}) %collective-permute-start) | collective-permute-done | bytes 147488 | tf_op jit(solution)/shard_map/ppermute | solution.py:472
  42.0 2.1 %fusion = (bf16[256,288]{1,0:T(8,128)(2,1)S(1)}, f32[256,288]{1,0:T(8,128)}, bf16[256,288]{1,0:T(8,128)(2,1)S(1)}, f32[256,288]{1,0:T(8,128)}) fusion(bf16[256,288]{1,0:T(8,128)(2,1)S(1)} %collective-permute-done.2, f32[512,288]{1,0:T(8,128)} %get-tuple-element.21, bf16[256,288]{1,0:T(8,128)(2,1)S(1)} %collective-permute-done), kind=kLoop, calls=%fused_computation.2 | loop fusion | flops 442368 | bytes 1769472 | tf_op jit(solution)/shard_map/convert_element_type | solution.py:474
  44.1 1.4 %collective-permute-start.3 = (bf16[256,288]{1,0:T(8,128)(2,1)S(1)}, bf16[256,288]{1,0:T(8,128)(2,1)S(1)}, u32[]{:S(2)}, u32[]{:S(2)}) collective-permute-start(bf16[256,288]{1,0:T(8,128)(2,1)S(1)} %get-tuple-element.33), channel_id=1, source_target_pairs={{0,1},{1,0},{2,3},{3,2},{4,5},{5,4},{6,7},{7,6},{8,9},{9,8},{10,11... | collective-permute-start | bytes 442376 | tf_op jit(solution)/shard_map/ppermute | solution.py:474
  45.5 1.9 %collective-permute-start.1 = (bf16[256,288]{1,0:T(8,128)(2,1)S(1)}, bf16[256,288]{1,0:T(8,128)(2,1)S(1)}, u32[]{:S(2)}, u32[]{:S(2)}) collective-permute-start(bf16[256,288]{1,0:T(8,128)(2,1)S(1)} %get-tuple-element.37), channel_id=1, source_target_pairs={{0,3},{1,2},{2,1},{3,0},{4,7},{5,6},{6,5},{7,4},{8,11},{9,10},{10,... | collective-permute-start | bytes 442376 | tf_op jit(solution)/shard_map/ppermute | solution.py:474
  47.4 0.0 copy-done.4
  47.4 0.1 copy.21.slot_ref
  47.5 0.0 copy-done.3
  47.5 0.0 copy-start.1
  47.5 0.9 copy-done.1
  48.4 0.9 save.2
  49.4 0.0 collective-permute-done.3.refs_3_
  49.4 0.0 copy-start.5
  49.4 2.4 %collective-permute-done.1.refs_1_ = bf16[256,288]{1,0:T(8,128)(2,1)S(1)} collective-permute-done((bf16[256,288]{1,0:T(8,128)(2,1)S(1)}, bf16[256,288]{1,0:T(8,128)(2,1)S(1)}, u32[]{:S(2)}, u32[]{:S(2)}) %collective-permute-start.1) | collective-permute-done | bytes 147488 | tf_op jit(solution)/shard_map/ppermute | solution.py:474
  51.7 0.0 copy-start.6
  51.7 0.0 copy-done.5
  51.8 0.7 copy-done.6
  52.4 0.0 copy-start.2
  52.4 46.8 %scan_rows.1 = (bf16[512,4096]{1,0:T(8,128)(2,1)}, bf16[64,8,128]{2,1,0:T(8,128)(2,1)}) custom-call(s32[1]{0:T(128)S(6)} %copy.27.length_ref, f32[256,288]{1,0:T(8,128)} %get-tuple-element.24.refs_0_, bf16[256,288]{1,0:T(8,128)(2,1)} %copy-done.6, f32[256,288]{1,0:T(8,128)} %get-tuple-element.26.refs_2_, bf16[256,288]{1,0:T(8,128)(2,1)} %copy-done.5, ...), custom_call_target="tpu_custom_call" | custom-call | flops 4429185024 | bytes 16777216 | tf_op jit(solution)/shard_map/scan_rows/pallas_call | solution.py:386
  99.2 21.3 %all_to_all.10.tiles_ref = bf16[64,8,128]{2,1,0:T(8,128)(2,1)S(1)} all-to-all(bf16[64,8,128]{2,1,0:T(8,128)(2,1)} %get-tuple-element.31), channel_id=1, replica_groups=mesh['req'=64,'tp'=4] {'req'}, dimensions={0} | all-to-all | bytes 262144 | tf_op jit(solution)/shard_map/all_to_all | solution.py:519
  120.6 0.0 copy-done.2
  120.6 1.1 save.3
Async XLA Ops:
  4.1 26.2 %all-to-all-start = ((bf16[64,16,128]{2,1,0:T(8,128)(2,1)}), bf16[64,16,128]{2,1,0:T(8,128)(2,1)S(1)}, u32[]{:S(2)}, u32[]{:S(2)}) async-start(bf16[64,16,128]{2,1,0:T(8,128)(2,1)} %pack.1), calls=%async_computation | async-start | bytes 524288 | tf_op jit(solution)/shard_map/all_to_all | solution.py:502
  26.4 10.5 %collective-permute-start.2 = (bf16[256,288]{1,0:T(8,128)(2,1)}, bf16[256,288]{1,0:T(8,128)(2,1)S(1)}, u32[]{:S(2)}, u32[]{:S(2)}) collective-permute-start(bf16[256,288]{1,0:T(8,128)(2,1)} %get-tuple-element.23), channel_id=1, source_target_pairs={{0,3},{1,2},{2,1},{3,0},{4,7},{5,6},{6,5},{7,4},{8,11},{9,10},{10,... | collective-permute-start | bytes 442376 | tf_op jit(solution)/shard_map/ppermute | solution.py:472
  30.3 0.7 copy-start
  31.0 16.4 %copy-start.4 = (s32[64]{0:T(128)S(1)}, s32[64]{0:T(128)}, u32[]{:S(2)}) copy-start(s32[64]{0:T(128)} %param.27) | copy-start | bytes 772
  31.0 16.5 %copy-start.3 = (bf16[128,1,3,64]{0,3,2,1:T(8,128)(2,1)S(1)}, bf16[128,1,3,64]{0,3,2,1:T(8,128)(2,1)}, u32[]{:S(2)}) copy-start(bf16[128,1,3,64]{0,3,2,1:T(8,128)(2,1)} %param.25) | copy-start | bytes 147460
  35.5 6.4 %collective-permute-start = (bf16[256,288]{1,0:T(8,128)(2,1)}, bf16[256,288]{1,0:T(8,128)(2,1)S(1)}, u32[]{:S(2)}, u32[]{:S(2)}) collective-permute-start(bf16[256,288]{1,0:T(8,128)(2,1)} %get-tuple-element.22), channel_id=1, source_target_pairs={{0,1},{1,0},{2,3},{3,2},{4,5},{5,4},{6,7},{7,6},{8,9},{9,8},{10,11... | collective-permute-start | bytes 442376 | tf_op jit(solution)/shard_map/ppermute | solution.py:472
  44.1 5.3 %collective-permute-start.3 = (bf16[256,288]{1,0:T(8,128)(2,1)S(1)}, bf16[256,288]{1,0:T(8,128)(2,1)S(1)}, u32[]{:S(2)}, u32[]{:S(2)}) collective-permute-start(bf16[256,288]{1,0:T(8,128)(2,1)S(1)} %get-tuple-element.33), channel_id=1, source_target_pairs={{0,1},{1,0},{2,3},{3,2},{4,5},{5,4},{6,7},{7,6},{8,9},{9,8},{10,11... | collective-permute-start | bytes 442376 | tf_op jit(solution)/shard_map/ppermute | solution.py:474
  45.5 6.3 %collective-permute-start.1 = (bf16[256,288]{1,0:T(8,128)(2,1)S(1)}, bf16[256,288]{1,0:T(8,128)(2,1)S(1)}, u32[]{:S(2)}, u32[]{:S(2)}) collective-permute-start(bf16[256,288]{1,0:T(8,128)(2,1)S(1)} %get-tuple-element.37), channel_id=1, source_target_pairs={{0,3},{1,2},{2,1},{3,0},{4,7},{5,6},{6,5},{7,4},{8,11},{9,10},{10,... | collective-permute-start | bytes 442376 | tf_op jit(solution)/shard_map/ppermute | solution.py:474
  47.5 1.0 copy-start.1
  49.4 2.4 %copy-start.5 = (bf16[256,288]{1,0:T(8,128)(2,1)}, bf16[256,288]{1,0:T(8,128)(2,1)S(1)}, u32[]{:S(2)}) copy-start(bf16[256,288]{1,0:T(8,128)(2,1)S(1)} %collective-permute-done.3.refs_3_) | copy-start | bytes 442372
  51.7 0.7 copy-start.6
  52.4 68.1 %copy-start.2 = (f32[128,1,16,64]{0,3,2,1:T(8,128)S(1)}, f32[128,1,16,64]{0,3,2,1:T(8,128)}, u32[]{:S(2)}) copy-start(f32[128,1,16,64]{0,3,2,1:T(8,128)} %param.24) | copy-start | bytes 1572868

commit v4 on v3

--- a/solution.py
+++ b/solution.py
@@ -99,7 +99,7 @@
     )(length, read_slot.reshape(1, n_req), store, edges, x)
 
 
-def conv_block(prev, x_ref, weight_ref, bias_ref, select_hbm, mixed_ref, part_ref, send, rows_scr, select_ref, sems):
+def conv_block(prev, x_ref, weight_ref, bias_ref, select_hbm, mixed_ref, part_ref, send_ref, rows_scr, select_ref, sems):
     rows = x_ref.shape[0]
     groups = x_ref.shape[1] // LANES
     is_first = pl.program_id(0) == 0
@@ -141,32 +141,19 @@
         select_ref[...], mixed_ref[...], (((1,), (1,)), ((), ())), preferred_element_type=F32
     ).T
     part_ref[...] = part
-    send(part.astype(BF16))
-
-
-def late_kernel(
-    prev_ref, x_ref, weight_ref, bias_ref, select_ref, mixed_ref, part_ref, upper_ref, lower_ref, *scr, per_half
+    send_ref[...] = part.astype(BF16)
+
+
+def late_kernel(prev_ref, x_ref, weight_ref, bias_ref, select_ref, mixed_ref, part_ref, send_ref, *scr):
+    prev = lambda group: prev_ref[:, pl.ds(pl.multiple_of(group * LANES, LANES), LANES)].astype(F32)
+    conv_block(prev, x_ref, weight_ref, bias_ref, select_ref, mixed_ref, part_ref, send_ref, *scr)
+
+
+def early_kernel(
+    hit_ref, arrived_ref, x_ref, weight_ref, bias_ref, select_ref, late_ref, mixed_ref, part_ref, send_ref, start_ref,
+    tiles_scr, edge_scr, *scr
 ):
-    prev = lambda group: prev_ref[:, pl.ds(pl.multiple_of(group * LANES, LANES), LANES)].astype(F32)
-    block = 1 + pl.program_id(0)
-
-    def send(part):
-        @pl.when(block < per_half)
-        def _():
-            upper_ref[...] = part
-
-        @pl.when(block >= per_half)
-        def _():
-            lower_ref[...] = part
-
-    conv_block(prev, x_ref, weight_ref, bias_ref, select_ref, mixed_ref, part_ref, send, *scr)
-
-
-def early_kernel(
-    hit_ref, arrived_ref, x_ref, weight_ref, bias_ref, select_ref, late_mixed, late_part, late_upper,
-    mixed_ref, part_ref, upper_ref, start_ref, tiles_scr, edge_scr, *scr
-):
-    del late_mixed, late_part, late_upper
+    del late_ref
     hit = hit_ref[0] > 0
     n_req = arrived_ref.shape[0]
     pairs = n_req // 2
@@ -186,11 +173,7 @@
     for row in range(CONV - 1):
         edge_scr[pl.ds(HALO - (CONV - 1) + row, pairs, stride=HALO), :] = jnp.where(low, even(EDGE_AT + row), odd(EDGE_AT + row))
     prev = lambda group: edge_scr[pl.ds(pl.multiple_of(group * HALO, HALO), HALO), :]
-
-    def send(part):
-        upper_ref[...] = part
-
-    conv_block(prev, x_ref, weight_ref, bias_ref, select_ref, mixed_ref, part_ref, send, *scr)
+    conv_block(prev, x_ref, weight_ref, bias_ref, select_ref, mixed_ref, part_ref, send_ref, *scr)
 
 
 def conv_rows(x, weight, bias, select_t, block, arrived=None, hit=None, late=None):
@@ -198,7 +181,6 @@
     wide = select_t.shape[0]
     first = 1 if late is None else 0
     steps = rows // block - 1 if late is None else 1
-    per_half = rows // block // 2
     fixed = lambda *_: (0, 0)
     at = lambda i, *_: (first + i, 0)
     in_specs = [
@@ -207,17 +189,11 @@
         pl.BlockSpec((1, channels), fixed),
         pl.BlockSpec(memory_space=pl.ANY),
     ]
-    upper_at = lambda i, *_: (jnp.minimum(first + i, per_half - 1), 0)
-    lower_at = lambda i, *_: (jnp.maximum(first + i - per_half, 0), 0)
-    out_specs = [
-        pl.BlockSpec((block, channels), at),
-        pl.BlockSpec((block, wide), at),
-        pl.BlockSpec((block, wide), upper_at),
-    ]
+    out_specs = [pl.BlockSpec((block, channels), at)] + [pl.BlockSpec((block, wide), lambda i, *_: (i, 0))] * 2
     out_shape = [
         jax.ShapeDtypeStruct((rows, channels), BF16),
-        jax.ShapeDtypeStruct((rows, wide), F32),
-        jax.ShapeDtypeStruct((rows // 2, wide), BF16),
+        jax.ShapeDtypeStruct((steps * block, wide), F32),
+        jax.ShapeDtypeStruct((steps * block, wide), BF16),
     ]
     scratch = [
         pltpu.VMEM((GROUPS_AT_ONCE, HALO + block, LANES), F32),
@@ -227,21 +203,17 @@
     operands = [x, weight, bias, select_t]
     aliases = {}
     if late is None:
-        kernel, name, scalars = functools.partial(late_kernel, per_half=per_half), "conv_late", []
+        kernel, name, scalars = late_kernel, "conv_late", []
         in_specs = [
             pl.BlockSpec((HALO, channels), lambda i, *_: ((first + i) * (block // HALO) - 1, 0))
         ] + in_specs
         operands = [x] + operands
-        out_specs.append(pl.BlockSpec((block, wide), lower_at))
-        out_shape.append(jax.ShapeDtypeStruct((rows // 2, wide), BF16))
     else:
         kernel, name, scalars = early_kernel, "conv_early", [hit]
         n_req = arrived.shape[0]
-        in_specs = (
-            [pl.BlockSpec(arrived.shape, lambda *_: (0, 0, 0))] + in_specs + [pl.BlockSpec(memory_space=pl.ANY)] * 3
-        )
-        operands = [arrived] + operands + list(late)
-        aliases = {6: 0, 7: 1, 8: 2}
+        in_specs = [pl.BlockSpec(arrived.shape, lambda *_: (0, 0, 0))] + in_specs + [pl.BlockSpec(memory_space=pl.ANY)]
+        operands = [arrived] + operands + [late]
+        aliases = {6: 0}
         start_shape = (channels // WIDE, STATE, SUBLANES, LANES)
         out_specs.append(pl.BlockSpec(start_shape, lambda *_: (0, 0, 0, 0)))
         out_shape.append(jax.ShapeDtypeStruct(start_shape, F32))
@@ -283,11 +255,12 @@
         shape = (4 * STATE, 2 * STATE * LANES)
         source = lax.broadcasted_iota(jnp.int32, shape, 0) % (2 * STATE)
         spread = (source == lax.broadcasted_iota(jnp.int32, shape, 1) // LANES).astype(BF16)
-        for half in range(2):
-            sum_ref, more_ref = part_refs[2 * half : 2 * half + 2]
-            for first in range(0, rows // 2, LANES):
+        done = 0
+        for sum_ref, more_ref in (part_refs[:2], part_refs[2:]):
+            for first in range(0, sum_ref.shape[0], LANES):
                 here = slice(first, first + LANES)
-                there = slice(half * rows // 2 + first, half * rows // 2 + first + LANES)
+                there = slice(done, done + LANES)
+                done += LANES
                 projected = sum_ref[here, :] + more_ref[here, :].astype(F32)
                 low = projected[:, :RANK]
                 scale = lax.rsqrt(jnp.mean(low * low, axis=-1, keepdims=True) + 1e-06)
@@ -464,15 +437,9 @@
     )(save_slot.reshape(n_req, 1), half, tiles, store)
 
 
-def pairwise(part, sent, n_tp):
-    rows = sent[0].shape[0]
-    inner = [(d, d ^ 1) for d in range(n_tp)]
-    outer = [(d, n_tp - 1 - d) for d in range(n_tp)]
-    orders = ((inner, outer), (outer, inner))
-    got = [lax.ppermute(half, "tp", order[0]) for half, order in zip(sent, orders)]
-    sums = [part[k * rows : (k + 1) * rows] + got[k].astype(F32) for k in range(2)]
-    more = [lax.ppermute(total.astype(BF16), "tp", order[1]) for total, order in zip(sums, orders)]
-    return [sums[0], more[0], sums[1], more[1]]
+def pairwise(part, sent, orders):
+    total = part + lax.ppermute(sent, "tp", orders[0]).astype(F32)
+    return [total, lax.ppermute(total.astype(BF16), "tp", orders[1])]
 
 
 def local(
@@ -507,11 +474,14 @@
     skip_gain = skip_gain.reshape(1, channels)
     block = local_rows // 4
     conv = functools.partial(conv_rows, conv_input, conv_weight, conv_bias, select_t, block)
-    *late, lower = conv()
-    mixed, part, upper, start = conv(arrived, cache_hit, late)
+    inner = [(d, d ^ 1) for d in range(n_tp)]
+    outer = [(d, n_tp - 1 - d) for d in range(n_tp)]
+    late, late_part, late_sent = conv()
+    late_parts = pairwise(late_part, late_sent, (outer, inner))
+    mixed, early_part, early_sent, start = conv(arrived, cache_hit, late)
+    parts = pairwise(early_part, early_sent, (inner, outer)) + late_parts
     half = (lax.axis_index("req") % 2).astype(jnp.int32).reshape(1)
     new_edges = save(save_slot, half, arrived, edges, edge_rows, NEXT_AT, True)
-    parts = pairwise(part, (upper, lower), n_tp)
     new_edges, *parts = lax.optimization_barrier((new_edges, *parts))
     out, back = scan_rows(
         suffix_length, parts, step_weight, step_bias, decay_log, skip_gain, mixed, gate_input, start

time: 122 us -> 118 us (0.967)
  waiting for transfers between devices: 7.82 us -> 2.87 us
  blocking collectives: 21.3 us -> 22.8 us
    ppermute x4, waiting for transfers between devices: 7.43 us -> 2 us  [the longest x2 1.98 us: pairwise(): total = part + lax.ppermute(sent, 'tp', orders[0]).astype(F32)]
    all_to_all x1, blocking collectives: 21.3 us -> 22.8 us  [local(): back = lax.all_to_all(back, 'req', split_axis=0, concat_axis=0, tiled=True)]
    convert_element_type x1 -> x2, other arithmetic: 2.11 us -> 2.54 us  [pairwise(): return [total, lax.ppermute(total.astype(BF16), 'tp', orders[1])]]
  transfers between devices with their start and end apart: 5 -> 5, of which waited for: 3 -> 2; matrix products, arithmetic and copies ran while one was open for 0% -> 2% of each run, Pallas kernels for 12% -> 12%
where the time goes in v4:
time: 118 us
  Pallas kernels  65.1 us (55%)
  blocking collectives  22.8 us (19%)
  starting transfers between devices  20.1 us (17%)
  waiting for transfers between devices  2.87 us (2%)
  other arithmetic  2.54 us (2%)
  local copies, waits for them, and re-layouts  2.52 us (2%)
  between operations  1.98 us (2%)
    pallas_call x1, Pallas kernels, scan_rows(): pl.pallas_call(scan_kernel, grid_spec=pltpu.PrefetchScalarGridSpec(num_sc...  46.8 us
    all_to_all x1, blocking collectives, local(): back = lax.all_to_all(back, 'req', split_axis=0, concat_axis=0, tiled=True)  22.8 us
    pallas_call x2, Pallas kernels, conv_rows(): pl.pallas_call(kernel, grid_spec=pltpu.PrefetchScalarGridSpec(num_scalar_...  13.4 us
    all_to_all x1, starting transfers between devices, local(): lax.all_to_all(outgoing, 'req', split_axis=0, concat_axis=0, tiled=True)  13 us
    ppermute x2, starting transfers between devices, pairwise(): total = part + lax.ppermute(sent, 'tp', orders[0]).astype(F32)  4.21 us
    ppermute x2, starting transfers between devices, pairwise(): return [total, lax.ppermute(total.astype(BF16), 'tp', orders[1])]  2.9 us
    pallas_call x1, Pallas kernels, pack(): pl.pallas_call(pack_kernel, grid_spec=pltpu.PrefetchScalarGridSpec(num_sc...  2.87 us
    convert_element_type x2, other arithmetic, pairwise(): return [total, lax.ppermute(total.astype(BF16), 'tp', orders[1])]  2.54 us
  transfers between devices with their start and end apart: 5, of which 2 were waited for; matrix products, arithmetic and copies ran while one was open for 2% of the time, Pallas kernels for 12%

profile of v4, /device:TPU:1, one launch (start us, length us, event | category | flops | bytes accessed | tf_op | source)
XLA Modules:
  0.0 117.9 jit_solution(6815581892811051560)
XLA Ops:
  1.3 2.9 %pack.1 = bf16[64,16,128]{2,1,0:T(8,128)(2,1)} custom-call(s32[1]{0:T(128)S(6)} %copy.23.length_ref, s32[1,64]{1,0:T(1,128)} %bitcast.29, f32[1024,128]{1,0:T(8,128)} %bitcast.19, bf16[192,128]{1,0:T(8,128)(2,1)} %bitcast.21, bf16[512,4096]{1,0:T(8,128)(2,1)} %x_ref.5), custom_call_target="tpu_custom_call" | custom-call | tf_op jit(solution)/shard_map/pack/pallas_call | solution.py:77
  4.2 13.0 %all-to-all-start = ((bf16[64,16,128]{2,1,0:T(8,128)(2,1)}), bf16[64,16,128]{2,1,0:T(8,128)(2,1)S(1)}, u32[]{:S(2)}, u32[]{:S(2)}) async-start(bf16[64,16,128]{2,1,0:T(8,128)(2,1)} %pack.1), calls=%async_computation | async-start | bytes 524288 | tf_op jit(solution)/shard_map/all_to_all | solution.py:469
  17.2 8.8 %conv_late.1 = (bf16[512,4096]{1,0:T(8,128)(2,1)}, f32[384,288]{1,0:T(8,128)}, bf16[384,288]{1,0:T(8,128)(2,1)}) custom-call(bf16[512,4096]{1,0:T(8,128)(2,1)} %x_ref.5, bf16[512,4096]{1,0:T(8,128)(2,1)} %x_ref.5, f32[4,4096]{1,0:T(4,128)} %weight_ref.3, f32[1,4096]{1,0:T(1,128)} %bitcast.26, bf16[288,4096]{1,0:T(8,128)(2,1)} %bitcast.23), custom_call_target="tpu_custom_call" | custom-call | flops 905969664 | bytes 37748736 | tf_op jit(solution)/shard_map/conv_late/pallas_call | solution.py:224
  26.0 2.8 %collective-permute-start.2 = (bf16[384,288]{1,0:T(8,128)(2,1)}, bf16[384,288]{1,0:T(8,128)(2,1)S(1)}, u32[]{:S(2)}, u32[]{:S(2)}) collective-permute-start(bf16[384,288]{1,0:T(8,128)(2,1)} %get-tuple-element.21), channel_id=1, source_target_pairs={{0,3},{1,2},{2,1},{3,0},{4,7},{5,6},{6,5},{7,4},{8,11},{9,10},{10,... | collective-permute-start | bytes 663560 | tf_op jit(solution)/shard_map/ppermute | solution.py:441
  29.5 0.9 all-to-all-done.tiles_ref.arrived_ref
  30.3 0.0 copy-start
  30.3 0.7 copy-done
  31.0 0.0 copy-start.4
  31.0 0.0 copy-start.5
  31.0 0.0 copy-start.3
  31.0 4.6 %conv_early.1 = (bf16[512,4096]{1,0:T(8,128)(2,1)}, f32[128,288]{1,0:T(8,128)}, bf16[128,288]{1,0:T(8,128)(2,1)}, f32[4,16,8,128]{3,2,1,0:T(8,128)}) custom-call(s32[1]{0:T(128)S(6)} %copy.22.hit_ref, bf16[64,16,128]{2,1,0:T(8,128)(2,1)} %copy-done, bf16[512,4096]{1,0:T(8,128)(2,1)} %x_ref.5, f32[4,4096]{1,0:T(4,128)} %weight_ref.3, ...), custom_call_target="tpu_custom_call", output_to_operand_aliasing={{0}: (6, {})} | custom-call | flops 301989888 | bytes 12582912 | tf_op jit(solution)/shard_map/conv_early/pallas_call | solution.py:224
  35.6 1.4 %collective-permute-start = (bf16[128,288]{1,0:T(8,128)(2,1)}, bf16[128,288]{1,0:T(8,128)(2,1)S(1)}, u32[]{:S(2)}, u32[]{:S(2)}) collective-permute-start(bf16[128,288]{1,0:T(8,128)(2,1)} %get-tuple-element.19), channel_id=1, source_target_pairs={{0,1},{1,0},{2,3},{3,2},{4,5},{5,4},{6,7},{7,6},{8,9},{9,8},{10,11... | collective-permute-start | bytes 221192 | tf_op jit(solution)/shard_map/ppermute | solution.py:441
  37.0 0.0 collective-permute-done.2
  37.0 0.0 copy-done.4
  37.0 0.9 fusion
  37.9 0.2 collective-permute-start.3
  38.1 2.0 %collective-permute-done = bf16[128,288]{1,0:T(8,128)(2,1)S(1)} collective-permute-done((bf16[128,288]{1,0:T(8,128)(2,1)}, bf16[128,288]{1,0:T(8,128)(2,1)S(1)}, u32[]{:S(2)}, u32[]{:S(2)}) %collective-permute-start) | collective-permute-done | bytes 73760 | tf_op jit(solution)/shard_map/ppermute | solution.py:441
  40.1 1.6 %fusion.1 = (bf16[128,288]{1,0:T(8,128)(2,1)S(1)}, f32[128,288]{1,0:T(8,128)}) fusion(f32[128,288]{1,0:T(8,128)} %get-tuple-element.18, bf16[128,288]{1,0:T(8,128)(2,1)S(1)} %collective-permute-done), kind=kLoop, calls=%fused_computation.3 | loop fusion | flops 110592 | bytes 442368 | tf_op jit(solution)/shard_map/convert_element_type | solution.py:442
  41.7 2.7 %collective-permute-start.1 = (bf16[128,288]{1,0:T(8,128)(2,1)S(1)}, bf16[128,288]{1,0:T(8,128)(2,1)S(1)}, u32[]{:S(2)}, u32[]{:S(2)}) collective-permute-start(bf16[128,288]{1,0:T(8,128)(2,1)S(1)} %get-tuple-element.33), channel_id=1, source_target_pairs={{0,3},{1,2},{2,1},{3,0},{4,7},{5,6},{6,5},{7,4},{8,11},{9,10},{10,... | collective-permute-start | bytes 221192 | tf_op jit(solution)/shard_map/ppermute | solution.py:442
  44.4 0.0 copy-done.5
  44.4 0.1 copy.19.slot_ref
  44.5 0.0 copy-done.3
  44.5 0.0 copy-start.1
  44.6 0.9 copy-done.1
  45.5 0.9 save.2
  46.4 0.0 collective-permute-done.3.refs_3_
  46.4 0.0 copy-start.6
  46.4 0.0 collective-permute-done.1.refs_1_
  46.4 0.0 copy-start.7
  46.5 0.7 copy-done.6
  47.1 0.0 copy-done.7
  47.2 0.0 copy-start.2
  47.2 46.8 %scan_rows.1 = (bf16[512,4096]{1,0:T(8,128)(2,1)}, bf16[64,8,128]{2,1,0:T(8,128)(2,1)}) custom-call(s32[1]{0:T(128)S(6)} %copy.23.length_ref, f32[128,288]{1,0:T(8,128)} %get-tuple-element.22.refs_0_, bf16[128,288]{1,0:T(8,128)(2,1)} %copy-done.7, f32[384,288]{1,0:T(8,128)} %get-tuple-element.24.refs_2_, bf16[384,288]{1,0:T(8,128)(2,1)} %copy-done.6, ...), custom_call_target="tpu_custom_call" | custom-call | flops 4429185024 | bytes 16777216 | tf_op jit(solution)/shard_map/scan_rows/pallas_call | solution.py:359
  94.0 22.8 %all_to_all.10.tiles_ref = bf16[64,8,128]{2,1,0:T(8,128)(2,1)S(1)} all-to-all(bf16[64,8,128]{2,1,0:T(8,128)(2,1)} %get-tuple-element.29), channel_id=1, replica_groups=mesh['req'=64,'tp'=4] {'req'}, dimensions={0} | all-to-all | bytes 262144 | tf_op jit(solution)/shard_map/all_to_all | solution.py:489
  116.8 0.0 copy-done.2
  116.8 1.1 save.3
Async XLA Ops:
  4.2 26.2 %all-to-all-start = ((bf16[64,16,128]{2,1,0:T(8,128)(2,1)}), bf16[64,16,128]{2,1,0:T(8,128)(2,1)S(1)}, u32[]{:S(2)}, u32[]{:S(2)}) async-start(bf16[64,16,128]{2,1,0:T(8,128)(2,1)} %pack.1), calls=%async_computation | async-start | bytes 524288 | tf_op jit(solution)/shard_map/all_to_all | solution.py:469
  26.0 11.0 %collective-permute-start.2 = (bf16[384,288]{1,0:T(8,128)(2,1)}, bf16[384,288]{1,0:T(8,128)(2,1)S(1)}, u32[]{:S(2)}, u32[]{:S(2)}) collective-permute-start(bf16[384,288]{1,0:T(8,128)(2,1)} %get-tuple-element.21), channel_id=1, source_target_pairs={{0,3},{1,2},{2,1},{3,0},{4,7},{5,6},{6,5},{7,4},{8,11},{9,10},{10,... | collective-permute-start | bytes 663560 | tf_op jit(solution)/shard_map/ppermute | solution.py:441
  30.3 0.7 copy-start
  31.0 6.0 %copy-start.4 = (f32[384,288]{1,0:T(8,128)S(1)}, f32[384,288]{1,0:T(8,128)}, u32[]{:S(2)}) copy-start(f32[384,288]{1,0:T(8,128)} %get-tuple-element.20) | copy-start | bytes 1327108
  31.0 13.4 %copy-start.5 = (s32[64]{0:T(128)S(1)}, s32[64]{0:T(128)}, u32[]{:S(2)}) copy-start(s32[64]{0:T(128)} %param.27) | copy-start | bytes 772
  31.0 13.5 %copy-start.3 = (bf16[128,1,3,64]{0,3,2,1:T(8,128)(2,1)S(1)}, bf16[128,1,3,64]{0,3,2,1:T(8,128)(2,1)}, u32[]{:S(2)}) copy-start(bf16[128,1,3,64]{0,3,2,1:T(8,128)(2,1)} %param.25) | copy-start | bytes 147460
  35.6 4.4 %collective-permute-start = (bf16[128,288]{1,0:T(8,128)(2,1)}, bf16[128,288]{1,0:T(8,128)(2,1)S(1)}, u32[]{:S(2)}, u32[]{:S(2)}) collective-permute-start(bf16[128,288]{1,0:T(8,128)(2,1)} %get-tuple-element.19), channel_id=1, source_target_pairs={{0,1},{1,0},{2,3},{3,2},{4,5},{5,4},{6,7},{7,6},{8,9},{9,8},{10,11... | collective-permute-start | bytes 221192 | tf_op jit(solution)/shard_map/ppermute | solution.py:441
  37.9 8.5 %collective-permute-start.3 = (bf16[384,288]{1,0:T(8,128)(2,1)S(1)}, bf16[384,288]{1,0:T(8,128)(2,1)S(1)}, u32[]{:S(2)}, u32[]{:S(2)}) collective-permute-start(bf16[384,288]{1,0:T(8,128)(2,1)S(1)} %get-tuple-element.31), channel_id=1, source_target_pairs={{0,1},{1,0},{2,3},{3,2},{4,5},{5,4},{6,7},{7,6},{8,9},{9,8},{10,11... | collective-permute-start | bytes 663560 | tf_op jit(solution)/shard_map/ppermute | solution.py:442
  41.7 4.7 %collective-permute-start.1 = (bf16[128,288]{1,0:T(8,128)(2,1)S(1)}, bf16[128,288]{1,0:T(8,128)(2,1)S(1)}, u32[]{:S(2)}, u32[]{:S(2)}) collective-permute-start(bf16[128,288]{1,0:T(8,128)(2,1)S(1)} %get-tuple-element.33), channel_id=1, source_target_pairs={{0,3},{1,2},{2,1},{3,0},{4,7},{5,6},{6,5},{7,4},{8,11},{9,10},{10,... | collective-permute-start | bytes 221192 | tf_op jit(solution)/shard_map/ppermute | solution.py:442
  44.5 1.0 copy-start.1
  46.4 0.7 copy-start.6
  46.4 0.7 copy-start.7
  47.2 69.6 %copy-start.2 = (f32[128,1,16,64]{0,3,2,1:T(8,128)S(1)}, f32[128,1,16,64]{0,3,2,1:T(8,128)}, u32[]{:S(2)}) copy-start(f32[128,1,16,64]{0,3,2,1:T(8,128)} %param.24) | copy-start | bytes 1572868

commit v5 on v4

--- a/solution.py
+++ b/solution.py
@@ -24,6 +24,7 @@
 FETCHES = 6
 GROUPS_AT_ONCE = 4
 PAIRS = 2
+EARLY_PARTS = 4
 VMEM_LIMIT = 60 * 1024 * 1024
 SMALL_LIMIT = 24 * 1024 * 1024
 
@@ -243,7 +244,7 @@
 
 
 def scan_kernel(length_ref, *refs):
-    part_refs, refs = refs[:4], refs[4:]
+    early_refs, late_refs, refs = refs[:EARLY_PARTS], refs[EARLY_PARTS : EARLY_PARTS + 2], refs[EARLY_PARTS + 2 :]
     step_ref, bias_ref, decay_ref, skip_ref, mixed_ref, gate_ref, start_ref, *refs = refs
     out_ref, end_ref, norm_scr, wide_scr, value_scr, state_scr, rate_scr, back_scr, *lines = refs
     sizes, drives, scans = lines[0:2], lines[2:4], lines[4:6]
@@ -256,12 +257,14 @@
         source = lax.broadcasted_iota(jnp.int32, shape, 0) % (2 * STATE)
         spread = (source == lax.broadcasted_iota(jnp.int32, shape, 1) // LANES).astype(BF16)
         done = 0
-        for sum_ref, more_ref in (part_refs[:2], part_refs[2:]):
+        for sum_ref, *more_refs in (early_refs, late_refs):
             for first in range(0, sum_ref.shape[0], LANES):
                 here = slice(first, first + LANES)
                 there = slice(done, done + LANES)
                 done += LANES
-                projected = sum_ref[here, :] + more_ref[here, :].astype(F32)
+                projected = sum_ref[here, :]
+                for more_ref in more_refs:
+                    projected = projected + more_ref[here, :].astype(F32)
                 low = projected[:, :RANK]
                 scale = lax.rsqrt(jnp.mean(low * low, axis=-1, keepdims=True) + 1e-06)
                 norm_scr[there, :] = (low * scale).astype(BF16)
@@ -432,14 +435,9 @@
         out_specs=pl.BlockSpec(store.shape, whole),
         out_shape=jax.ShapeDtypeStruct(store.shape, store.dtype),
         scratch_shapes=[pltpu.VMEM((n_req * chunk, LANES), F32)],
-        compiler_params=pltpu.CompilerParams(vmem_limit_bytes=SMALL_LIMIT),
+        compiler_params=pltpu.CompilerParams(vmem_limit_bytes=VMEM_LIMIT if halves else SMALL_LIMIT),
         name="save",
     )(save_slot.reshape(n_req, 1), half, tiles, store)
-
-
-def pairwise(part, sent, orders):
-    total = part + lax.ppermute(sent, "tp", orders[0]).astype(F32)
-    return [total, lax.ppermute(total.astype(BF16), "tp", orders[1])]
 
 
 def local(
@@ -466,10 +464,10 @@
     store = store_state.transpose(1, 2, 3, 0).reshape(STATE * stripe, slots)
     edges = store_edge.transpose(1, 2, 3, 0).reshape(edge_rows * stripe, slots)
     outgoing = pack(suffix_length, read_slot, store, edges, conv_input)
+    outgoing, conv_bias = lax.optimization_barrier((outgoing, conv_bias.reshape(1, channels)))
     arrived = lax.all_to_all(outgoing, "req", split_axis=0, concat_axis=0, tiled=True)
 
     select_t = select_weight.T
-    conv_bias = conv_bias.reshape(1, channels)
     step_bias = step_bias.reshape(1, channels)
     skip_gain = skip_gain.reshape(1, channels)
     block = local_rows // 4
@@ -477,12 +475,15 @@
     inner = [(d, d ^ 1) for d in range(n_tp)]
     outer = [(d, n_tp - 1 - d) for d in range(n_tp)]
     late, late_part, late_sent = conv()
-    late_parts = pairwise(late_part, late_sent, (outer, inner))
+    late_got = lax.ppermute(late_sent, "tp", outer)
     mixed, early_part, early_sent, start = conv(arrived, cache_hit, late)
-    parts = pairwise(early_part, early_sent, (inner, outer)) + late_parts
+    more = [lax.ppermute(early_sent, "tp", [(d, (d + k) % n_tp) for d in range(n_tp)]) for k in range(1, n_tp)]
+    late_got, early_sent = lax.optimization_barrier((late_got, early_sent))
+    late_total = late_part + late_got.astype(F32)
+    late_parts = [late_total, lax.ppermute(late_total.astype(BF16), "tp", inner)]
     half = (lax.axis_index("req") % 2).astype(jnp.int32).reshape(1)
     new_edges = save(save_slot, half, arrived, edges, edge_rows, NEXT_AT, True)
-    new_edges, *parts = lax.optimization_barrier((new_edges, *parts))
+    new_edges, *parts = lax.optimization_barrier((new_edges, early_part, *more, *late_parts))
     out, back = scan_rows(
         suffix_length, parts, step_weight, step_bias, decay_log, skip_gain, mixed, gate_input, start
     )

time: 118 us -> 122 us (1.034)
  waiting for transfers between devices: 2.87 us -> 5.39 us
  other arithmetic: 2.54 us -> 0.88 us
  blocking collectives: 22.8 us -> 24.4 us
    ppermute x4 -> x5, waiting for transfers between devices: 2 us -> 4.52 us  [the longest x3 4.4 us: local(): lax.ppermute(early_sent, 'tp', [(d, (d + k) % n_tp) for d in range(n_tp)])]
    convert_element_type x2 -> x1, other arithmetic: 2.54 us -> 0.88 us  [local(): late_total.astype(BF16)]
    all_to_all x1, blocking collectives: 22.8 us -> 24.4 us  [local(): back = lax.all_to_all(back, 'req', split_axis=0, concat_axis=0, tiled=True)]
    ppermute x4 -> x5, starting transfers between devices: 7.11 us -> 7.5 us  [the longest x3 3.48 us: local(): lax.ppermute(early_sent, 'tp', [(d, (d + k) % n_tp) for d in range(n_tp)])]
  transfers between devices with their start and end apart: 5 -> 6, of which waited for: 2 -> 5; matrix products, arithmetic and copies ran while one was open for 2% -> 1% of each run, Pallas kernels for 12% -> 13%
where the time goes in v5:
time: 122 us
  Pallas kernels  66.2 us (54%)
  blocking collectives  24.4 us (20%)
  starting transfers between devices  20.5 us (17%)
  waiting for transfers between devices  5.39 us (4%)
  local copies, waits for them, and re-layouts  2.18 us (2%)
  between operations  1.98 us (2%)
    pallas_call x1, Pallas kernels, scan_rows(): pl.pallas_call(scan_kernel, grid_spec=pltpu.PrefetchScalarGridSpec(num_sc...  46.9 us
    all_to_all x1, blocking collectives, local(): back = lax.all_to_all(back, 'req', split_axis=0, concat_axis=0, tiled=True)  24.4 us
    pallas_call x2, Pallas kernels, conv_rows(): pl.pallas_call(kernel, grid_spec=pltpu.PrefetchScalarGridSpec(num_scalar_...  13.4 us
    all_to_all x1, starting transfers between devices, local(): lax.all_to_all(outgoing, 'req', split_axis=0, concat_axis=0, tiled=True)  13 us
    ppermute x3, waiting for transfers between devices, local(): lax.ppermute(early_sent, 'tp', [(d, (d + k) % n_tp) for d in range(n_tp)])  4.4 us
    ppermute x3, starting transfers between devices, local(): lax.ppermute(early_sent, 'tp', [(d, (d + k) % n_tp) for d in range(n_tp)])  3.48 us
    pallas_call x2, Pallas kernels, save(): pl.pallas_call(functools.partial(save_kernel, n_rows=n_rows, first_row=fi...  2.98 us
    pallas_call x1, Pallas kernels, pack(): pl.pallas_call(pack_kernel, grid_spec=pltpu.PrefetchScalarGridSpec(num_sc...  2.88 us
  transfers between devices with their start and end apart: 6, of which 5 were waited for; matrix products, arithmetic and copies ran while one was open for 1% of the time, Pallas kernels for 13%

profile of v5, /device:TPU:1, one launch (start us, length us, event | category | flops | bytes accessed | tf_op | source)
XLA Modules:
  0.0 121.5 jit_solution(17849930980781226945)
XLA Ops:
  1.3 2.9 %pack.1 = bf16[64,16,128]{2,1,0:T(8,128)(2,1)} custom-call(s32[1]{0:T(128)S(6)} %copy.23.length_ref, s32[1,64]{1,0:T(1,128)} %bitcast.29, f32[1024,128]{1,0:T(8,128)} %bitcast.19, bf16[192,128]{1,0:T(8,128)(2,1)} %bitcast.24, bf16[512,4096]{1,0:T(8,128)(2,1)} %x_ref.5), custom_call_target="tpu_custom_call" | custom-call | tf_op jit(solution)/shard_map/pack/pallas_call | solution.py:78
  4.2 13.0 %all-to-all-start = ((bf16[64,16,128]{2,1,0:T(8,128)(2,1)}), bf16[64,16,128]{2,1,0:T(8,128)(2,1)S(1)}, u32[]{:S(2)}, u32[]{:S(2)}) async-start(bf16[64,16,128]{2,1,0:T(8,128)(2,1)} %pack.1), calls=%async_computation | async-start | bytes 524288 | tf_op jit(solution)/shard_map/all_to_all | solution.py:468
  17.2 8.8 %conv_late.1 = (bf16[512,4096]{1,0:T(8,128)(2,1)}, f32[384,288]{1,0:T(8,128)}, bf16[384,288]{1,0:T(8,128)(2,1)}) custom-call(bf16[512,4096]{1,0:T(8,128)(2,1)} %x_ref.5, bf16[512,4096]{1,0:T(8,128)(2,1)} %x_ref.5, f32[4,4096]{1,0:T(4,128)} %weight_ref.3, f32[1,4096]{1,0:T(1,128)} %bitcast.26, bf16[288,4096]{1,0:T(8,128)(2,1)} %bitcast.21), custom_call_target="tpu_custom_call" | custom-call | flops 905969664 | bytes 37748736 | tf_op jit(solution)/shard_map/conv_late/pallas_call | solution.py:225
  26.0 2.8 %collective-permute-start.3 = (bf16[384,288]{1,0:T(8,128)(2,1)}, bf16[384,288]{1,0:T(8,128)(2,1)S(1)}, u32[]{:S(2)}, u32[]{:S(2)}) collective-permute-start(bf16[384,288]{1,0:T(8,128)(2,1)} %get-tuple-element.28), channel_id=1, source_target_pairs={{0,3},{1,2},{2,1},{3,0},{4,7},{5,6},{6,5},{7,4},{8,11},{9,10},{10,... | collective-permute-start | bytes 663560 | tf_op jit(solution)/shard_map/ppermute | solution.py:478
  29.5 0.9 all-to-all-done.tiles_ref.arrived_ref
  30.3 0.0 copy-start.2
  30.3 0.7 copy-done.2
  31.1 0.0 copy-start.3
  31.1 0.0 copy-start.4
  31.1 4.6 %conv_early.1 = (bf16[512,4096]{1,0:T(8,128)(2,1)}, f32[128,288]{1,0:T(8,128)}, bf16[128,288]{1,0:T(8,128)(2,1)}, f32[4,16,8,128]{3,2,1,0:T(8,128)}) custom-call(s32[1]{0:T(128)S(6)} %copy.22.hit_ref, bf16[64,16,128]{2,1,0:T(8,128)(2,1)} %copy-done.2, bf16[512,4096]{1,0:T(8,128)(2,1)} %x_ref.5, ...), custom_call_target="tpu_custom_call", output_to_operand_aliasing={{0}: (6, {})} | custom-call | flops 301989888 | bytes 12582912 | tf_op jit(solution)/shard_map/conv_early/pallas_call | solution.py:225
  35.6 0.1 collective-permute-done.3
  35.8 0.0 copy-done.3
  35.8 0.9 fusion
  36.6 1.2 collective-permute-start.4
  37.8 1.9 %collective-permute-start.2 = (bf16[128,288]{1,0:T(8,128)(2,1)}, bf16[128,288]{1,0:T(8,128)(2,1)S(1)}, u32[]{:S(2)}, u32[]{:S(2)}) collective-permute-start(bf16[128,288]{1,0:T(8,128)(2,1)} %get-tuple-element.26), channel_id=1, source_target_pairs={{0,3},{1,0},{2,1},{3,2},{4,7},{5,4},{6,5},{7,6},{8,11},{9,8},{10,9... | collective-permute-start | bytes 221192 | tf_op jit(solution)/shard_map/ppermute | solution.py:480
  39.7 0.7 collective-permute-start.1
  40.5 0.9 collective-permute-start
  41.3 0.0 copy-done.4
  41.3 0.7 copy.19.slot_ref
  42.0 1.9 %save.2 = bf16[192,128]{1,0:T(8,128)(2,1)} custom-call(s32[64,1]{1,0:T(8,128)} %copy.19.slot_ref, s32[1]{0:T(128)} %bitcast.1.half_ref, bf16[64,16,128]{2,1,0:T(8,128)(2,1)} %copy-done.2, bf16[192,128]{1,0:T(8,128)(2,1)} %bitcast.25), custom_call_target="tpu_custom_call" | custom-call | tf_op jit(solution)/shard_map/save/pallas_call | solution.py:426
  43.9 2.1 %collective-permute-done.2.refs_3_ = bf16[128,288]{1,0:T(8,128)(2,1)S(1)} collective-permute-done((bf16[128,288]{1,0:T(8,128)(2,1)}, bf16[128,288]{1,0:T(8,128)(2,1)S(1)}, u32[]{:S(2)}, u32[]{:S(2)}) %collective-permute-start.2) | collective-permute-done | bytes 73760 | tf_op jit(solution)/shard_map/ppermute | solution.py:480
  46.0 0.0 copy-start.6
  46.0 2.0 %collective-permute-done.1.refs_2_ = bf16[128,288]{1,0:T(8,128)(2,1)S(1)} collective-permute-done((bf16[128,288]{1,0:T(8,128)(2,1)}, bf16[128,288]{1,0:T(8,128)(2,1)S(1)}, u32[]{:S(2)}, u32[]{:S(2)}) %collective-permute-start.1) | collective-permute-done | bytes 73760 | tf_op jit(solution)/shard_map/ppermute | solution.py:480
  48.1 0.0 copy-start.7
  48.1 0.3 collective-permute-done.refs_1_
  48.3 0.0 copy-start.8
  48.3 0.0 collective-permute-done.4.refs_5_
  48.3 0.0 copy-start.5
  48.3 0.0 copy-done.6
  48.3 0.4 copy-done.7
  48.7 0.3 copy-done.8
  49.0 0.1 copy-done.5
  49.1 0.0 copy-start
  49.1 0.0 copy-start.1
  49.1 46.9 %scan_rows.1 = (bf16[512,4096]{1,0:T(8,128)(2,1)}, bf16[64,8,128]{2,1,0:T(8,128)(2,1)}) custom-call(s32[1]{0:T(128)S(6)} %copy.23.length_ref, f32[128,288]{1,0:T(8,128)} %get-tuple-element.30.refs_0_, bf16[128,288]{1,0:T(8,128)(2,1)} %copy-done.8, bf16[128,288]{1,0:T(8,128)(2,1)} %copy-done.7, bf16[128,288]{1,0:T(8,128)(2,1)} %copy-done.6, ...), custom_call_target="tpu_custom_call" | custom-call | flops 4429185024 | bytes 16777216 | tf_op jit(solution)/shard_map/scan_rows/pallas_call | solution.py:362
  96.0 24.4 %all_to_all.10.tiles_ref = bf16[64,8,128]{2,1,0:T(8,128)(2,1)S(1)} all-to-all(bf16[64,8,128]{2,1,0:T(8,128)(2,1)} %get-tuple-element.39), channel_id=1, replica_groups=mesh['req'=64,'tp'=4] {'req'}, dimensions={0} | all-to-all | bytes 262144 | tf_op jit(solution)/shard_map/all_to_all | solution.py:490
  120.4 0.0 copy-done
  120.4 0.0 copy-done.1
  120.4 1.1 save.3
Async XLA Ops:
  4.2 26.2 %all-to-all-start = ((bf16[64,16,128]{2,1,0:T(8,128)(2,1)}), bf16[64,16,128]{2,1,0:T(8,128)(2,1)S(1)}, u32[]{:S(2)}, u32[]{:S(2)}) async-start(bf16[64,16,128]{2,1,0:T(8,128)(2,1)} %pack.1), calls=%async_computation | async-start | bytes 524288 | tf_op jit(solution)/shard_map/all_to_all | solution.py:468
  26.0 9.8 %collective-permute-start.3 = (bf16[384,288]{1,0:T(8,128)(2,1)}, bf16[384,288]{1,0:T(8,128)(2,1)S(1)}, u32[]{:S(2)}, u32[]{:S(2)}) collective-permute-start(bf16[384,288]{1,0:T(8,128)(2,1)} %get-tuple-element.28), channel_id=1, source_target_pairs={{0,3},{1,2},{2,1},{3,0},{4,7},{5,6},{6,5},{7,4},{8,11},{9,10},{10,... | collective-permute-start | bytes 663560 | tf_op jit(solution)/shard_map/ppermute | solution.py:478
  30.3 0.7 copy-start.2
  31.1 4.7 %copy-start.3 = (f32[384,288]{1,0:T(8,128)S(1)}, f32[384,288]{1,0:T(8,128)}, u32[]{:S(2)}) copy-start(f32[384,288]{1,0:T(8,128)} %get-tuple-element.27) | copy-start | bytes 1327108
  31.1 10.3 %copy-start.4 = (s32[64]{0:T(128)S(1)}, s32[64]{0:T(128)}, u32[]{:S(2)}) copy-start(s32[64]{0:T(128)} %param.27) | copy-start | bytes 772
  36.6 11.7 %collective-permute-start.4 = (bf16[384,288]{1,0:T(8,128)(2,1)S(1)}, bf16[384,288]{1,0:T(8,128)(2,1)S(1)}, u32[]{:S(2)}, u32[]{:S(2)}) collective-permute-start(bf16[384,288]{1,0:T(8,128)(2,1)S(1)} %get-tuple-element.41), channel_id=1, source_target_pairs={{0,1},{1,0},{2,3},{3,2},{4,5},{5,4},{6,7},{7,6},{8,9},{9,8},{10,11... | collective-permute-start | bytes 663560 | tf_op jit(solution)/shard_map/ppermute | solution.py:483
  37.8 8.2 %collective-permute-start.2 = (bf16[128,288]{1,0:T(8,128)(2,1)}, bf16[128,288]{1,0:T(8,128)(2,1)S(1)}, u32[]{:S(2)}, u32[]{:S(2)}) collective-permute-start(bf16[128,288]{1,0:T(8,128)(2,1)} %get-tuple-element.26), channel_id=1, source_target_pairs={{0,3},{1,0},{2,1},{3,2},{4,7},{5,4},{6,5},{7,6},{8,11},{9,8},{10,9... | collective-permute-start | bytes 221192 | tf_op jit(solution)/shard_map/ppermute | solution.py:480
  39.7 8.3 %collective-permute-start.1 = (bf16[128,288]{1,0:T(8,128)(2,1)}, bf16[128,288]{1,0:T(8,128)(2,1)S(1)}, u32[]{:S(2)}, u32[]{:S(2)}) collective-permute-start(bf16[128,288]{1,0:T(8,128)(2,1)} %get-tuple-element.26), channel_id=1, source_target_pairs={{0,2},{1,3},{2,0},{3,1},{4,6},{5,7},{6,4},{7,5},{8,10},{9,11},{10,... | collective-permute-start | bytes 221192 | tf_op jit(solution)/shard_map/ppermute | solution.py:480
  40.5 7.8 %collective-permute-start = (bf16[128,288]{1,0:T(8,128)(2,1)}, bf16[128,288]{1,0:T(8,128)(2,1)S(1)}, u32[]{:S(2)}, u32[]{:S(2)}) collective-permute-start(bf16[128,288]{1,0:T(8,128)(2,1)} %get-tuple-element.26), channel_id=1, source_target_pairs={{0,1},{1,2},{2,3},{3,0},{4,5},{5,6},{6,7},{7,4},{8,9},{9,10},{10,1... | collective-permute-start | bytes 221192 | tf_op jit(solution)/shard_map/ppermute | solution.py:480
  46.0 2.3 %copy-start.6 = (bf16[128,288]{1,0:T(8,128)(2,1)}, bf16[128,288]{1,0:T(8,128)(2,1)S(1)}, u32[]{:S(2)}) copy-start(bf16[128,288]{1,0:T(8,128)(2,1)S(1)} %collective-permute-done.2.refs_3_) | copy-start | bytes 221188
  48.1 0.6 copy-start.7
  48.3 0.7 copy-start.8
  48.3 0.7 copy-start.5
  49.1 71.4 %copy-start = (f32[128,1,16,64]{0,3,2,1:T(8,128)S(1)}, f32[128,1,16,64]{0,3,2,1:T(8,128)}, u32[]{:S(2)}) copy-start(f32[128,1,16,64]{0,3,2,1:T(8,128)} %param.24) | copy-start | bytes 1572868
  49.1 71.4 %copy-start.1 = (s32[64,1]{1,0:T(8,128)S(1)}, s32[64,1]{1,0:T(8,128)}, u32[]{:S(2)}) copy-start(s32[64,1]{1,0:T(8,128)} %copy.19.slot_ref) | copy-start | bytes 772

commit v6 on v4

--- a/solution.py
+++ b/solution.py
@@ -479,10 +479,12 @@
     late, late_part, late_sent = conv()
     late_parts = pairwise(late_part, late_sent, (outer, inner))
     mixed, early_part, early_sent, start = conv(arrived, cache_hit, late)
-    parts = pairwise(early_part, early_sent, (inner, outer)) + late_parts
     half = (lax.axis_index("req") % 2).astype(jnp.int32).reshape(1)
     new_edges = save(save_slot, half, arrived, edges, edge_rows, NEXT_AT, True)
-    new_edges, *parts = lax.optimization_barrier((new_edges, *parts))
+    early_got = lax.ppermute(early_sent, "tp", inner)
+    new_edges, early_got = lax.optimization_barrier((new_edges, early_got))
+    early_total = early_part + early_got.astype(F32)
+    parts = [early_total, lax.ppermute(early_total.astype(BF16), "tp", outer)] + late_parts
     out, back = scan_rows(
         suffix_length, parts, step_weight, step_bias, decay_log, skip_gain, mixed, gate_input, start
     )

time: 118 us -> 119 us (level)
    ppermute x0 -> x2, starting transfers between devices: none -> 4.12 us  [the longest x1 2.73 us: local(): lax.ppermute(early_total.astype(BF16), 'tp', outer)]
    ppermute x2 -> x1, starting transfers between devices: 2.9 us -> 0.17 us  [pairwise(): return [total, lax.ppermute(total.astype(BF16), 'tp', orders[1])]]
    ppermute x2 -> x1, waiting for transfers between devices: 1.98 us -> 0.01 us  [pairwise(): total = part + lax.ppermute(sent, 'tp', orders[0]).astype(F32)]
    ppermute x2 -> x1, waiting for transfers between devices: 0.01 us -> 1.75 us  [pairwise(): return [total, lax.ppermute(total.astype(BF16), 'tp', orders[1])]]
    convert_element_type x2 -> x1, other arithmetic: 2.54 us -> 0.9 us  [pairwise(): return [total, lax.ppermute(total.astype(BF16), 'tp', orders[1])]]
    convert_element_type x0 -> x1, other arithmetic: none -> 1.63 us  [local(): early_total.astype(BF16)]
    ppermute x2 -> x1, starting transfers between devices: 4.21 us -> 2.82 us  [pairwise(): total = part + lax.ppermute(sent, 'tp', orders[0]).astype(F32)]
  transfers between devices with their start and end apart: 5 -> 5, of which waited for: 2 -> 4; matrix products, arithmetic and copies ran while one was open for 2% -> 2% of each run, Pallas kernels for 12% -> 12%
where the time goes in v6:
time: 119 us; the launch traced here: 118 us
  Pallas kernels  65.2 us (55%)
  blocking collectives  23.1 us (19%)
  starting transfers between devices  20.1 us (17%)
  waiting for transfers between devices  2.84 us (2%)
  other arithmetic  2.53 us (2%)
  local copies, waits for them, and re-layouts  2.41 us (2%)
  between operations  1.99 us (2%)
    pallas_call x1, Pallas kernels, scan_rows(): pl.pallas_call(scan_kernel, grid_spec=pltpu.PrefetchScalarGridSpec(num_sc...  46.9 us
    all_to_all x1, blocking collectives, local(): back = lax.all_to_all(back, 'req', split_axis=0, concat_axis=0, tiled=True)  23.1 us
    pallas_call x2, Pallas kernels, conv_rows(): pl.pallas_call(kernel, grid_spec=pltpu.PrefetchScalarGridSpec(num_scalar_...  13.4 us
    all_to_all x1, starting transfers between devices, local(): lax.all_to_all(outgoing, 'req', split_axis=0, concat_axis=0, tiled=True)  13 us
    pallas_call x1, Pallas kernels, pack(): pl.pallas_call(pack_kernel, grid_spec=pltpu.PrefetchScalarGridSpec(num_sc...  2.87 us
    ppermute x1, starting transfers between devices, pairwise(): total = part + lax.ppermute(sent, 'tp', orders[0]).astype(F32)  2.82 us
    ppermute x1, starting transfers between devices, local(): lax.ppermute(early_total.astype(BF16), 'tp', outer)  2.73 us
  transfers between devices with their start and end apart: 5, of which 4 were waited for; matrix products, arithmetic and copies ran while one was open for 2% of the time, Pallas kernels for 12%

profile of v6, /device:TPU:1, one launch (start us, length us, event | category | flops | bytes accessed | tf_op | source)
XLA Modules:
  0.0 118.2 jit_solution(4766934910294629142)
XLA Ops:
  1.3 2.9 %pack.1 = bf16[64,16,128]{2,1,0:T(8,128)(2,1)} custom-call(s32[1]{0:T(128)S(6)} %copy.23.length_ref, s32[1,64]{1,0:T(1,128)} %bitcast.29, f32[1024,128]{1,0:T(8,128)} %bitcast.19, bf16[192,128]{1,0:T(8,128)(2,1)} %bitcast.21, bf16[512,4096]{1,0:T(8,128)(2,1)} %x_ref.5), custom_call_target="tpu_custom_call" | custom-call | tf_op jit(solution)/shard_map/pack/pallas_call | solution.py:77
  4.2 13.0 %all-to-all-start = ((bf16[64,16,128]{2,1,0:T(8,128)(2,1)}), bf16[64,16,128]{2,1,0:T(8,128)(2,1)S(1)}, u32[]{:S(2)}, u32[]{:S(2)}) async-start(bf16[64,16,128]{2,1,0:T(8,128)(2,1)} %pack.1), calls=%async_computation | async-start | bytes 524288 | tf_op jit(solution)/shard_map/all_to_all | solution.py:469
  17.2 0.0 copy-start.5
  17.2 8.8 %conv_late.1 = (bf16[512,4096]{1,0:T(8,128)(2,1)}, f32[384,288]{1,0:T(8,128)}, bf16[384,288]{1,0:T(8,128)(2,1)}) custom-call(bf16[512,4096]{1,0:T(8,128)(2,1)} %x_ref.5, bf16[512,4096]{1,0:T(8,128)(2,1)} %x_ref.5, f32[4,4096]{1,0:T(4,128)} %weight_ref.3, f32[1,4096]{1,0:T(1,128)} %bitcast.26, bf16[288,4096]{1,0:T(8,128)(2,1)} %bitcast.23), custom_call_target="tpu_custom_call" | custom-call | flops 905969664 | bytes 37748736 | tf_op jit(solution)/shard_map/conv_late/pallas_call | solution.py:224
  26.0 2.8 %collective-permute-start.2 = (bf16[384,288]{1,0:T(8,128)(2,1)}, bf16[384,288]{1,0:T(8,128)(2,1)S(1)}, u32[]{:S(2)}, u32[]{:S(2)}) collective-permute-start(bf16[384,288]{1,0:T(8,128)(2,1)} %get-tuple-element.19), channel_id=1, source_target_pairs={{0,3},{1,2},{2,1},{3,0},{4,7},{5,6},{6,5},{7,4},{8,11},{9,10},{10,... | collective-permute-start | bytes 663560 | tf_op jit(solution)/shard_map/ppermute | solution.py:441
  29.5 0.0 copy-done.5
  29.5 0.1 copy.19.slot_ref
  29.6 0.7 all-to-all-done.arrived_ref.tiles_ref
  30.3 0.0 copy-start
  30.3 0.7 copy-done
  31.0 0.0 copy-start.4
  31.0 0.0 copy-start.3
  31.0 4.6 %conv_early.1 = (bf16[512,4096]{1,0:T(8,128)(2,1)}, f32[128,288]{1,0:T(8,128)}, bf16[128,288]{1,0:T(8,128)(2,1)}, f32[4,16,8,128]{3,2,1,0:T(8,128)}) custom-call(s32[1]{0:T(128)S(6)} %copy.22.hit_ref, bf16[64,16,128]{2,1,0:T(8,128)(2,1)} %copy-done, bf16[512,4096]{1,0:T(8,128)(2,1)} %x_ref.5, f32[4,4096]{1,0:T(4,128)} %weight_ref.3, ...), custom_call_target="tpu_custom_call", output_to_operand_aliasing={{0}: (6, {})} | custom-call | flops 301989888 | bytes 12582912 | tf_op jit(solution)/shard_map/conv_early/pallas_call | solution.py:224
  35.6 1.4 %collective-permute-start = (bf16[128,288]{1,0:T(8,128)(2,1)}, bf16[128,288]{1,0:T(8,128)(2,1)S(1)}, u32[]{:S(2)}, u32[]{:S(2)}) collective-permute-start(bf16[128,288]{1,0:T(8,128)(2,1)} %get-tuple-element.16), channel_id=1, source_target_pairs={{0,1},{1,0},{2,3},{3,2},{4,5},{5,4},{6,7},{7,6},{8,9},{9,8},{10,11... | collective-permute-start | bytes 221192 | tf_op jit(solution)/shard_map/ppermute | solution.py:484
  37.0 0.0 collective-permute-done.2
  37.0 0.0 copy-done.4
  37.0 0.9 fusion
  37.9 0.2 collective-permute-start.3
  38.1 0.0 copy-done.3
  38.1 0.0 copy-start.1
  38.1 0.9 copy-done.1
  39.0 0.9 save.2
  40.0 0.1 collective-permute-done
  40.0 1.6 %fusion.1 = (bf16[128,288]{1,0:T(8,128)(2,1)S(1)}, f32[128,288]{1,0:T(8,128)}) fusion(f32[128,288]{1,0:T(8,128)} %get-tuple-element.15, bf16[128,288]{1,0:T(8,128)(2,1)S(1)} %collective-permute-done), kind=kLoop, calls=%fused_computation.3 | loop fusion | flops 110592 | bytes 442368 | tf_op jit(solution)/shard_map/convert_element_type | solution.py:487
  41.7 2.7 %collective-permute-start.1 = (bf16[128,288]{1,0:T(8,128)(2,1)S(1)}, bf16[128,288]{1,0:T(8,128)(2,1)S(1)}, u32[]{:S(2)}, u32[]{:S(2)}) collective-permute-start(bf16[128,288]{1,0:T(8,128)(2,1)S(1)} %get-tuple-element.27), channel_id=1, source_target_pairs={{0,3},{1,2},{2,1},{3,0},{4,7},{5,6},{6,5},{7,4},{8,11},{9,10},{10,... | collective-permute-start | bytes 221192 | tf_op jit(solution)/shard_map/ppermute | solution.py:487
  44.4 1.7 %collective-permute-done.3.refs_3_ = bf16[384,288]{1,0:T(8,128)(2,1)S(1)} collective-permute-done((bf16[384,288]{1,0:T(8,128)(2,1)S(1)}, bf16[384,288]{1,0:T(8,128)(2,1)S(1)}, u32[]{:S(2)}, u32[]{:S(2)}) %collective-permute-start.3) | collective-permute-done | bytes 221216 | tf_op jit(solution)/shard_map/ppermute | solution.py:442
  46.2 0.0 copy-start.6
  46.2 0.3 collective-permute-done.1.refs_1_
  46.4 0.0 copy-start.7
  46.4 0.5 copy-done.6
  46.9 0.2 copy-done.7
  47.0 0.0 copy-start.2
  47.1 46.9 %scan_rows.1 = (bf16[512,4096]{1,0:T(8,128)(2,1)}, bf16[64,8,128]{2,1,0:T(8,128)(2,1)}) custom-call(s32[1]{0:T(128)S(6)} %copy.23.length_ref, f32[128,288]{1,0:T(8,128)} %get-tuple-element.28.refs_0_, bf16[128,288]{1,0:T(8,128)(2,1)} %copy-done.7, f32[384,288]{1,0:T(8,128)} %get-tuple-element.26.refs_2_, bf16[384,288]{1,0:T(8,128)(2,1)} %copy-done.6, ...), custom_call_target="tpu_custom_call" | custom-call | flops 4429185024 | bytes 16777216 | tf_op jit(solution)/shard_map/scan_rows/pallas_call | solution.py:359
  94.0 23.1 %all_to_all.10.tiles_ref = bf16[64,8,128]{2,1,0:T(8,128)(2,1)S(1)} all-to-all(bf16[64,8,128]{2,1,0:T(8,128)(2,1)} %get-tuple-element.23), channel_id=1, replica_groups=mesh['req'=64,'tp'=4] {'req'}, dimensions={0} | all-to-all | bytes 262144 | tf_op jit(solution)/shard_map/all_to_all | solution.py:491
  117.1 0.0 copy-done.2
  117.1 1.1 save.3
Async XLA Ops:
  4.2 26.2 %all-to-all-start = ((bf16[64,16,128]{2,1,0:T(8,128)(2,1)}), bf16[64,16,128]{2,1,0:T(8,128)(2,1)S(1)}, u32[]{:S(2)}, u32[]{:S(2)}) async-start(bf16[64,16,128]{2,1,0:T(8,128)(2,1)} %pack.1), calls=%async_computation | async-start | bytes 524288 | tf_op jit(solution)/shard_map/all_to_all | solution.py:469
  17.2 12.3 %copy-start.5 = (s32[64]{0:T(128)S(1)}, s32[64]{0:T(128)}, u32[]{:S(2)}) copy-start(s32[64]{0:T(128)} %param.27) | copy-start | bytes 772
  26.0 11.0 %collective-permute-start.2 = (bf16[384,288]{1,0:T(8,128)(2,1)}, bf16[384,288]{1,0:T(8,128)(2,1)S(1)}, u32[]{:S(2)}, u32[]{:S(2)}) collective-permute-start(bf16[384,288]{1,0:T(8,128)(2,1)} %get-tuple-element.19), channel_id=1, source_target_pairs={{0,3},{1,2},{2,1},{3,0},{4,7},{5,6},{6,5},{7,4},{8,11},{9,10},{10,... | collective-permute-start | bytes 663560 | tf_op jit(solution)/shard_map/ppermute | solution.py:441
  30.3 0.7 copy-start
  31.0 6.0 %copy-start.4 = (f32[384,288]{1,0:T(8,128)S(1)}, f32[384,288]{1,0:T(8,128)}, u32[]{:S(2)}) copy-start(f32[384,288]{1,0:T(8,128)} %get-tuple-element.18) | copy-start | bytes 1327108
  31.0 7.0 %copy-start.3 = (bf16[128,1,3,64]{0,3,2,1:T(8,128)(2,1)S(1)}, bf16[128,1,3,64]{0,3,2,1:T(8,128)(2,1)}, u32[]{:S(2)}) copy-start(bf16[128,1,3,64]{0,3,2,1:T(8,128)(2,1)} %param.25) | copy-start | bytes 147460
  35.6 4.4 %collective-permute-start = (bf16[128,288]{1,0:T(8,128)(2,1)}, bf16[128,288]{1,0:T(8,128)(2,1)S(1)}, u32[]{:S(2)}, u32[]{:S(2)}) collective-permute-start(bf16[128,288]{1,0:T(8,128)(2,1)} %get-tuple-element.16), channel_id=1, source_target_pairs={{0,1},{1,0},{2,3},{3,2},{4,5},{5,4},{6,7},{7,6},{8,9},{9,8},{10,11... | collective-permute-start | bytes 221192 | tf_op jit(solution)/shard_map/ppermute | solution.py:484
  37.9 8.3 %collective-permute-start.3 = (bf16[384,288]{1,0:T(8,128)(2,1)S(1)}, bf16[384,288]{1,0:T(8,128)(2,1)S(1)}, u32[]{:S(2)}, u32[]{:S(2)}) collective-permute-start(bf16[384,288]{1,0:T(8,128)(2,1)S(1)} %get-tuple-element.25), channel_id=1, source_target_pairs={{0,1},{1,0},{2,3},{3,2},{4,5},{5,4},{6,7},{7,6},{8,9},{9,8},{10,11... | collective-permute-start | bytes 663560 | tf_op jit(solution)/shard_map/ppermute | solution.py:442
  38.1 1.0 copy-start.1
  41.7 4.7 %collective-permute-start.1 = (bf16[128,288]{1,0:T(8,128)(2,1)S(1)}, bf16[128,288]{1,0:T(8,128)(2,1)S(1)}, u32[]{:S(2)}, u32[]{:S(2)}) collective-permute-start(bf16[128,288]{1,0:T(8,128)(2,1)S(1)} %get-tuple-element.27), channel_id=1, source_target_pairs={{0,3},{1,2},{2,1},{3,0},{4,7},{5,6},{6,5},{7,4},{8,11},{9,10},{10,... | collective-permute-start | bytes 221192 | tf_op jit(solution)/shard_map/ppermute | solution.py:487
  46.2 0.7 copy-start.6
  46.4 0.6 copy-start.7
  47.0 70.0 %copy-start.2 = (f32[128,1,16,64]{0,3,2,1:T(8,128)S(1)}, f32[128,1,16,64]{0,3,2,1:T(8,128)}, u32[]{:S(2)}) copy-start(f32[128,1,16,64]{0,3,2,1:T(8,128)} %param.24) | copy-start | bytes 1572868

commit v7 on v4

--- a/solution.py
+++ b/solution.py
@@ -22,7 +22,7 @@
 NEXT_AT = 11
 CHUNK = 16
 FETCHES = 6
-GROUPS_AT_ONCE = 4
+GROUPS_AT_ONCE = 8
 PAIRS = 2
 VMEM_LIMIT = 60 * 1024 * 1024
 SMALL_LIMIT = 24 * 1024 * 1024

time: 118 us -> 118 us (level)
  no operation moved by 1% of the time
where the time goes in v7:
time: 118 us
  Pallas kernels  64.9 us (55%)
  blocking collectives  22.7 us (19%)
  starting transfers between devices  20.1 us (17%)
  waiting for transfers between devices  3 us (3%)
  other arithmetic  2.54 us (2%)
  local copies, waits for them, and re-layouts  2.52 us (2%)
  between operations  1.98 us (2%)
    pallas_call x1, Pallas kernels, scan_rows(): pl.pallas_call(scan_kernel, grid_spec=pltpu.PrefetchScalarGridSpec(num_sc...  46.8 us
    all_to_all x1, blocking collectives, local(): back = lax.all_to_all(back, 'req', split_axis=0, concat_axis=0, tiled=True)  22.7 us
    pallas_call x2, Pallas kernels, conv_rows(): pl.pallas_call(kernel, grid_spec=pltpu.PrefetchScalarGridSpec(num_scalar_...  13.3 us
    all_to_all x1, starting transfers between devices, local(): lax.all_to_all(outgoing, 'req', split_axis=0, concat_axis=0, tiled=True)  13 us
    ppermute x2, starting transfers between devices, pairwise(): total = part + lax.ppermute(sent, 'tp', orders[0]).astype(F32)  4.21 us
    ppermute x2, starting transfers between devices, pairwise(): return [total, lax.ppermute(total.astype(BF16), 'tp', orders[1])]  2.9 us
    pallas_call x1, Pallas kernels, pack(): pl.pallas_call(pack_kernel, grid_spec=pltpu.PrefetchScalarGridSpec(num_sc...  2.87 us
    convert_element_type x2, other arithmetic, pairwise(): return [total, lax.ppermute(total.astype(BF16), 'tp', orders[1])]  2.54 us
  transfers between devices with their start and end apart: 5, of which 2 were waited for; matrix products, arithmetic and copies ran while one was open for 2% of the time, Pallas kernels for 12%

profile of v7, /device:TPU:1, one launch (start us, length us, event | category | flops | bytes accessed | tf_op | source)
XLA Modules:
  0.0 117.8 jit_solution(10061253466000701263)
XLA Ops:
  1.3 2.9 %pack.1 = bf16[64,16,128]{2,1,0:T(8,128)(2,1)} custom-call(s32[1]{0:T(128)S(6)} %copy.23.length_ref, s32[1,64]{1,0:T(1,128)} %bitcast.29, f32[1024,128]{1,0:T(8,128)} %bitcast.19, bf16[192,128]{1,0:T(8,128)(2,1)} %bitcast.21, bf16[512,4096]{1,0:T(8,128)(2,1)} %x_ref.5), custom_call_target="tpu_custom_call" | custom-call | tf_op jit(solution)/shard_map/pack/pallas_call | solution.py:77
  4.2 13.0 %all-to-all-start = ((bf16[64,16,128]{2,1,0:T(8,128)(2,1)}), bf16[64,16,128]{2,1,0:T(8,128)(2,1)S(1)}, u32[]{:S(2)}, u32[]{:S(2)}) async-start(bf16[64,16,128]{2,1,0:T(8,128)(2,1)} %pack.1), calls=%async_computation | async-start | bytes 524288 | tf_op jit(solution)/shard_map/all_to_all | solution.py:469
  17.2 8.7 %conv_late.1 = (bf16[512,4096]{1,0:T(8,128)(2,1)}, f32[384,288]{1,0:T(8,128)}, bf16[384,288]{1,0:T(8,128)(2,1)}) custom-call(bf16[512,4096]{1,0:T(8,128)(2,1)} %x_ref.5, bf16[512,4096]{1,0:T(8,128)(2,1)} %x_ref.5, f32[4,4096]{1,0:T(4,128)} %weight_ref.3, f32[1,4096]{1,0:T(1,128)} %bitcast.26, bf16[288,4096]{1,0:T(8,128)(2,1)} %bitcast.23), custom_call_target="tpu_custom_call" | custom-call | flops 905969664 | bytes 37748736 | tf_op jit(solution)/shard_map/conv_late/pallas_call | solution.py:224
  25.8 2.8 %collective-permute-start.2 = (bf16[384,288]{1,0:T(8,128)(2,1)}, bf16[384,288]{1,0:T(8,128)(2,1)S(1)}, u32[]{:S(2)}, u32[]{:S(2)}) collective-permute-start(bf16[384,288]{1,0:T(8,128)(2,1)} %get-tuple-element.21), channel_id=1, source_target_pairs={{0,3},{1,2},{2,1},{3,0},{4,7},{5,6},{6,5},{7,4},{8,11},{9,10},{10,... | collective-permute-start | bytes 663560 | tf_op jit(solution)/shard_map/ppermute | solution.py:441
  29.3 1.0 all-to-all-done.tiles_ref.arrived_ref
  30.3 0.0 copy-start
  30.3 0.7 copy-done
  31.0 0.0 copy-start.4
  31.0 0.0 copy-start.5
  31.0 0.0 copy-start.3
  31.0 4.6 %conv_early.1 = (bf16[512,4096]{1,0:T(8,128)(2,1)}, f32[128,288]{1,0:T(8,128)}, bf16[128,288]{1,0:T(8,128)(2,1)}, f32[4,16,8,128]{3,2,1,0:T(8,128)}) custom-call(s32[1]{0:T(128)S(6)} %copy.22.hit_ref, bf16[64,16,128]{2,1,0:T(8,128)(2,1)} %copy-done, bf16[512,4096]{1,0:T(8,128)(2,1)} %x_ref.5, f32[4,4096]{1,0:T(4,128)} %weight_ref.3, ...), custom_call_target="tpu_custom_call", output_to_operand_aliasing={{0}: (6, {})} | custom-call | flops 301989888 | bytes 12582912 | tf_op jit(solution)/shard_map/conv_early/pallas_call | solution.py:224
  35.6 1.4 %collective-permute-start = (bf16[128,288]{1,0:T(8,128)(2,1)}, bf16[128,288]{1,0:T(8,128)(2,1)S(1)}, u32[]{:S(2)}, u32[]{:S(2)}) collective-permute-start(bf16[128,288]{1,0:T(8,128)(2,1)} %get-tuple-element.19), channel_id=1, source_target_pairs={{0,1},{1,0},{2,3},{3,2},{4,5},{5,4},{6,7},{7,6},{8,9},{9,8},{10,11... | collective-permute-start | bytes 221192 | tf_op jit(solution)/shard_map/ppermute | solution.py:441
  37.0 0.0 collective-permute-done.2
  37.0 0.0 copy-done.4
  37.0 0.9 fusion
  37.9 0.2 collective-permute-start.3
  38.1 2.0 %collective-permute-done = bf16[128,288]{1,0:T(8,128)(2,1)S(1)} collective-permute-done((bf16[128,288]{1,0:T(8,128)(2,1)}, bf16[128,288]{1,0:T(8,128)(2,1)S(1)}, u32[]{:S(2)}, u32[]{:S(2)}) %collective-permute-start) | collective-permute-done | bytes 73760 | tf_op jit(solution)/shard_map/ppermute | solution.py:441
  40.1 1.6 %fusion.1 = (bf16[128,288]{1,0:T(8,128)(2,1)S(1)}, f32[128,288]{1,0:T(8,128)}) fusion(f32[128,288]{1,0:T(8,128)} %get-tuple-element.18, bf16[128,288]{1,0:T(8,128)(2,1)S(1)} %collective-permute-done), kind=kLoop, calls=%fused_computation.3 | loop fusion | flops 110592 | bytes 442368 | tf_op jit(solution)/shard_map/convert_element_type | solution.py:442
  41.7 2.7 %collective-permute-start.1 = (bf16[128,288]{1,0:T(8,128)(2,1)S(1)}, bf16[128,288]{1,0:T(8,128)(2,1)S(1)}, u32[]{:S(2)}, u32[]{:S(2)}) collective-permute-start(bf16[128,288]{1,0:T(8,128)(2,1)S(1)} %get-tuple-element.33), channel_id=1, source_target_pairs={{0,3},{1,2},{2,1},{3,0},{4,7},{5,6},{6,5},{7,4},{8,11},{9,10},{10,... | collective-permute-start | bytes 221192 | tf_op jit(solution)/shard_map/ppermute | solution.py:442
  44.4 0.0 copy-done.5
  44.4 0.1 copy.19.slot_ref
  44.5 0.0 copy-done.3
  44.5 0.0 copy-start.1
  44.6 0.9 copy-done.1
  45.5 0.9 save.2
  46.4 0.0 collective-permute-done.3.refs_3_
  46.4 0.0 copy-start.6
  46.4 0.0 collective-permute-done.1.refs_1_
  46.4 0.0 copy-start.7
  46.5 0.7 copy-done.6
  47.1 0.0 copy-done.7
  47.2 0.0 copy-start.2
  47.2 46.8 %scan_rows.1 = (bf16[512,4096]{1,0:T(8,128)(2,1)}, bf16[64,8,128]{2,1,0:T(8,128)(2,1)}) custom-call(s32[1]{0:T(128)S(6)} %copy.23.length_ref, f32[128,288]{1,0:T(8,128)} %get-tuple-element.22.refs_0_, bf16[128,288]{1,0:T(8,128)(2,1)} %copy-done.7, f32[384,288]{1,0:T(8,128)} %get-tuple-element.24.refs_2_, bf16[384,288]{1,0:T(8,128)(2,1)} %copy-done.6, ...), custom_call_target="tpu_custom_call" | custom-call | flops 4429185024 | bytes 16777216 | tf_op jit(solution)/shard_map/scan_rows/pallas_call | solution.py:359
  94.0 22.7 %all_to_all.10.tiles_ref = bf16[64,8,128]{2,1,0:T(8,128)(2,1)S(1)} all-to-all(bf16[64,8,128]{2,1,0:T(8,128)(2,1)} %get-tuple-element.29), channel_id=1, replica_groups=mesh['req'=64,'tp'=4] {'req'}, dimensions={0} | all-to-all | bytes 262144 | tf_op jit(solution)/shard_map/all_to_all | solution.py:489
  116.7 0.0 copy-done.2
  116.7 1.1 save.3
Async XLA Ops:
  4.2 26.2 %all-to-all-start = ((bf16[64,16,128]{2,1,0:T(8,128)(2,1)}), bf16[64,16,128]{2,1,0:T(8,128)(2,1)S(1)}, u32[]{:S(2)}, u32[]{:S(2)}) async-start(bf16[64,16,128]{2,1,0:T(8,128)(2,1)} %pack.1), calls=%async_computation | async-start | bytes 524288 | tf_op jit(solution)/shard_map/all_to_all | solution.py:469
  25.8 11.2 %collective-permute-start.2 = (bf16[384,288]{1,0:T(8,128)(2,1)}, bf16[384,288]{1,0:T(8,128)(2,1)S(1)}, u32[]{:S(2)}, u32[]{:S(2)}) collective-permute-start(bf16[384,288]{1,0:T(8,128)(2,1)} %get-tuple-element.21), channel_id=1, source_target_pairs={{0,3},{1,2},{2,1},{3,0},{4,7},{5,6},{6,5},{7,4},{8,11},{9,10},{10,... | collective-permute-start | bytes 663560 | tf_op jit(solution)/shard_map/ppermute | solution.py:441
  30.3 0.7 copy-start
  31.0 6.0 %copy-start.4 = (f32[384,288]{1,0:T(8,128)S(1)}, f32[384,288]{1,0:T(8,128)}, u32[]{:S(2)}) copy-start(f32[384,288]{1,0:T(8,128)} %get-tuple-element.20) | copy-start | bytes 1327108
  31.0 13.4 %copy-start.5 = (s32[64]{0:T(128)S(1)}, s32[64]{0:T(128)}, u32[]{:S(2)}) copy-start(s32[64]{0:T(128)} %param.27) | copy-start | bytes 772
  31.0 13.5 %copy-start.3 = (bf16[128,1,3,64]{0,3,2,1:T(8,128)(2,1)S(1)}, bf16[128,1,3,64]{0,3,2,1:T(8,128)(2,1)}, u32[]{:S(2)}) copy-start(bf16[128,1,3,64]{0,3,2,1:T(8,128)(2,1)} %param.25) | copy-start | bytes 147460
  35.6 4.4 %collective-permute-start = (bf16[128,288]{1,0:T(8,128)(2,1)}, bf16[128,288]{1,0:T(8,128)(2,1)S(1)}, u32[]{:S(2)}, u32[]{:S(2)}) collective-permute-start(bf16[128,288]{1,0:T(8,128)(2,1)} %get-tuple-element.19), channel_id=1, source_target_pairs={{0,1},{1,0},{2,3},{3,2},{4,5},{5,4},{6,7},{7,6},{8,9},{9,8},{10,11... | collective-permute-start | bytes 221192 | tf_op jit(solution)/shard_map/ppermute | solution.py:441
  37.9 8.5 %collective-permute-start.3 = (bf16[384,288]{1,0:T(8,128)(2,1)S(1)}, bf16[384,288]{1,0:T(8,128)(2,1)S(1)}, u32[]{:S(2)}, u32[]{:S(2)}) collective-permute-start(bf16[384,288]{1,0:T(8,128)(2,1)S(1)} %get-tuple-element.31), channel_id=1, source_target_pairs={{0,1},{1,0},{2,3},{3,2},{4,5},{5,4},{6,7},{7,6},{8,9},{9,8},{10,11... | collective-permute-start | bytes 663560 | tf_op jit(solution)/shard_map/ppermute | solution.py:442
  41.7 4.7 %collective-permute-start.1 = (bf16[128,288]{1,0:T(8,128)(2,1)S(1)}, bf16[128,288]{1,0:T(8,128)(2,1)S(1)}, u32[]{:S(2)}, u32[]{:S(2)}) collective-permute-start(bf16[128,288]{1,0:T(8,128)(2,1)S(1)} %get-tuple-element.33), channel_id=1, source_target_pairs={{0,3},{1,2},{2,1},{3,0},{4,7},{5,6},{6,5},{7,4},{8,11},{9,10},{10,... | collective-permute-start | bytes 221192 | tf_op jit(solution)/shard_map/ppermute | solution.py:442
  44.5 1.0 copy-start.1
  46.4 0.7 copy-start.6
  46.4 0.7 copy-start.7
  47.2 69.5 %copy-start.2 = (f32[128,1,16,64]{0,3,2,1:T(8,128)S(1)}, f32[128,1,16,64]{0,3,2,1:T(8,128)}, u32[]{:S(2)}) copy-start(f32[128,1,16,64]{0,3,2,1:T(8,128)} %param.24) | copy-start | bytes 1572868
